TPU v7x, 32 devices: a whole 2x2x4 slice. The times are simulated.
32 devices in a mesh: node: 8 (over y, x, core), fld: 4 (over z).
Axes of the slice: x: 2, y: 2, z: 4, core: 2. Of those that a mesh axis runs over, the one named last changes fastest.
Arguments:
- pressure: bfloat16 [57344, 128], P(('node', 'fld')), may hold values from -6 to 6
- modes: bfloat16 [57344, 2816], P(('node', 'fld')), may hold values from -0.0234375 to 0.0234375
- omega_mode: float32 [2816], replicated, may hold values from 0.5 to 4
- damping: float32 [2816], replicated, may hold values from 0.02 to 0.2
- omega_force: float32 [8], replicated, may hold values from 0.8 to 3
- panel_of: int32 [57344], P(('node', 'fld')), may hold values from 0 to 255
- dist_bin: int32 [8192, 256], P('node', 'fld'), may hold values from 0 to 399
Outputs:
- field_pressure: float32 [256, 128], P('fld')
All inputs are finite; a program needn't handle non-finite values.
Results may differ from a plain program's by a relative error of at most 0.0031.
Values may be sent and summed in bfloat16 or wider, within the bound.
No kernel may reach another device: no remote copies, remote signals or barrier semaphores. Data moves between devices by JAX's collectives and lax.ppermute only.
A program may use at most 64 MiB of HBM per device.

v0:
```python
import jax
import jax.numpy as jnp
from jax import lax
from jax.sharding import PartitionSpec as P

PANEL_DEV = 256


def modal_response(forces, omega_mode, damping, omega_force):
    half = forces.shape[1] // 2
    wcol = jnp.repeat(omega_force, half // omega_force.shape[0])[None, :]
    wmod = omega_mode[:, None]
    real_part = wmod * wmod - wcol * wcol
    imag_part = 2.0 * damping[:, None] * wmod * wcol
    magnitude = real_part * real_part + imag_part * imag_part
    h_real = real_part / magnitude
    h_imag = -imag_part / magnitude
    f_real = forces[:, :half]
    f_imag = forces[:, half:]
    a_real = h_real * f_real - h_imag * f_imag
    a_imag = h_real * f_imag + h_imag * f_real
    return jnp.concatenate([a_real, a_imag], axis=1).astype(jnp.bfloat16)


def shards(pressure, modes, omega_mode, damping, omega_force, panel_of, dist_bin):
    columns = pressure.shape[1]
    half = columns // 2
    freq_count = omega_force.shape[0]
    local_forces = lax.dot_general(
        modes, pressure, (((0,), (0,)), ((), ())), preferred_element_type=jnp.float32
    )
    forces = lax.psum(local_forces, ("node", "fld"))
    response = modal_response(forces, omega_mode, damping, omega_force)
    raw = jnp.dot(modes, response, preferred_element_type=jnp.float32)
    wcol = jnp.repeat(omega_force, half // freq_count)[None, :]
    velocity = jnp.concatenate([-wcol * raw[:, half:], wcol * raw[:, :half]], axis=1)
    panel_count = PANEL_DEV
    onehot = (panel_of[:, None] == jnp.arange(panel_count, dtype=jnp.int32)[None, :]).astype(
        jnp.float32
    )
    panel_velocity = lax.dot_general(
        onehot,
        velocity,
        (((0,), (0,)), ((), ())),
        precision=lax.Precision.HIGHEST,
        preferred_element_type=jnp.float32,
    )
    field_rows = dist_bin.shape[1]
    realiz = half // freq_count
    hp = lax.Precision.HIGHEST
    piece = lax.all_gather(panel_velocity, "fld", axis=0, tiled=True)
    dist = 1.0 + 0.05 * dist_bin.astype(jnp.float32)
    omega = omega_force[:, None, None]
    amplitude = 0.01 * omega / (2.0 * jnp.pi * dist[None])
    k_real = amplitude * jnp.sin(omega * dist[None])
    k_imag = amplitude * jnp.cos(omega * dist[None])
    shaped = piece.reshape(piece.shape[0], 2, freq_count, realiz)
    u_real = shaped[:, 0]
    u_imag = shaped[:, 1]
    p_real = jnp.einsum("fjx,jfr->xfr", k_real, u_real, precision=hp) - jnp.einsum(
        "fjx,jfr->xfr", k_imag, u_imag, precision=hp
    )
    p_imag = jnp.einsum("fjx,jfr->xfr", k_real, u_imag, precision=hp) + jnp.einsum(
        "fjx,jfr->xfr", k_imag, u_real, precision=hp
    )
    joined = jnp.stack([p_real, p_imag], axis=1).reshape(field_rows, columns)
    return lax.psum(joined, "node")


def solution(mesh):
    in_specs = (
        P(("node", "fld"), None),
        P(("node", "fld"), None),
        P(),
        P(),
        P(),
        P(("node", "fld")),
        P("node", "fld"),
    )
    out_specs = P("fld", None)
    return jax.shard_map(shards, mesh=mesh, in_specs=in_specs, out_specs=out_specs, check_vma=False)
```

profile of v0, /device:TPU:0, one launch (start us, length us, event | category | flops | bytes accessed | tf_op | source)
XLA Modules:
  0.0 241.1 jit_solution(11055946253518422310)
XLA Ops:
  6.5 0.0 copy-start
  6.5 0.0 copy-start.4
  6.5 0.0 copy-start.3
  6.5 0.0 copy-start.2
  6.5 0.0 copy-start.1
  6.5 0.0 all-reduce.2.cloned.1.call-start
  6.6 1.0 copy-done
  7.6 6.5 %fusion.53 = f32[2816,128]{0,1:T(8,128)} fusion(bf16[1792,2816]{1,0:T(8,128)(2,1)} %param.8, bf16[1792,128]{1,0:T(8,128)(2,1)S(1)} %copy-done), kind=kOutput, calls=%fused_computation.59 | convolution fusion | flops 1291845632 | bytes 11993088 | tf_op jit(solution)/shard_map/dot_general | solution.py:29
  14.1 0.0 all-reduce.2.cloned.1.call-update
  14.1 0.0 copy-done.4
  14.1 0.1 broadcast_in_dim.2
  14.2 0.1 broadcast_in_dim_reshape.4
  14.3 0.0 copy-done.3
  14.3 0.0 copy-done.2
  14.3 0.0 copy-done.1
  14.3 0.1 broadcast_multiply_fusion
  14.4 134.5 %all-reduce.2.cloned.1.call-done = f32[2816,128]{0,1:T(8,128)} async-done(((f32[2816,128]{0,1:T(8,128)}), f32[2816,128]{0,1:T(8,128)}) %all-reduce.2.cloned.1.call-update) | async-done | bytes 1441808 | tf_op jit(solution)/shard_map/psum | solution.py:32
  148.9 1.8 subtract_convert_fusion
  150.6 0.0 copy-start.5
  150.7 7.2 %convolution_bitcast_fusion = f32[1792,128]{0,1:T(8,128)S(1)} fusion(bf16[1792,2816]{1,0:T(8,128)(2,1)} %param.8, bf16[2816,64]{0,1:T(8,128)(2,1)S(1)} %get-tuple-element.6, bf16[2816,64]{0,1:T(8,128)(2,1)S(1)} %get-tuple-element.5), kind=kOutput, calls=%fused_computation.2 | convolution fusion | flops 1293287424 | bytes 11730944 | tf_op jit(solution)/shard_map/dot_general | solution.py:34
  157.9 0.1 slice_multiply_fusion.1
  158.0 0.0 copy-done.5
  158.0 1.4 fusion.39
  159.4 16.1 %all_gather.3 = f32[1024,128]{1,0:T(8,128)S(1)} all-gather(f32[256,128]{1,0:T(8,128)S(1)} %fusion.39), channel_id=1, replica_groups=mesh['node'=8,'fld'=4] {'fld'}, dimensions={0}, use_global_device_ids=true | all-gather | bytes 655360 | tf_op jit(solution)/shard_map/all_gather | solution.py:51
  175.6 0.2 copy.14
  175.8 8.6 %fusion.5 = f32[8,8,64]{2,1,0:T(8,128)S(1)} fusion(f32[1024,64]{0,1:T(8,128)S(1)} %get-tuple-element.10, f32[8]{0:T(128)S(1)} %copy-done.4, f32[1024,64]{0,1:T(8,128)S(1)} %get-tuple-element.9, f32[8]{0:T(128)S(1)} %broadcast_multiply_fusion.1, f32[1024,2,8,8]{0,3,2,1:T(8,128)S(1)} %bitcast.23), kind=kOutput, calls=%fused_computation.8 | convolution fusion | flops 51904512 | bytes 803840 | tf_op jit(solution)/shard_map/fjx,jfr->xfr/dot_general | solution.py:60
  184.3 8.8 %fusion.3 = f32[8,8,64]{2,1,0:T(8,128)S(1)} fusion(f32[1024,64]{0,1:T(8,128)S(1)} %get-tuple-element.10, f32[8]{0:T(128)S(1)} %copy-done.4, f32[1024,64]{0,1:T(8,128)S(1)} %get-tuple-element.9, f32[8]{0:T(128)S(1)} %broadcast_multiply_fusion.1, f32[1024,2,8,8]{0,3,2,1:T(8,128)S(1)} %bitcast.24), kind=kOutput, calls=%fused_computation.7 | convolution fusion | flops 51904512 | bytes 803840 | tf_op jit(solution)/shard_map/fjx,jfr->xfr/dot_general | solution.py:63
  193.2 8.9 %fusion.14 = f32[64,1,8,8]{0,3,2,1:T(8,128)S(1)} fusion(f32[8,8,64]{2,1,0:T(8,128)S(1)} %fusion.5, f32[1024,64]{0,1:T(8,128)S(1)} %get-tuple-element.10, f32[8]{0:T(128)S(1)} %copy-done.4, f32[1024,64]{0,1:T(8,128)S(1)} %get-tuple-element.9, f32[8]{0:T(128)S(1)} %broadcast_multiply_fusion.1, f32[1024,2,8,8]{0,3,2,1:T(8,128)S(1)} %bitcast.25), kind=kOutput, calls=%fused_computation.12 | convolution fusion | flops 51908608 | bytes 836608 | tf_op jit(solution)/shard_map/fjx,jfr->xfr/dot_general | solution.py:60
  202.1 8.7 %fusion.20 = f32[64,1,8,8]{0,3,2,1:T(8,128)S(1)} fusion(f32[8,8,64]{2,1,0:T(8,128)S(1)} %fusion.3, f32[1024,64]{0,1:T(8,128)S(1)} %get-tuple-element.10, f32[8]{0:T(128)S(1)} %copy-done.4, f32[1024,64]{0,1:T(8,128)S(1)} %get-tuple-element.9, f32[8]{0:T(128)S(1)} %broadcast_multiply_fusion.1, f32[1024,2,8,8]{0,3,2,1:T(8,128)S(1)} %bitcast.26), kind=kOutput, calls=%fused_computation.14 | convolution fusion | flops 51908608 | bytes 836608 | tf_op jit(solution)/shard_map/fjx,jfr->xfr/dot_general | solution.py:63
  210.8 0.1 copy.15
  210.9 23.0 %psum.15 = f32[64,128]{1,0:T(8,128)} all-reduce(f32[64,128]{1,0:T(8,128)S(1)} %copy.15), channel_id=1, replica_groups=mesh['node'=8,'fld'=4] {'node'}, use_global_device_ids=true, to_apply=%region_1.0 | all-reduce | flops 8192 | bytes 65536 | tf_op jit(solution)/shard_map/psum | solution.py:67
  (4 shorter events, 0.1 us)
Async XLA Ops:
  6.5 1.0 copy-start
  6.5 7.6 %copy-start.4 = (f32[8]{0:T(128)S(1)}, f32[8]{0:T(128)}, u32[]{:S(2)}) copy-start(f32[8]{0:T(128)} %param.11) | copy-start | bytes 100
  6.5 7.7 %copy-start.3 = (f32[2816]{0:T(1024)S(1)}, f32[2816]{0:T(1024)}, u32[]{:S(2)}) copy-start(f32[2816]{0:T(1024)} %param.10) | copy-start | bytes 33796
  6.5 7.7 %copy-start.2 = (f32[2816]{0:T(1024)S(1)}, f32[2816]{0:T(1024)}, u32[]{:S(2)}) copy-start(f32[2816]{0:T(1024)} %param.9) | copy-start | bytes 33796
  6.5 7.7 %copy-start.1 = (s32[1024,64]{0,1:T(8,128)S(1)}, s32[1024,64]{0,1:T(8,128)}, u32[]{:S(2)}) copy-start(s32[1024,64]{0,1:T(8,128)} %param.13) | copy-start | bytes 786436
  6.5 142.3 %all-reduce.2.cloned.1.call-start = ((), (), s32[]{:S(2)}) async-start(), calls=%async_computation | async-start | bytes 2883584 | tf_op jit(solution)/shard_map/psum | solution.py:32
  150.6 7.4 %copy-start.5 = (s32[1792]{0:T(1024)S(1)}, s32[1792]{0:T(1024)}, u32[]{:S(2)}) copy-start(s32[1792]{0:T(1024)} %param.12) | copy-start | bytes 21508
Sparse Core Ops, SparseCore 0:
  14.2 134.6 all-reduce.1
where the time goes:
time: 246 us; the launch traced here: 241 us
  waiting for transfers between devices  135 us (55%)
  matrix products  50.1 us (20%)
  blocking collectives  39.1 us (16%)
  between operations  14 us (6%)
    psum x1, waiting for transfers between devices, shards(): forces = lax.psum(local_forces, ('node', 'fld'))  134 us
    psum x1, blocking collectives, shards(): return lax.psum(joined, 'node')  23 us
    all_gather x1, blocking collectives, shards(): piece = lax.all_gather(panel_velocity, 'fld', axis=0, tiled=True)  16.1 us
    dot_general x1, matrix products, shards(): jnp.einsum('fjx,jfr->xfr', k_real, u_real, precision=hp)  8.93 us
    dot_general x1, matrix products, shards(): jnp.einsum('fjx,jfr->xfr', k_imag, u_real, precision=hp)  8.82 us
    dot_general x1, matrix products, shards(): jnp.einsum('fjx,jfr->xfr', k_real, u_imag, precision=hp)  8.66 us
    dot_general x1, matrix products, shards(): jnp.einsum('fjx,jfr->xfr', k_imag, u_imag, precision=hp)  8.59 us
    dot_general x1, matrix products, shards(): raw = jnp.dot(modes, response, preferred_element_type=jnp.float32)  7.22 us
  transfers between devices with their start and end apart: 1, of which 1 were waited for; matrix products, arithmetic and copies ran while one was open for 0% of the time, Pallas kernels for 0%

commit v1 on v0

v1 whole, which is shorter than its diff:
```python
import math

import jax
import jax.numpy as jnp
from jax import lax
from jax.experimental import pallas as pl
from jax.experimental.pallas import tpu as pltpu
from jax.sharding import PartitionSpec as P

PANEL_DEV = 256
BF16, F16, F32 = jnp.bfloat16, jnp.float16, jnp.float32
NT = (((1,), (1,)), ((), ()))
MIB = 1024 * 1024


def row_block(rows):
    return next(b for b in (256, 128, 64, 32, 16, rows) if rows % b == 0)


def forces_kernel(half_ref, pressure_ref, modes_ref, out_ref, top_ref):
    step = pl.program_id(0)
    part = lax.dot_general(
        pressure_ref[...], modes_ref[...], (((0,), (0,)), ((), ())), preferred_element_type=F32
    )

    @pl.when(step == 0)
    def _():
        out_ref[...] = part

    @pl.when(step > 0)
    def _():
        out_ref[...] += part

    @pl.when(step == pl.num_programs(0) - 1)
    def _():
        top_ref[...] = jnp.full(top_ref.shape, jnp.max(jnp.abs(out_ref[...])), F32)


def forces_half(half, pressure, modes):
    nodes, columns = pressure.shape
    width = modes.shape[1] // 2
    rows = row_block(nodes)
    return pl.pallas_call(
        forces_kernel,
        grid_spec=pltpu.PrefetchScalarGridSpec(
            num_scalar_prefetch=1,
            grid=(nodes // rows,),
            in_specs=[
                pl.BlockSpec((rows, columns), lambda k, h: (k, 0)),
                pl.BlockSpec((rows, width), lambda k, h: (k, h[0])),
            ],
            out_specs=[
                pl.BlockSpec((columns, width), lambda k, h: (0, 0)),
                pl.BlockSpec((8, 128), lambda k, h: (0, 0)),
            ],
        ),
        out_shape=[
            jax.ShapeDtypeStruct((columns, width), F32),
            jax.ShapeDtypeStruct((8, 128), F32),
        ],
        compiler_params=pltpu.CompilerParams(vmem_limit_bytes=16 * MIB),
        cost_estimate=pl.CostEstimate(
            flops=2 * nodes * columns * width, bytes_accessed=2 * nodes * width, transcendentals=0
        ),
        name="forces_half",
    )(half, pressure, modes)


def panel_modes_kernel(panel_ref, modes_ref, high_ref, low_ref, onehot_ref):
    @pl.when(pl.program_id(0) == 0)
    def _():
        panels = lax.broadcasted_iota(jnp.int32, onehot_ref.shape, 0)
        onehot_ref[...] = jnp.where(panels == panel_ref[...], 1.0, 0.0).astype(BF16)

    total = jnp.dot(onehot_ref[...], modes_ref[...], preferred_element_type=F32)
    high = total.astype(BF16)
    high_ref[...] = high
    low_ref[...] = (total - high.astype(F32)).astype(BF16)


def panel_modes(panel_of, modes):
    nodes, count = modes.shape
    width = 256
    return pl.pallas_call(
        panel_modes_kernel,
        grid=(count // width,),
        in_specs=[
            pl.BlockSpec((1, nodes), lambda j: (0, 0)),
            pl.BlockSpec((nodes, width), lambda j: (0, j)),
        ],
        out_specs=[pl.BlockSpec((PANEL_DEV, width), lambda j: (0, j))] * 2,
        out_shape=[jax.ShapeDtypeStruct((PANEL_DEV, count), BF16)] * 2,
        scratch_shapes=[pltpu.VMEM((PANEL_DEV, nodes), BF16)],
        compiler_params=pltpu.CompilerParams(vmem_limit_bytes=16 * MIB),
        cost_estimate=pl.CostEstimate(
            flops=2 * nodes * PANEL_DEV * count, bytes_accessed=2 * nodes * count, transcendentals=0
        ),
        name="panel_modes",
    )(panel_of.reshape(1, nodes), modes)


def sin_cos(angle):
    turns = jnp.floor(angle * (2.0 / math.pi) + 0.5)
    rest = angle - turns * 1.5703125
    rest = rest - turns * 4.837512969970703125e-4
    rest = rest - turns * 7.549789948768648e-8
    square = rest * rest
    sine = rest + rest * square * (
        -1.6666654611e-1 + square * (8.3321608736e-3 - square * 1.9515295891e-4)
    )
    cosine = (1.0 - 0.5 * square) + square * square * (
        4.166664568298827e-2 + square * (-1.388731625493765e-3 + square * 2.443315711809948e-5)
    )
    quadrant = turns.astype(jnp.int32)
    swap = (quadrant & 1) == 1
    sin_sign = jnp.where((quadrant & 2) == 2, -1.0, 1.0)
    cos_sign = jnp.where(((quadrant + 1) & 2) == 2, -1.0, 1.0)
    return jnp.where(swap, cosine, sine) * sin_sign, jnp.where(swap, sine, cosine) * cos_sign


def radiation_kernel(omega_ref, bins_ref, high_ref, low_ref):
    omega = omega_ref[pl.program_id(0)]
    dist = 1.0 + 0.05 * bins_ref[...].astype(F32)
    sine, cosine = sin_cos(omega * dist)
    gain = (-0.01 / (2.0 * math.pi)) * omega * omega / dist
    for part, value in enumerate((gain * cosine, -gain * sine)):
        high = value.astype(BF16)
        high_ref[part, 0] = high
        low_ref[part, 0] = (value - high.astype(F32)).astype(BF16)


def radiation(omega_force, bins):
    field, panels = bins.shape
    freqs = omega_force.shape[0]
    return pl.pallas_call(
        radiation_kernel,
        grid=(freqs,),
        in_specs=[
            pl.BlockSpec(memory_space=pltpu.SMEM),
            pl.BlockSpec((field, panels), lambda f: (0, 0)),
        ],
        out_specs=[pl.BlockSpec((2, 1, field, panels), lambda f: (0, f, 0, 0))] * 2,
        out_shape=[jax.ShapeDtypeStruct((2, freqs, field, panels), BF16)] * 2,
        compiler_params=pltpu.CompilerParams(vmem_limit_bytes=16 * MIB),
        cost_estimate=pl.CostEstimate(
            flops=40 * freqs * field * panels, bytes_accessed=4 * freqs * field * panels, transcendentals=0
        ),
        name="radiation",
    )(omega_force, bins)


def panel_sums_kernel(place_ref, *refs):
    *slots, high_ref, low_ref, out_ref, held_ref = refs
    core, chip = place_ref[0], place_ref[1]
    count = len(slots) // 2
    group = slots[0].shape[1]
    half = held_ref.shape[1] // 2
    width = held_ref.shape[2]
    if count == 1:
        for side in range(2):
            held_ref[side] = slots[side][...].reshape(2 * half, width)
    else:
        for side in range(2):
            for k in range(count):
                start = pl.multiple_of((chip ^ k) * group, group)
                for part in range(2):
                    held_ref[side, pl.ds(part * half + start, group), :] = slots[side * count + k][part]
    total = None
    for side in range(2):
        columns = pl.ds(pl.multiple_of((core ^ side) * width, 128), width)
        for ref in (high_ref, low_ref):
            term = lax.dot_general(held_ref[side], ref[:, columns], NT, preferred_element_type=F32)
            total = term if total is None else total + term
    out_ref[...] = total.astype(out_ref.dtype)


def panel_sums(place, slots, high, low):
    half = slots[0].shape[1] * (len(slots) // 2)
    width = slots[0].shape[2]
    vmem = pl.BlockSpec(memory_space=pltpu.VMEM)
    return pl.pallas_call(
        panel_sums_kernel,
        in_specs=[pl.BlockSpec(memory_space=pltpu.SMEM)] + [vmem] * (len(slots) + 2),
        out_specs=vmem,
        out_shape=jax.ShapeDtypeStruct((2 * half, PANEL_DEV), BF16),
        scratch_shapes=[pltpu.VMEM((2, 2 * half, width), BF16)],
        compiler_params=pltpu.CompilerParams(vmem_limit_bytes=16 * MIB),
        name="panel_sums",
    )(place, *slots, high, low)


def field_kernel(place_ref, *refs):
    *pieces, high_ref, low_ref, out_ref = refs
    parts, freqs, field, panels = high_ref.shape
    own = place_ref[2]
    total = [None, None]
    for k, piece in enumerate(pieces):
        columns = pl.ds(pl.multiple_of((own ^ k) * PANEL_DEV, PANEL_DEV), PANEL_DEV)
        for part in range(2):
            for ref in (high_ref, low_ref):
                left = ref[part, :, :, columns].reshape(freqs * field, PANEL_DEV)
                term = lax.dot_general(left, piece[...], NT, preferred_element_type=F32)
                total[part] = term if total[part] is None else total[part] + term
    columns = out_ref.shape[1]
    half = columns // 2
    column = lax.broadcasted_iota(jnp.int32, (field, columns), 1)
    freq_of = (column % half) // (half // freqs)
    sums = []
    for part in range(2):
        shaped = total[part].reshape(freqs, field, columns)
        picked = jnp.zeros((field, columns), F32)
        for f in range(freqs):
            picked = jnp.where(freq_of == f, shaped[f], picked)
        sums.append(picked)
    turned = pltpu.roll(sums[1], half, 1)
    out_ref[...] = sums[0] + jnp.where(column < half, -turned, turned)


def field_sums(place, pieces, high, low):
    parts, freqs, field, panels = high.shape
    columns = pieces[0].shape[0]
    vmem = pl.BlockSpec(memory_space=pltpu.VMEM)
    return pl.pallas_call(
        field_kernel,
        in_specs=[pl.BlockSpec(memory_space=pltpu.SMEM)] + [vmem] * (len(pieces) + 2),
        out_specs=vmem,
        out_shape=jax.ShapeDtypeStruct((field, columns), F32),
        compiler_params=pltpu.CompilerParams(vmem_limit_bytes=24 * MIB),
        name="field_sums",
    )(place, *pieces, high, low)


def tree(terms):
    while len(terms) > 1:
        terms = [a + b for a, b in zip(terms[::2], terms[1::2], strict=True)]
    return terms[0]


def swap(x, axis, size, k):
    return lax.ppermute(x, axis, [(i, i ^ k) for i in range(size)])


def pack(x, shift):
    scaled = (x * jnp.exp2(shift)).astype(F16)
    note = jnp.broadcast_to(shift.astype(F16), (*x.shape[:-1], 128))
    return jnp.concatenate([scaled, note], axis=-1)


def unpack(y):
    shift = y[(0,) * (y.ndim - 1) + (-1,)].astype(F32)
    return y[..., :-128].astype(F32) * jnp.exp2(-shift), shift


def shards(nodes_axis, field_axis):
    chips = nodes_axis // 2
    chip_bits = chips.bit_length() - 1

    def body(pressure, modes, omega_mode, damping, omega_force, panel_of, dist_bin):
        columns = pressure.shape[1]
        half = columns // 2
        width = modes.shape[1] // 2
        group = half // chips
        node = lax.axis_index("node")
        core, chip, fld = node % 2, node // 2, lax.axis_index("fld")
        place = jnp.stack([core, chip, fld]).astype(jnp.int32)

        away, away_top = forces_half((1 - core).reshape(1), pressure, modes)
        came, came_top = (swap(x, "node", nodes_axis, 1) for x in (away, away_top))
        home, home_top = forces_half(core.reshape(1), pressure, modes)
        total = (home + came).reshape(2, half, width)
        bound = jnp.maximum(home_top[0, 0] + came_top[0, 0], 1e-30)
        shift = 14.0 - jnp.ceil(jnp.log2(bound))

        packed = pack(total, shift)
        terms, shifts = [lax.dynamic_slice_in_dim(total, chip * group, group, 1)], [shift]
        for k in range(1, chips):
            piece = lax.dynamic_slice_in_dim(packed, (chip ^ k) * group, group, 1)
            value, other = unpack(swap(piece, "node", nodes_axis, 2 * k))
            terms.append(value)
            shifts.append(other)
        forces = tree(terms)
        shift = jnp.min(jnp.stack(shifts)) - chip_bits

        for bit in range(field_axis.bit_length() - 1):
            value, other = unpack(swap(pack(forces, shift), "fld", field_axis, 1 << bit))
            forces = forces + value
            shift = jnp.minimum(shift, other) - 1.0

        wmod = lax.dynamic_slice_in_dim(omega_mode, core * width, width)[None, :]
        damp = lax.dynamic_slice_in_dim(damping, core * width, width)[None, :]
        wcol = jnp.repeat(omega_force, half // omega_force.shape[0])
        wcol = lax.dynamic_slice_in_dim(wcol, chip * group, group)[:, None]
        real_part = wmod * wmod - wcol * wcol
        imag_part = 2.0 * damp * wmod * wcol
        magnitude = real_part * real_part + imag_part * imag_part
        h_real = real_part / magnitude
        h_imag = -imag_part / magnitude
        a_real = h_real * forces[0] - h_imag * forces[1]
        a_imag = h_real * forces[1] + h_imag * forces[0]
        response = jnp.stack([a_real, a_imag]).astype(BF16)

        slots = [response] + [swap(response, "node", nodes_axis, 2 * k) for k in range(1, chips)]
        slots += [swap(slot, "node", nodes_axis, 1) for slot in slots]
        if group % 16:
            order = chip ^ jnp.arange(chips)
            slots = [
                jnp.moveaxis(jnp.stack(side)[order], 0, 1).reshape(2, half, width)
                for side in (slots[:chips], slots[chips:])
            ]

        sums = panel_sums(place, slots, *panel_modes(panel_of, modes))
        pieces = [sums] + [swap(sums, "fld", field_axis, k) for k in range(1, field_axis)]
        field = field_sums(place, pieces, *radiation(omega_force, dist_bin.T))
        field = field + swap(field, "node", nodes_axis, 1)
        return tree([field] + [swap(field, "node", nodes_axis, 2 * k) for k in range(1, chips)])

    return body


def solution(mesh):
    in_specs = (
        P(("node", "fld"), None),
        P(("node", "fld"), None),
        P(),
        P(),
        P(),
        P(("node", "fld")),
        P("node", "fld"),
    )
    out_specs = P("fld", None)
    body = shards(mesh.shape["node"], mesh.shape["fld"])
    return jax.shard_map(body, mesh=mesh, in_specs=in_specs, out_specs=out_specs, check_vma=False)
```

time: 246 us -> 78 us (0.32); the launches traced: 241 us -> 77.7 us
  waiting for transfers between devices: 135 us -> 13.5 us
  matrix products: 50.1 us -> 0 us
  blocking collectives: 39.1 us -> 0 us
  starting transfers between devices: 0.04 us -> 23.8 us
  Pallas kernels: 0 us -> 20.5 us
  local copies, waits for them, and re-layouts: 1.39 us -> 13.4 us
  between operations: 14 us -> 5.24 us
    psum x1 -> x0, waiting for transfers between devices: 134 us -> none  [shards(): forces = lax.psum(local_forces, ('node', 'fld'))]
    dot_general x7 -> x0, matrix products: 50.1 us -> none  [the longest x1 8.93 us: shards(): jnp.einsum('fjx,jfr->xfr', k_real, u_real, precision=hp)]
    ppermute x0 -> x21, starting transfers between devices: none -> 23.8 us  [swap(): return lax.ppermute(x, axis, [(i, i ^ k) for i in range(size)])]
    psum x1 -> x0, blocking collectives: 23 us -> none  [shards(): return lax.psum(joined, 'node')]
    pallas_call x0 -> x6, Pallas kernels: none -> 20.5 us  [the longest x2 6.42 us: forces_half(): pl.pallas_call(forces_kernel, grid_spec=pltpu.PrefetchScalarGridSpec(num_...]
    all_gather x1 -> x0, blocking collectives: 16.1 us -> none  [shards(): piece = lax.all_gather(panel_velocity, 'fld', axis=0, tiled=True)]
    ppermute x0 -> x21, waiting for transfers between devices: none -> 13.5 us  [swap(): return lax.ppermute(x, axis, [(i, i ^ k) for i in range(size)])]
    unnamed x12 -> x20, local copies, waits for them, and re-layouts: 0.98 us -> 9.07 us
  transfers between devices with their start and end apart: 1 -> 21, of which waited for: 1 -> 12; matrix products, arithmetic and copies ran while one was open for 0% -> 3% of each run, Pallas kernels for 0% -> 18%
where the time goes in v1:
time: 78 us; the launch traced here: 77.7 us
  starting transfers between devices  23.8 us (31%)
  Pallas kernels  20.5 us (26%)
  waiting for transfers between devices  13.5 us (17%)
  local copies, waits for them, and re-layouts  13.4 us (17%)
  between operations  5.24 us (7%)
  other arithmetic  1.32 us (2%)
    ppermute x21, starting transfers between devices, swap(): return lax.ppermute(x, axis, [(i, i ^ k) for i in range(size)])  23.8 us
    ppermute x21, waiting for transfers between devices, swap(): return lax.ppermute(x, axis, [(i, i ^ k) for i in range(size)])  13.5 us
    unnamed x20, local copies, waits for them, and re-layouts  9.07 us
    pallas_call x2, Pallas kernels, forces_half(): pl.pallas_call(forces_kernel, grid_spec=pltpu.PrefetchScalarGridSpec(num_...  6.42 us
    pallas_call x1, Pallas kernels, panel_modes(): pl.pallas_call(panel_modes_kernel, grid=(count // width,), in_specs=[pl.B...  5.74 us
    pallas_call x1, Pallas kernels, radiation(): pl.pallas_call(radiation_kernel, grid=(freqs,), in_specs=[pl.BlockSpec(me...  5 us
    slice x5, local copies, waits for them, and re-layouts, unpack(): shift = y[(0,) * (y.ndim - 1) + (-1,)].astype(F32)  3 us
    pallas_call x1, Pallas kernels, field_sums(): pl.pallas_call(field_kernel, in_specs=[pl.BlockSpec(memory_space=pltpu.SM...  1.85 us
  transfers between devices with their start and end apart: 21, of which 12 were waited for; matrix products, arithmetic and copies ran while one was open for 3% of the time, Pallas kernels for 18%

profile of v1, /device:TPU:0, one launch (start us, length us, event | category | flops | bytes accessed | tf_op | source)
XLA Modules:
  0.0 77.7 jit_solution(8564300903015274868)
XLA Ops:
  0.0 3.9 %copy-done = bf16[1792,2816]{1,0:T(8,128)(2,1)S(1)} copy-done((bf16[1792,2816]{1,0:T(8,128)(2,1)S(1)}, bf16[1792,2816]{1,0:T(8,128)(2,1)}, u32[]{:S(2)}) %copy-start) | copy-done | bytes 10092568
  3.9 1.0 %copy-done.3 = bf16[1792,128]{1,0:T(8,128)(2,1)S(1)} copy-done((bf16[1792,128]{1,0:T(8,128)(2,1)S(1)}, bf16[1792,128]{1,0:T(8,128)(2,1)}, u32[]{:S(2)}) %copy-start.3) | copy-done | bytes 458776
  4.9 3.2 %forces_half.3 = (f32[128,1408]{1,0:T(8,128)S(1)}, f32[8,128]{1,0:T(8,128)S(1)}) custom-call(s32[1]{0:T(128)} %bitcast.3.half_ref, bf16[1792,128]{1,0:T(8,128)(2,1)S(1)} %copy-done.3, bf16[1792,2816]{1,0:T(8,128)(2,1)S(1)} %copy-done), custom_call_target="tpu_custom_call" | custom-call | flops 645922816 | bytes 5046272 | tf_op jit(solution)/shard_map/forces_half/pallas_call | solution.py:43
  8.1 0.5 collective-permute-start
  8.8 0.2 copy-done.4
  9.0 3.2 %forces_half.2 = (f32[128,1408]{1,0:T(8,128)S(1)}, f32[8,128]{1,0:T(8,128)S(1)}) custom-call(s32[1]{0:T(128)} %bitcast.half_ref, bf16[1792,128]{1,0:T(8,128)(2,1)S(1)} %copy-done.4, bf16[1792,2816]{1,0:T(8,128)(2,1)S(1)} %copy-done.1), custom_call_target="tpu_custom_call" | custom-call | flops 645922816 | bytes 5046272 | tf_op jit(solution)/shard_map/forces_half/pallas_call | solution.py:43
  12.3 0.5 slice.44
  12.8 0.5 slice.45
  14.7 0.1 add.86
  15.0 4.0 %collective-permute-start.4 = (f16[2,16,1536]{2,1,0:T(8,128)(2,1)S(1)}, f16[2,16,1536]{2,1,0:T(8,128)(2,1)S(1)}, u32[]{:S(2)}, u32[]{:S(2)}) collective-permute-start(f16[2,16,1536]{2,1,0:T(8,128)(2,1)S(1)} %get-tuple-element.25), channel_id=1, source_target_pairs={{0,24},{4,28},{8,16},{12,20},{16,8},{20,12},{24,0},{28,4},{1,25},{... | collective-permute-start | bytes 294920 | tf_op jit(solution)/shard_map/ppermute | solution.py:240
  18.9 0.5 collective-permute-start.3
  19.4 0.1 collective-permute-start.2
  19.7 2.4 %collective-permute-done.4 = f16[2,16,1536]{2,1,0:T(8,128)(2,1)S(1)} collective-permute-done((f16[2,16,1536]{2,1,0:T(8,128)(2,1)S(1)}, f16[2,16,1536]{2,1,0:T(8,128)(2,1)S(1)}, u32[]{:S(2)}, u32[]{:S(2)}) %collective-permute-start.4) | collective-permute-done | bytes 98336 | tf_op jit(solution)/shard_map/ppermute | solution.py:240
  22.1 0.6 slice.63
  23.4 0.5 collective-permute-done.3
  23.8 0.6 slice.61
  25.1 0.6 slice.59
  26.7 1.9 %collective-permute-start.5 = (f16[2,16,1536]{2,1,0:T(8,128)(2,1)S(1)}, f16[2,16,1536]{2,1,0:T(8,128)(2,1)S(1)}, u32[]{:S(2)}, u32[]{:S(2)}) collective-permute-start(f16[2,16,1536]{2,1,0:T(8,128)(2,1)S(1)} %concatenate.10), channel_id=1, source_target_pairs={{0,1},{1,0},{2,3},{3,2},{4,5},{5,4},{6,7},{7,6},{8,9},{9,8},{10,11... | collective-permute-start | bytes 294920 | tf_op jit(solution)/shard_map/ppermute | solution.py:240
  28.7 2.7 %collective-permute-done.5 = f16[2,16,1536]{2,1,0:T(8,128)(2,1)S(1)} collective-permute-done((f16[2,16,1536]{2,1,0:T(8,128)(2,1)S(1)}, f16[2,16,1536]{2,1,0:T(8,128)(2,1)S(1)}, u32[]{:S(2)}, u32[]{:S(2)}) %collective-permute-start.5) | collective-permute-done | bytes 98336 | tf_op jit(solution)/shard_map/ppermute | solution.py:240
  31.3 0.6 slice.65
  32.7 2.9 %collective-permute-start.6 = (f16[2,16,1536]{2,1,0:T(8,128)(2,1)S(1)}, f16[2,16,1536]{2,1,0:T(8,128)(2,1)S(1)}, u32[]{:S(2)}, u32[]{:S(2)}) collective-permute-start(f16[2,16,1536]{2,1,0:T(8,128)(2,1)S(1)} %concatenate.11), channel_id=1, source_target_pairs={{0,2},{1,3},{2,0},{3,1},{4,6},{5,7},{6,4},{7,5},{8,10},{9,11},{10,... | collective-permute-start | bytes 294920 | tf_op jit(solution)/shard_map/ppermute | solution.py:240
  35.7 2.6 %collective-permute-done.6 = f16[2,16,1536]{2,1,0:T(8,128)(2,1)S(1)} collective-permute-done((f16[2,16,1536]{2,1,0:T(8,128)(2,1)S(1)}, f16[2,16,1536]{2,1,0:T(8,128)(2,1)S(1)}, u32[]{:S(2)}, u32[]{:S(2)}) %collective-permute-start.6) | collective-permute-done | bytes 98336 | tf_op jit(solution)/shard_map/ppermute | solution.py:240
  38.3 0.6 slice.67
  39.7 0.1 subtract_convert_fusion
  39.8 3.0 %collective-permute-start.9 = (bf16[2,16,1408]{2,1,0:T(8,128)(2,1)S(1)}, bf16[2,16,1408]{2,1,0:T(8,128)(2,1)S(1)}, u32[]{:S(2)}, u32[]{:S(2)}) collective-permute-start(bf16[2,16,1408]{2,1,0:T(8,128)(2,1)S(1)} %pad_maximum_fusion.refs_0_), channel_id=1, source_target_pairs={{0,24},{4,28},{8,16},{12,20},{16,8},{20,12},{24,0},{28,4},{1,25},{... | collective-permute-start | bytes 270344 | tf_op jit(solution)/shard_map/ppermute | solution.py:240
  42.8 0.3 collective-permute-start.8
  43.0 0.4 collective-permute-start.7
  43.4 3.9 %copy-done.2 = bf16[1792,2816]{1,0:T(8,128)(2,1)S(1)} copy-done((bf16[1792,2816]{1,0:T(8,128)(2,1)S(1)}, bf16[1792,2816]{1,0:T(8,128)(2,1)}, u32[]{:S(2)}) %copy-start.2) | copy-done | bytes 10092568
  47.3 5.7 %panel_modes.1 = (bf16[256,2816]{1,0:T(8,128)(2,1)S(1)}, bf16[256,2816]{1,0:T(8,128)(2,1)S(1)}) custom-call(s32[1,1792]{1,0:T(1,128)S(1)} %reshape.223.panel_ref, bf16[1792,2816]{1,0:T(8,128)(2,1)S(1)} %copy-done.2), custom_call_target="tpu_custom_call" | custom-call | flops 2583691264 | bytes 10092544 | tf_op jit(solution)/shard_map/panel_modes/pallas_call | solution.py:84
  53.1 0.5 collective-permute-start.13
  53.7 0.4 collective-permute-start.11
  54.2 0.2 collective-permute-done.10.refs_4_
  54.4 0.2 collective-permute-done.13.refs_7_
  54.6 0.4 collective-permute-done.12.refs_6_
  54.9 0.2 collective-permute-done.11.refs_5_
  55.1 1.5 %panel_sums.1.refs_0_ = bf16[128,256]{1,0:T(8,128)(2,1)S(1)} custom-call(s32[3]{0:T(128)S(1)} %pad_add_fusion.place_ref, bf16[2,16,1408]{2,1,0:T(8,128)(2,1)S(1)} %pad_maximum_fusion.refs_0_, bf16[2,16,1408]{2,1,0:T(8,128)(2,1)S(1)} %collective-permute-done.7.refs_1_, bf16[2,16,1408]{2,1,0:T(8,128)(2,1)S(1)} %collective-permute-done.8.refs_2_, ...), custom_call_target="tpu_custom_call" | custom-call | tf_op jit(solution)/shard_map/panel_sums/pallas_call | solution.py:181
  56.6 4.8 %collective-permute-start.16 = (bf16[128,256]{1,0:T(8,128)(2,1)S(1)}, bf16[128,256]{1,0:T(8,128)(2,1)S(1)}, u32[]{:S(2)}, u32[]{:S(2)}) collective-permute-start(bf16[128,256]{1,0:T(8,128)(2,1)S(1)} %panel_sums.1.refs_0_), channel_id=1, source_target_pairs={{0,3},{1,2},{2,1},{3,0},{4,7},{5,6},{6,5},{7,4},{8,11},{9,10},{10,... | collective-permute-start | bytes 196616 | tf_op jit(solution)/shard_map/ppermute | solution.py:240
  61.4 0.6 collective-permute-start.14
  62.1 5.0 %radiation.1 = (bf16[2,8,64,1024]{3,2,1,0:T(8,128)(2,1)S(1)}, bf16[2,8,64,1024]{3,2,1,0:T(8,128)(2,1)S(1)}) custom-call(f32[8]{0:T(128)S(1)} %copy-done.6, s32[64,1024]{1,0:T(8,128)S(1)} %bitcast.16), custom_call_target="tpu_custom_call" | custom-call | flops 20971520 | bytes 2097152 | tf_op jit(solution)/shard_map/radiation/pallas_call | solution.py:135
  67.1 1.8 %field_sums.1 = f32[64,128]{1,0:T(8,128)S(1)} custom-call(s32[3]{0:T(128)S(1)} %pad_add_fusion.place_ref, bf16[128,256]{1,0:T(8,128)(2,1)S(1)} %panel_sums.1.refs_0_, bf16[128,256]{1,0:T(8,128)(2,1)S(1)} %collective-permute-done.14.refs_1_, bf16[128,256]{1,0:T(8,128)(2,1)S(1)} %collective-permute-done.15.refs_2_, ...), custom_call_target="tpu_custom_call" | custom-call | tf_op jit(solution)/shard_map/field_sums/pallas_call | solution.py:223
  69.1 1.2 %collective-permute-done.17 = f32[64,128]{1,0:T(8,128)S(1)} collective-permute-done((f32[64,128]{1,0:T(8,128)S(1)}, f32[64,128]{1,0:T(8,128)S(1)}, u32[]{:S(2)}, u32[]{:S(2)}) %collective-permute-start.17) | collective-permute-done | bytes 32800 | tf_op jit(solution)/shard_map/ppermute | solution.py:240
  70.3 2.6 %collective-permute-start.20 = (f32[64,128]{1,0:T(8,128)S(1)}, f32[64,128]{1,0:T(8,128)S(1)}, u32[]{:S(2)}, u32[]{:S(2)}) collective-permute-start(f32[64,128]{1,0:T(8,128)S(1)} %add.97), channel_id=1, source_target_pairs={{0,24},{4,28},{8,16},{12,20},{16,8},{20,12},{24,0},{28,4},{1,25},{... | collective-permute-start | bytes 98312 | tf_op jit(solution)/shard_map/ppermute | solution.py:240
  72.9 0.3 collective-permute-start.19
  73.2 0.6 collective-permute-start.18
  73.8 1.3 %collective-permute-done.20 = f32[64,128]{1,0:T(8,128)S(1)} collective-permute-done((f32[64,128]{1,0:T(8,128)S(1)}, f32[64,128]{1,0:T(8,128)S(1)}, u32[]{:S(2)}, u32[]{:S(2)}) %collective-permute-start.20) | collective-permute-done | bytes 32800 | tf_op jit(solution)/shard_map/ppermute | solution.py:240
  75.1 1.7 %collective-permute-done.19 = f32[64,128]{1,0:T(8,128)S(1)} collective-permute-done((f32[64,128]{1,0:T(8,128)S(1)}, f32[64,128]{1,0:T(8,128)S(1)}, u32[]{:S(2)}, u32[]{:S(2)}) %collective-permute-start.19) | collective-permute-done | bytes 32800 | tf_op jit(solution)/shard_map/ppermute | solution.py:240
  76.8 0.3 collective-permute-done.18
  77.1 0.6 add_add_fusion.1
  (45 shorter events, 1.2 us)
Async XLA Ops:
  0.0 3.9 %copy-start = (bf16[1792,2816]{1,0:T(8,128)(2,1)S(1)}, bf16[1792,2816]{1,0:T(8,128)(2,1)}, u32[]{:S(2)}) copy-start(bf16[1792,2816]{1,0:T(8,128)(2,1)} %modes_ref.5) | copy-start | bytes 30277636
  3.9 1.0 %copy-start.3 = (bf16[1792,128]{1,0:T(8,128)(2,1)S(1)}, bf16[1792,128]{1,0:T(8,128)(2,1)}, u32[]{:S(2)}) copy-start(bf16[1792,128]{1,0:T(8,128)(2,1)} %pressure_ref.3) | copy-start | bytes 1376260
  4.9 3.9 %copy-start.1 = (bf16[1792,2816]{1,0:T(8,128)(2,1)S(1)}, bf16[1792,2816]{1,0:T(8,128)(2,1)}, u32[]{:S(2)}) copy-start(bf16[1792,2816]{1,0:T(8,128)(2,1)} %modes_ref.5) | copy-start | bytes 30277636
  4.9 4.1 %copy-start.4 = (bf16[1792,128]{1,0:T(8,128)(2,1)S(1)}, bf16[1792,128]{1,0:T(8,128)(2,1)}, u32[]{:S(2)}) copy-start(bf16[1792,128]{1,0:T(8,128)(2,1)} %pressure_ref.3) | copy-start | bytes 1376260
  8.1 6.6 %collective-permute-start = (f32[128,1408]{1,0:T(8,128)S(1)}, f32[128,1408]{1,0:T(8,128)S(1)}, u32[]{:S(2)}, u32[]{:S(2)}) collective-permute-start(f32[128,1408]{1,0:T(8,128)S(1)} %get-tuple-element.14), channel_id=1, source_target_pairs={{0,4},{4,0},{8,12},{12,8},{16,20},{20,16},{24,28},{28,24},{1,5},{5... | collective-permute-start | bytes 2162696 | tf_op jit(solution)/shard_map/ppermute | solution.py:240
  8.6 4.1 %collective-permute-start.1 = (f32[8,128]{1,0:T(8,128)S(1)}, f32[8,128]{1,0:T(8,128)S(1)}, u32[]{:S(2)}, u32[]{:S(2)}) collective-permute-start(f32[8,128]{1,0:T(8,128)S(1)} %get-tuple-element.16), channel_id=1, source_target_pairs={{0,4},{4,0},{8,12},{12,8},{16,20},{20,16},{24,28},{28,24},{1,5},{5... | collective-permute-start | bytes 12296 | tf_op jit(solution)/shard_map/ppermute | solution.py:240
  12.2 7.4 %copy-start.6 = (f32[8]{0:T(128)S(1)}, f32[8]{0:T(128)}, u32[]{:S(2)}) copy-start(f32[8]{0:T(128)} %omega_ref.1) | copy-start | bytes 100
  12.2 7.5 %copy-start.7 = (s32[1792]{0:T(1024)S(1)}, s32[1792]{0:T(1024)}, u32[]{:S(2)}) copy-start(s32[1792]{0:T(1024)} %param.12) | copy-start | bytes 21508
  14.7 13.9 %copy-start.8 = (f32[2816]{0:T(1024)S(1)}, f32[2816]{0:T(1024)}, u32[]{:S(2)}) copy-start(f32[2816]{0:T(1024)} %param.9) | copy-start | bytes 33796
  14.7 13.9 %copy-start.9 = (f32[2816]{0:T(1024)S(1)}, f32[2816]{0:T(1024)}, u32[]{:S(2)}) copy-start(f32[2816]{0:T(1024)} %param.10) | copy-start | bytes 33796
  15.0 7.1 %collective-permute-start.4 = (f16[2,16,1536]{2,1,0:T(8,128)(2,1)S(1)}, f16[2,16,1536]{2,1,0:T(8,128)(2,1)S(1)}, u32[]{:S(2)}, u32[]{:S(2)}) collective-permute-start(f16[2,16,1536]{2,1,0:T(8,128)(2,1)S(1)} %get-tuple-element.25), channel_id=1, source_target_pairs={{0,24},{4,28},{8,16},{12,20},{16,8},{20,12},{24,0},{28,4},{1,25},{... | collective-permute-start | bytes 294920 | tf_op jit(solution)/shard_map/ppermute | solution.py:240
  18.9 4.9 %collective-permute-start.3 = (f16[2,16,1536]{2,1,0:T(8,128)(2,1)S(1)}, f16[2,16,1536]{2,1,0:T(8,128)(2,1)S(1)}, u32[]{:S(2)}, u32[]{:S(2)}) collective-permute-start(f16[2,16,1536]{2,1,0:T(8,128)(2,1)S(1)} %get-tuple-element.26), channel_id=1, source_target_pairs={{0,16},{4,20},{8,24},{12,28},{16,0},{20,4},{24,8},{28,12},{1,17},{... | collective-permute-start | bytes 294920 | tf_op jit(solution)/shard_map/ppermute | solution.py:240
  19.4 5.7 %collective-permute-start.2 = (f16[2,16,1536]{2,1,0:T(8,128)(2,1)S(1)}, f16[2,16,1536]{2,1,0:T(8,128)(2,1)S(1)}, u32[]{:S(2)}, u32[]{:S(2)}) collective-permute-start(f16[2,16,1536]{2,1,0:T(8,128)(2,1)S(1)} %get-tuple-element.27), channel_id=1, source_target_pairs={{0,8},{4,12},{8,0},{12,4},{16,24},{20,28},{24,16},{28,20},{1,9},{5... | collective-permute-start | bytes 294920 | tf_op jit(solution)/shard_map/ppermute | solution.py:240
  26.7 4.7 %collective-permute-start.5 = (f16[2,16,1536]{2,1,0:T(8,128)(2,1)S(1)}, f16[2,16,1536]{2,1,0:T(8,128)(2,1)S(1)}, u32[]{:S(2)}, u32[]{:S(2)}) collective-permute-start(f16[2,16,1536]{2,1,0:T(8,128)(2,1)S(1)} %concatenate.10), channel_id=1, source_target_pairs={{0,1},{1,0},{2,3},{3,2},{4,5},{5,4},{6,7},{7,6},{8,9},{9,8},{10,11... | collective-permute-start | bytes 294920 | tf_op jit(solution)/shard_map/ppermute | solution.py:240
  32.7 5.6 %collective-permute-start.6 = (f16[2,16,1536]{2,1,0:T(8,128)(2,1)S(1)}, f16[2,16,1536]{2,1,0:T(8,128)(2,1)S(1)}, u32[]{:S(2)}, u32[]{:S(2)}) collective-permute-start(f16[2,16,1536]{2,1,0:T(8,128)(2,1)S(1)} %concatenate.11), channel_id=1, source_target_pairs={{0,2},{1,3},{2,0},{3,1},{4,6},{5,7},{6,4},{7,5},{8,10},{9,11},{10,... | collective-permute-start | bytes 294920 | tf_op jit(solution)/shard_map/ppermute | solution.py:240
  39.8 13.3 %collective-permute-start.9 = (bf16[2,16,1408]{2,1,0:T(8,128)(2,1)S(1)}, bf16[2,16,1408]{2,1,0:T(8,128)(2,1)S(1)}, u32[]{:S(2)}, u32[]{:S(2)}) collective-permute-start(bf16[2,16,1408]{2,1,0:T(8,128)(2,1)S(1)} %pad_maximum_fusion.refs_0_), channel_id=1, source_target_pairs={{0,24},{4,28},{8,16},{12,20},{16,8},{20,12},{24,0},{28,4},{1,25},{... | collective-permute-start | bytes 270344 | tf_op jit(solution)/shard_map/ppermute | solution.py:240
  42.8 10.9 %collective-permute-start.8 = (bf16[2,16,1408]{2,1,0:T(8,128)(2,1)S(1)}, bf16[2,16,1408]{2,1,0:T(8,128)(2,1)S(1)}, u32[]{:S(2)}, u32[]{:S(2)}) collective-permute-start(bf16[2,16,1408]{2,1,0:T(8,128)(2,1)S(1)} %pad_maximum_fusion.refs_0_), channel_id=1, source_target_pairs={{0,16},{4,20},{8,24},{12,28},{16,0},{20,4},{24,8},{28,12},{1,17},{... | collective-permute-start | bytes 270344 | tf_op jit(solution)/shard_map/ppermute | solution.py:240
  43.0 10.7 %collective-permute-start.7 = (bf16[2,16,1408]{2,1,0:T(8,128)(2,1)S(1)}, bf16[2,16,1408]{2,1,0:T(8,128)(2,1)S(1)}, u32[]{:S(2)}, u32[]{:S(2)}) collective-permute-start(bf16[2,16,1408]{2,1,0:T(8,128)(2,1)S(1)} %pad_maximum_fusion.refs_0_), channel_id=1, source_target_pairs={{0,8},{4,12},{8,0},{12,4},{16,24},{20,28},{24,16},{28,20},{1,9},{5... | collective-permute-start | bytes 270344 | tf_op jit(solution)/shard_map/ppermute | solution.py:240
  43.4 3.9 %copy-start.2 = (bf16[1792,2816]{1,0:T(8,128)(2,1)S(1)}, bf16[1792,2816]{1,0:T(8,128)(2,1)}, u32[]{:S(2)}) copy-start(bf16[1792,2816]{1,0:T(8,128)(2,1)} %modes_ref.5) | copy-start | bytes 30277636
  53.0 9.0 %copy-start.5 = (s32[1024,64]{0,1:T(8,128)S(1)}, s32[1024,64]{0,1:T(8,128)}, u32[]{:S(2)}) copy-start(s32[1024,64]{0,1:T(8,128)} %param.13) | copy-start | bytes 786436
  53.1 1.4 %collective-permute-start.10 = (bf16[2,16,1408]{2,1,0:T(8,128)(2,1)S(1)}, bf16[2,16,1408]{2,1,0:T(8,128)(2,1)S(1)}, u32[]{:S(2)}, u32[]{:S(2)}) collective-permute-start(bf16[2,16,1408]{2,1,0:T(8,128)(2,1)S(1)} %pad_maximum_fusion.refs_0_), channel_id=1, source_target_pairs={{0,4},{4,0},{8,12},{12,8},{16,20},{20,16},{24,28},{28,24},{1,5},{5... | collective-permute-start | bytes 270344 | tf_op jit(solution)/shard_map/ppermute | solution.py:240
  53.1 1.4 %collective-permute-start.13 = (bf16[2,16,1408]{2,1,0:T(8,128)(2,1)S(1)}, bf16[2,16,1408]{2,1,0:T(8,128)(2,1)S(1)}, u32[]{:S(2)}, u32[]{:S(2)}) collective-permute-start(bf16[2,16,1408]{2,1,0:T(8,128)(2,1)S(1)} %collective-permute-done.9.refs_3_), channel_id=1, source_target_pairs={{0,4},{4,0},{8,12},{12,8},{16,20},{20,16},{24,28},{28,24},{1,5},{5... | collective-permute-start | bytes 270344 | tf_op jit(solution)/shard_map/ppermute | solution.py:240
  53.6 1.3 %collective-permute-start.12 = (bf16[2,16,1408]{2,1,0:T(8,128)(2,1)S(1)}, bf16[2,16,1408]{2,1,0:T(8,128)(2,1)S(1)}, u32[]{:S(2)}, u32[]{:S(2)}) collective-permute-start(bf16[2,16,1408]{2,1,0:T(8,128)(2,1)S(1)} %collective-permute-done.8.refs_2_), channel_id=1, source_target_pairs={{0,4},{4,0},{8,12},{12,8},{16,20},{20,16},{24,28},{28,24},{1,5},{5... | collective-permute-start | bytes 270344 | tf_op jit(solution)/shard_map/ppermute | solution.py:240
  53.7 1.4 %collective-permute-start.11 = (bf16[2,16,1408]{2,1,0:T(8,128)(2,1)S(1)}, bf16[2,16,1408]{2,1,0:T(8,128)(2,1)S(1)}, u32[]{:S(2)}, u32[]{:S(2)}) collective-permute-start(bf16[2,16,1408]{2,1,0:T(8,128)(2,1)S(1)} %collective-permute-done.7.refs_1_), channel_id=1, source_target_pairs={{0,4},{4,0},{8,12},{12,8},{16,20},{20,16},{24,28},{28,24},{1,5},{5... | collective-permute-start | bytes 270344 | tf_op jit(solution)/shard_map/ppermute | solution.py:240
  56.6 10.5 %collective-permute-start.16 = (bf16[128,256]{1,0:T(8,128)(2,1)S(1)}, bf16[128,256]{1,0:T(8,128)(2,1)S(1)}, u32[]{:S(2)}, u32[]{:S(2)}) collective-permute-start(bf16[128,256]{1,0:T(8,128)(2,1)S(1)} %panel_sums.1.refs_0_), channel_id=1, source_target_pairs={{0,3},{1,2},{2,1},{3,0},{4,7},{5,6},{6,5},{7,4},{8,11},{9,10},{10,... | collective-permute-start | bytes 196616 | tf_op jit(solution)/shard_map/ppermute | solution.py:240
  61.4 5.7 %collective-permute-start.15 = (bf16[128,256]{1,0:T(8,128)(2,1)S(1)}, bf16[128,256]{1,0:T(8,128)(2,1)S(1)}, u32[]{:S(2)}, u32[]{:S(2)}) collective-permute-start(bf16[128,256]{1,0:T(8,128)(2,1)S(1)} %panel_sums.1.refs_0_), channel_id=1, source_target_pairs={{0,2},{1,3},{2,0},{3,1},{4,6},{5,7},{6,4},{7,5},{8,10},{9,11},{10,... | collective-permute-start | bytes 196616 | tf_op jit(solution)/shard_map/ppermute | solution.py:240
  61.4 5.7 %collective-permute-start.14 = (bf16[128,256]{1,0:T(8,128)(2,1)S(1)}, bf16[128,256]{1,0:T(8,128)(2,1)S(1)}, u32[]{:S(2)}, u32[]{:S(2)}) collective-permute-start(bf16[128,256]{1,0:T(8,128)(2,1)S(1)} %panel_sums.1.refs_0_), channel_id=1, source_target_pairs={{0,1},{1,0},{2,3},{3,2},{4,5},{5,4},{6,7},{7,6},{8,9},{9,8},{10,11... | collective-permute-start | bytes 196616 | tf_op jit(solution)/shard_map/ppermute | solution.py:240
  69.0 1.3 %collective-permute-start.17 = (f32[64,128]{1,0:T(8,128)S(1)}, f32[64,128]{1,0:T(8,128)S(1)}, u32[]{:S(2)}, u32[]{:S(2)}) collective-permute-start(f32[64,128]{1,0:T(8,128)S(1)} %field_sums.1), channel_id=1, source_target_pairs={{0,4},{4,0},{8,12},{12,8},{16,20},{20,16},{24,28},{28,24},{1,5},{5... | collective-permute-start | bytes 98312 | tf_op jit(solution)/shard_map/ppermute | solution.py:240
  70.3 4.8 %collective-permute-start.20 = (f32[64,128]{1,0:T(8,128)S(1)}, f32[64,128]{1,0:T(8,128)S(1)}, u32[]{:S(2)}, u32[]{:S(2)}) collective-permute-start(f32[64,128]{1,0:T(8,128)S(1)} %add.97), channel_id=1, source_target_pairs={{0,24},{4,28},{8,16},{12,20},{16,8},{20,12},{24,0},{28,4},{1,25},{... | collective-permute-start | bytes 98312 | tf_op jit(solution)/shard_map/ppermute | solution.py:240
  72.9 3.9 %collective-permute-start.19 = (f32[64,128]{1,0:T(8,128)S(1)}, f32[64,128]{1,0:T(8,128)S(1)}, u32[]{:S(2)}, u32[]{:S(2)}) collective-permute-start(f32[64,128]{1,0:T(8,128)S(1)} %add.97), channel_id=1, source_target_pairs={{0,16},{4,20},{8,24},{12,28},{16,0},{20,4},{24,8},{28,12},{1,17},{... | collective-permute-start | bytes 98312 | tf_op jit(solution)/shard_map/ppermute | solution.py:240
  73.2 3.9 %collective-permute-start.18 = (f32[64,128]{1,0:T(8,128)S(1)}, f32[64,128]{1,0:T(8,128)S(1)}, u32[]{:S(2)}, u32[]{:S(2)}) collective-permute-start(f32[64,128]{1,0:T(8,128)S(1)} %add.97), channel_id=1, source_target_pairs={{0,8},{4,12},{8,0},{12,4},{16,24},{20,28},{24,16},{28,20},{1,9},{5... | collective-permute-start | bytes 98312 | tf_op jit(solution)/shard_map/ppermute | solution.py:240

commit v2 on v1

v2 whole, which is shorter than its diff:
```python
import functools
import math

import jax
import jax.numpy as jnp
from jax import lax
from jax.experimental import pallas as pl
from jax.experimental.pallas import tpu as pltpu
from jax.sharding import PartitionSpec as P

PANEL_DEV = 256
BF16, F16, F32 = jnp.bfloat16, jnp.float16, jnp.float32
NT = (((1,), (1,)), ((), ()))
MIB = 1024 * 1024


def row_block(rows):
    return next(b for b in (256, 128, 64, 32, 16, rows) if rows % b == 0)


def start_rows(modes_ref, held_ref, sems, first):
    nodes, width = held_ref.shape
    rows = nodes // sems.shape[0]
    copies = []
    for k in range(sems.shape[0]):
        block = pl.ds(k * rows, rows)
        copies.append(
            pltpu.make_async_copy(
                modes_ref.at[block, pl.ds(first, width)], held_ref.at[block, :], sems.at[k]
            )
        )
        copies[-1].start()
    return rows, copies


def forces_sums(half_ref, left_ref, modes_ref, out_ref, top_ref, held_ref, sems, ready):
    width = held_ref.shape[1]
    rows, copies = start_rows(modes_ref, held_ref, sems, pl.multiple_of(half_ref[0] * width, 128))
    ready()
    for k, copy in enumerate(copies):
        copy.wait()
        block = slice(k * rows, (k + 1) * rows)
        part = jnp.dot(left_ref[:, block], held_ref[block, :], preferred_element_type=F32)
        for t in range(width // 128):
            tile = part[:, t * 128 : (t + 1) * 128]
            out_ref[t] = tile if k == 0 else out_ref[t] + tile
    top_ref[...] = jnp.full(top_ref.shape, jnp.max(jnp.abs(out_ref[...])), F32)


def first_kernel(half_ref, pressure_ref, modes_ref, out_ref, top_ref, left_ref, loads_ref, held_ref, sem, sems):
    load = pltpu.make_async_copy(pressure_ref, loads_ref, sem)
    load.start()

    def ready():
        load.wait()
        left_ref[...] = loads_ref[...].T

    forces_sums(half_ref, left_ref, modes_ref, out_ref, top_ref, held_ref, sems, ready)


def second_kernel(half_ref, left_ref, modes_ref, out_ref, top_ref, held_ref, sems):
    forces_sums(half_ref, left_ref, modes_ref, out_ref, top_ref, held_ref, sems, lambda: None)


def forces_half(half, pressure, modes, first):
    nodes, columns = pressure.shape if first else pressure.shape[::-1]
    width = modes.shape[1] // 2
    vmem, hbm = pl.BlockSpec(memory_space=pltpu.VMEM), pl.BlockSpec(memory_space=pltpu.HBM)
    outs = [
        jax.ShapeDtypeStruct((width // 128, columns, 128), F32),
        jax.ShapeDtypeStruct((8, 128), F32),
        jax.ShapeDtypeStruct((columns, nodes), BF16),
    ][: 3 if first else 2]
    scratch = [
        pltpu.VMEM((nodes, columns), BF16),
        pltpu.VMEM((nodes, width), BF16),
        pltpu.SemaphoreType.DMA,
        pltpu.SemaphoreType.DMA((nodes // row_block(nodes),)),
    ]
    return pl.pallas_call(
        first_kernel if first else second_kernel,
        in_specs=[pl.BlockSpec(memory_space=pltpu.SMEM), hbm if first else vmem, hbm],
        out_specs=[vmem] * len(outs),
        out_shape=outs,
        scratch_shapes=scratch if first else scratch[1::2],
        compiler_params=pltpu.CompilerParams(vmem_limit_bytes=51 * MIB),
        cost_estimate=pl.CostEstimate(
            flops=2 * nodes * columns * width, bytes_accessed=2 * nodes * width, transcendentals=0
        ),
        name="forces_half",
    )(half, pressure, modes)


def panel_modes_kernel(half, panel_ref, modes_ref, high_ref, low_ref, onehot_ref, held_ref, total_ref, sems):
    width = held_ref.shape[1]
    rows, copies = start_rows(modes_ref, held_ref, sems, half * width)
    panels = lax.broadcasted_iota(jnp.int32, onehot_ref.shape, 0)
    onehot_ref[...] = jnp.where(panels == panel_ref[...], 1.0, 0.0).astype(BF16)
    for k, copy in enumerate(copies):
        copy.wait()
        block = slice(k * rows, (k + 1) * rows)
        part = jnp.dot(onehot_ref[:, block], held_ref[block, :], preferred_element_type=F32)
        total_ref[...] = part if k == 0 else total_ref[...] + part
    total = total_ref[...]
    high = total.astype(BF16)
    high_ref[...] = high
    low_ref[...] = (total - high.astype(F32)).astype(BF16)


def panel_modes(half, panel_of, modes):
    nodes, count = modes.shape
    width = count // 2
    blocks = 4 if nodes % 64 == 0 else 1
    return pl.pallas_call(
        functools.partial(panel_modes_kernel, half),
        in_specs=[pl.BlockSpec(memory_space=pltpu.VMEM), pl.BlockSpec(memory_space=pltpu.HBM)],
        out_specs=[pl.BlockSpec(memory_space=pltpu.VMEM)] * 2,
        out_shape=[jax.ShapeDtypeStruct((PANEL_DEV, width), BF16)] * 2,
        scratch_shapes=[
            pltpu.VMEM((PANEL_DEV, nodes), BF16),
            pltpu.VMEM((nodes, width), BF16),
            pltpu.VMEM((PANEL_DEV, width), F32),
            pltpu.SemaphoreType.DMA((blocks,)),
        ],
        compiler_params=pltpu.CompilerParams(vmem_limit_bytes=51 * MIB),
        cost_estimate=pl.CostEstimate(
            flops=2 * nodes * PANEL_DEV * width, bytes_accessed=2 * nodes * width, transcendentals=0
        ),
        name="panel_modes",
    )(panel_of.reshape(1, nodes), modes)


def sin_cos(angle):
    turns = jnp.floor(angle * (2.0 / math.pi) + 0.5)
    rest = angle - turns * 1.5703125
    rest = rest - turns * 4.837512969970703125e-4
    rest = rest - turns * 7.549789948768648e-8
    square = rest * rest
    sine = rest + rest * square * (
        -1.6666654611e-1 + square * (8.3321608736e-3 - square * 1.9515295891e-4)
    )
    cosine = (1.0 - 0.5 * square) + square * square * (
        4.166664568298827e-2 + square * (-1.388731625493765e-3 + square * 2.443315711809948e-5)
    )
    quadrant = turns.astype(jnp.int32)
    swap = (quadrant & 1) == 1
    sin_sign = jnp.where((quadrant & 2) == 2, -1.0, 1.0)
    cos_sign = jnp.where(((quadrant + 1) & 2) == 2, -1.0, 1.0)
    return jnp.where(swap, cosine, sine) * sin_sign, jnp.where(swap, sine, cosine) * cos_sign


def radiation_kernel(first, omega_ref, bins_ref, high_ref, low_ref, dist_ref):
    pair = pl.program_id(0)

    @pl.when(pair == 0)
    def _():
        dist = 1.0 + 0.05 * bins_ref[...].astype(F32)
        dist_ref[...] = jnp.concatenate([dist, dist], axis=0).T

    dist = dist_ref[...]
    lane = lax.broadcasted_iota(jnp.int32, (1, dist.shape[1]), 1)
    freq = first + 2 * pair
    omega = jnp.where(lane < dist.shape[1] // 2, omega_ref[freq], omega_ref[freq + 1])
    sine, cosine = sin_cos(omega * dist)
    gain = (-0.01 / (2.0 * math.pi)) * omega * omega / dist
    for part, value in enumerate((gain * cosine, -gain * sine)):
        high = value.astype(BF16)
        high_ref[part] = high
        low_ref[part] = (value - high.astype(F32)).astype(BF16)


def radiation(first, count, omega_force, bins):
    field, panels = bins.shape
    return pl.pallas_call(
        functools.partial(radiation_kernel, first),
        grid=(count // 2,),
        in_specs=[
            pl.BlockSpec(memory_space=pltpu.SMEM),
            pl.BlockSpec((field, panels), lambda q: (0, 0)),
        ],
        out_specs=[pl.BlockSpec((2, panels, 2 * field), lambda q: (0, 0, q))] * 2,
        out_shape=[jax.ShapeDtypeStruct((2, panels, count * field), BF16)] * 2,
        scratch_shapes=[pltpu.VMEM((panels, 2 * field), F32)],
        compiler_params=pltpu.CompilerParams(vmem_limit_bytes=16 * MIB),
        cost_estimate=pl.CostEstimate(
            flops=40 * count * field * panels, bytes_accessed=4 * count * field * panels, transcendentals=0
        ),
        name="radiation",
    )(omega_force, bins)


def panel_sums_kernel(place_ref, *refs):
    *slots, high0, low0, high1, low1, out_ref, held_ref = refs
    core, chip = place_ref[0], place_ref[1]
    count = len(slots) // 2
    tiles, _, group, lanes = slots[0].shape
    half = held_ref.shape[1] // 2
    for side in range(2):
        for k in range(count):
            slot = slots[side * count + k]
            start = 0 if count == 1 else pl.multiple_of((chip ^ k) * group, group)
            for part in range(2):
                for t in range(tiles):
                    held_ref[core ^ side, pl.ds(part * half + start, group), t * lanes : (t + 1) * lanes] = slot[t, part]
    total = None
    for side, pair in enumerate(((high0, low0), (high1, low1))):
        for ref in pair:
            term = lax.dot_general(held_ref[side], ref[...], NT, preferred_element_type=F32)
            total = term if total is None else total + term
    out_ref[...] = total.astype(out_ref.dtype)


def panel_sums(place, slots, first, second):
    half = slots[0].shape[2] * (len(slots) // 2)
    width = slots[0].shape[0] * slots[0].shape[3]
    vmem = pl.BlockSpec(memory_space=pltpu.VMEM)
    return pl.pallas_call(
        panel_sums_kernel,
        in_specs=[pl.BlockSpec(memory_space=pltpu.SMEM)] + [vmem] * (len(slots) + 4),
        out_specs=vmem,
        out_shape=jax.ShapeDtypeStruct((2 * half, PANEL_DEV), BF16),
        scratch_shapes=[pltpu.VMEM((2, 2 * half, width), BF16)],
        compiler_params=pltpu.CompilerParams(vmem_limit_bytes=16 * MIB),
        name="panel_sums",
    )(place, *slots, *first, *second)


def field_kernel(freqs, place_ref, *refs):
    *pieces, high0, low0, high1, low1, out_ref = refs
    own = place_ref[2]
    columns = pieces[0].shape[0]
    half = columns // 2
    field = out_ref.shape[0]
    wide = 2 * field
    parts = [None] * 4
    for k, piece in enumerate(pieces):
        rows = pl.ds(pl.multiple_of((own ^ k) * PANEL_DEV, PANEL_DEV), PANEL_DEV)
        for part in range(2):
            for side, pair in enumerate(((high0, low0), (high1, low1))):
                for ref in pair:
                    term = jnp.dot(piece[...], ref[part, rows, :], preferred_element_type=F32)
                    at = 2 * part + side
                    parts[at] = term if parts[at] is None else parts[at] + term
    row = lax.broadcasted_iota(jnp.int32, (columns, wide), 0)
    freq_of = (row % half) // (half // freqs)
    sums = []
    for part in range(2):
        picked = None
        for pair in range(freqs // 2):
            side, at = divmod(pair, freqs // 4)
            block = parts[2 * part + side][:, at * wide : (at + 1) * wide]
            picked = block if picked is None else jnp.where(freq_of // 2 == pair, block, picked)
        sums.append(jnp.where(freq_of % 2 == 1, pltpu.roll(picked, field, 1), picked))
    real = sums[0][:half] - sums[1][half:]
    imag = sums[0][half:] + sums[1][:half]
    out_ref[...] = jnp.concatenate([real, imag], axis=0).T[:field]


def field_sums(freqs, field, place, pieces, first, second):
    columns = pieces[0].shape[0]
    vmem = pl.BlockSpec(memory_space=pltpu.VMEM)
    return pl.pallas_call(
        functools.partial(field_kernel, freqs),
        in_specs=[pl.BlockSpec(memory_space=pltpu.SMEM)] + [vmem] * (len(pieces) + 4),
        out_specs=vmem,
        out_shape=jax.ShapeDtypeStruct((field, columns), F32),
        compiler_params=pltpu.CompilerParams(vmem_limit_bytes=24 * MIB),
        name="field_sums",
    )(place, *pieces, *first, *second)


def tree(terms):
    while len(terms) > 1:
        terms = [a + b for a, b in zip(terms[::2], terms[1::2], strict=True)]
    return terms[0]


def swap(x, axis, size, k):
    return lax.ppermute(x, axis, [(i, i ^ k) for i in range(size)])


def pack(x, shift):
    scaled = (x * jnp.exp2(shift)).astype(F16)
    note = jnp.broadcast_to(shift, (1, *x.shape[1:])).astype(F16)
    return jnp.concatenate([scaled, note], axis=0)


def unpack(y):
    shift = y[-1:].astype(F32)
    return y[:-1].astype(F32) * jnp.exp2(-shift), shift


def beside(x, work):
    return lax.optimization_barrier((x, work))


def shards(nodes_axis, field_axis):
    chips = nodes_axis // 2
    chip_bits = chips.bit_length() - 1

    def body(pressure, modes, omega_mode, damping, omega_force, panel_of, dist_bin):
        columns = pressure.shape[1]
        half = columns // 2
        width = modes.shape[1] // 2
        tiles = width // 128
        group = half // chips
        node = lax.axis_index("node")
        core, chip, fld = node % 2, node // 2, lax.axis_index("fld")
        place = jnp.stack([core, chip, fld]).astype(jnp.int32)

        away, away_top, left = forces_half((1 - core).reshape(1), pressure, modes, True)
        came, came_top = (swap(x, "node", nodes_axis, 1) for x in (away, away_top))
        home, home_top = forces_half(core.reshape(1), left, modes, False)
        total = (home + came).reshape(tiles, 2, half, 128)
        bound = jnp.maximum(home_top[:1] + came_top[:1], 1e-30)
        shift = jnp.broadcast_to(14.0 - jnp.ceil(jnp.log2(bound)), (1, 2, group, 128))

        packed, panel_known = beside(pack(total, shift[:, :, :1]), panel_of)
        came = [
            swap(lax.dynamic_slice_in_dim(packed, (chip ^ k) * group, group, 2), "node", nodes_axis, 2 * k)
            for k in range(1, chips)
        ]
        came, first = beside(came, panel_modes(0, panel_known, modes))
        terms, shifts = [lax.dynamic_slice_in_dim(total, chip * group, group, 2)], [shift]
        for piece in came:
            value, other = unpack(piece)
            terms.append(value)
            shifts.append(other)
        forces = tree(terms)
        shift = functools.reduce(jnp.minimum, shifts) - chip_bits

        freqs = omega_force.shape[0]
        bins, kernels = dist_bin.T, []
        steps = field_axis.bit_length() - 1
        for bit in range(steps):
            packed, bins = beside(pack(forces, shift), bins)
            came = swap(packed, "fld", field_axis, 1 << bit)
            if bit < 2:
                came, kernel = beside(came, radiation(bit * freqs // 2, freqs // 2, omega_force, bins))
                kernels.append(kernel)
            value, other = unpack(came)
            forces = forces + value
            shift = jnp.minimum(shift, other) - 1.0
        for rest in range(len(kernels), 2):
            kernels.append(radiation(rest * freqs // 2, freqs // 2, omega_force, bins))

        wmod = lax.dynamic_slice_in_dim(omega_mode, core * width, width).reshape(tiles, 1, 128)
        damp = lax.dynamic_slice_in_dim(damping, core * width, width).reshape(tiles, 1, 128)
        wcol = jnp.repeat(omega_force, half // omega_force.shape[0])
        wcol = lax.dynamic_slice_in_dim(wcol, chip * group, group)[None, :, None]
        real_part = wmod * wmod - wcol * wcol
        imag_part = 2.0 * damp * wmod * wcol
        magnitude = real_part * real_part + imag_part * imag_part
        h_real = real_part / magnitude
        h_imag = -imag_part / magnitude
        a_real = h_real * forces[:, 0] - h_imag * forces[:, 1]
        a_imag = h_real * forces[:, 1] + h_imag * forces[:, 0]
        response = jnp.stack([a_real, a_imag], axis=1).astype(BF16)

        response, panel_known = beside(response, panel_known)
        came = [swap(response, "node", nodes_axis, 2 * k) for k in range(1, chips)]
        came, second = beside(came, panel_modes(1, panel_known, modes))
        slots = [response, *came]
        slots += [swap(slot, "node", nodes_axis, 1) for slot in slots]
        if group % 16:
            order = chip ^ jnp.arange(chips)
            slots = [
                jnp.moveaxis(jnp.stack(side)[order], 0, 2).reshape(tiles, 2, half, 128)
                for side in (slots[:chips], slots[chips:])
            ]

        sums = panel_sums(place, slots, first, second)
        pieces = [sums] + [swap(sums, "fld", field_axis, k) for k in range(1, field_axis)]
        field = field_sums(freqs, dist_bin.shape[1], place, pieces, *kernels)
        field = field + swap(field, "node", nodes_axis, 1)
        return tree([field] + [swap(field, "node", nodes_axis, 2 * k) for k in range(1, chips)])

    return body


def solution(mesh):
    in_specs = (
        P(("node", "fld"), None),
        P(("node", "fld"), None),
        P(),
        P(),
        P(),
        P(("node", "fld")),
        P("node", "fld"),
    )
    out_specs = P("fld", None)
    body = shards(mesh.shape["node"], mesh.shape["fld"])
    return jax.shard_map(body, mesh=mesh, in_specs=in_specs, out_specs=out_specs, check_vma=False)
```

time: 78 us -> 61.6 us (0.79)
  local copies, waits for them, and re-layouts: 13.4 us -> 1.3 us
  between operations: 5.24 us -> 0.31 us
  Pallas kernels: 20.5 us -> 22.9 us
  starting transfers between devices: 23.8 us -> 21.6 us
    unnamed x20 -> x12, local copies, waits for them, and re-layouts: 9.07 us -> 1.04 us
    slice x7 -> x0, local copies, waits for them, and re-layouts: 4.05 us -> none  [the longest x5 3 us: unpack(): shift = y[(0,) * (y.ndim - 1) + (-1,)].astype(F32)]
    pallas_call x5 -> x7, Pallas kernels: 19 us -> 21.3 us  [the longest x2 7 us: panel_modes(): pl.pallas_call(functools.partial(panel_modes_kernel, half), in_specs=[pl....]
    ppermute x21, starting transfers between devices: 23.8 us -> 21.6 us  [swap(): return lax.ppermute(x, axis, [(i, i ^ k) for i in range(size)])]
  transfers between devices with their start and end apart: 21 -> 21, of which waited for: 12 -> 15; matrix products, arithmetic and copies ran while one was open for 3% -> 1% of each run, Pallas kernels for 18% -> 27%
where the time goes in v2:
time: 61.6 us; the launch traced here: 61.4 us
  Pallas kernels  22.9 us (37%)
  starting transfers between devices  21.6 us (35%)
  waiting for transfers between devices  13.7 us (22%)
  other arithmetic  1.62 us (3%)
  local copies, waits for them, and re-layouts  1.3 us (2%)
    ppermute x21, starting transfers between devices, swap(): return lax.ppermute(x, axis, [(i, i ^ k) for i in range(size)])  21.6 us
    ppermute x21, waiting for transfers between devices, swap(): return lax.ppermute(x, axis, [(i, i ^ k) for i in range(size)])  13.7 us
    pallas_call x2, Pallas kernels, panel_modes(): pl.pallas_call(functools.partial(panel_modes_kernel, half), in_specs=[pl....  7 us
    pallas_call x2, Pallas kernels, forces_half(): pl.pallas_call(first_kernel if first else second_kernel, in_specs=[pl.Blo...  6.66 us
    pallas_call x2, Pallas kernels, radiation(): pl.pallas_call(functools.partial(radiation_kernel, first), grid=(count //...  6.24 us
    pallas_call x1, Pallas kernels, panel_sums(): pl.pallas_call(panel_sums_kernel, in_specs=[pl.BlockSpec(memory_space=plt...  1.61 us
    pallas_call x1, Pallas kernels, field_sums(): pl.pallas_call(functools.partial(field_kernel, freqs), in_specs=[pl.Block...  1.4 us
  transfers between devices with their start and end apart: 21, of which 15 were waited for; matrix products, arithmetic and copies ran while one was open for 1% of the time, Pallas kernels for 27%

profile of v2, /device:TPU:0, one launch (start us, length us, event | category | flops | bytes accessed | tf_op | source)
XLA Modules:
  0.0 61.4 jit_solution(11214186085480765711)
XLA Ops:
  0.0 1.0 %copy-done.1 = bf16[1792,128]{1,0:T(8,128)(2,1)S(1)} copy-done((bf16[1792,128]{1,0:T(8,128)(2,1)S(1)}, bf16[1792,128]{1,0:T(8,128)(2,1)}, u32[]{:S(2)}) %copy-start.1) | copy-done | bytes 458776
  1.0 3.5 %forces_half.2 = (f32[11,128,128]{2,1,0:T(8,128)S(1)}, f32[8,128]{1,0:T(8,128)S(1)}, bf16[128,1792]{1,0:T(8,128)(2,1)S(1)}) custom-call(s32[1]{0:T(128)} %bitcast.5.half_ref, bf16[1792,128]{1,0:T(8,128)(2,1)S(1)} %copy-done.1, bf16[1792,2816]{1,0:T(8,128)(2,1)} %modes_ref.7), custom_call_target="tpu_custom_call" | custom-call | flops 645922816 | bytes 5046272 | tf_op jit(solution)/shard_map/forces_half/pallas_call | solution.py:80
  4.5 0.5 collective-permute-start
  5.0 0.1 collective-permute-start.1
  5.1 3.2 %forces_half.3 = (f32[11,128,128]{2,1,0:T(8,128)S(1)}, f32[8,128]{1,0:T(8,128)S(1)}) custom-call(s32[1]{0:T(128)} %bitcast.half_ref, bf16[128,1792]{1,0:T(8,128)(2,1)S(1)} %get-tuple-element.42.left_ref, bf16[1792,2816]{1,0:T(8,128)(2,1)} %modes_ref.7), custom_call_target="tpu_custom_call" | custom-call | flops 645922816 | bytes 5046272 | tf_op jit(solution)/shard_map/forces_half/pallas_call | solution.py:80
  8.5 0.1 reshape.81
  8.6 0.1 add.79
  8.7 0.1 multiply_convert_fusion
  8.8 0.1 pad_maximum_fusion
  8.9 0.1 constant_dynamic-slice_fusion
  9.0 3.9 %collective-permute-start.4 = (f16[12,2,16,128]{3,2,1,0:T(8,128)(2,1)S(1)}, f16[12,2,16,128]{3,2,1,0:T(8,128)(2,1)S(1)}, u32[]{:S(2)}, u32[]{:S(2)}) collective-permute-start(f16[12,2,16,128]{3,2,1,0:T(8,128)(2,1)S(1)} %get-tuple-element.87), channel_id=1, source_target_pairs={{0,24},{4,28},{8,16},{12,20},{16,8},{20,12},{24,0},{28,4},{1,25},{... | collective-permute-start | bytes 294920 | tf_op jit(solution)/shard_map/ppermute | solution.py:279
  13.0 0.5 collective-permute-start.3
  13.5 0.1 collective-permute-start.2
  13.6 3.5 %panel_modes.2 = (bf16[256,1408]{1,0:T(8,128)(2,1)S(1)}, bf16[256,1408]{1,0:T(8,128)(2,1)S(1)}) custom-call(s32[1,1792]{1,0:T(1,128)S(1)} %reshape.84.panel_ref, bf16[1792,2816]{1,0:T(8,128)(2,1)} %modes_ref.7), custom_call_target="tpu_custom_call" | custom-call | flops 1291845632 | bytes 5046272 | tf_op jit(solution)/shard_map/panel_modes/pallas_call | solution.py:114
  17.1 1.0 %collective-permute-done.3 = f16[12,2,16,128]{3,2,1,0:T(8,128)(2,1)S(1)} collective-permute-done((f16[12,2,16,128]{3,2,1,0:T(8,128)(2,1)S(1)}, f16[12,2,16,128]{3,2,1,0:T(8,128)(2,1)S(1)}, u32[]{:S(2)}, u32[]{:S(2)}) %collective-permute-start.3) | collective-permute-done | bytes 98336 | tf_op jit(solution)/shard_map/ppermute | solution.py:279
  18.1 0.3 collective-permute-done.2
  18.4 0.1 multiply_convert_fusion.2
  18.5 1.6 %collective-permute-start.5 = (f16[12,2,16,128]{3,2,1,0:T(8,128)(2,1)S(1)}, f16[12,2,16,128]{3,2,1,0:T(8,128)(2,1)S(1)}, u32[]{:S(2)}, u32[]{:S(2)}) collective-permute-start(f16[12,2,16,128]{3,2,1,0:T(8,128)(2,1)S(1)} %pad_maximum_fusion.1), channel_id=1, source_target_pairs={{0,1},{1,0},{2,3},{3,2},{4,5},{5,4},{6,7},{7,6},{8,9},{9,8},{10,11... | collective-permute-start | bytes 294920 | tf_op jit(solution)/shard_map/ppermute | solution.py:279
  20.3 3.0 %radiation.2 = (bf16[2,1024,256]{2,1,0:T(8,128)(2,1)S(1)}, bf16[2,1024,256]{2,1,0:T(8,128)(2,1)S(1)}) custom-call(f32[8]{0:T(128)S(1)} %copy-done.2, s32[64,1024]{1,0:T(8,128)S(1)} %bitcast.27), custom_call_target="tpu_custom_call" | custom-call | flops 10485760 | bytes 1048576 | tf_op jit(solution)/shard_map/radiation/pallas_call | solution.py:174
  23.4 2.7 %collective-permute-start.6 = (f16[12,2,16,128]{3,2,1,0:T(8,128)(2,1)S(1)}, f16[12,2,16,128]{3,2,1,0:T(8,128)(2,1)S(1)}, u32[]{:S(2)}, u32[]{:S(2)}) collective-permute-start(f16[12,2,16,128]{3,2,1,0:T(8,128)(2,1)S(1)} %pad_maximum_fusion.2), channel_id=1, source_target_pairs={{0,2},{1,3},{2,0},{3,1},{4,6},{5,7},{6,4},{7,5},{8,10},{9,11},{10,... | collective-permute-start | bytes 294920 | tf_op jit(solution)/shard_map/ppermute | solution.py:279
  26.1 3.2 %radiation.3 = (bf16[2,1024,256]{2,1,0:T(8,128)(2,1)S(1)}, bf16[2,1024,256]{2,1,0:T(8,128)(2,1)S(1)}) custom-call(f32[8]{0:T(128)S(1)} %copy-done.2, s32[64,1024]{1,0:T(8,128)S(1)} %bitcast.28), custom_call_target="tpu_custom_call" | custom-call | flops 10485760 | bytes 1048576 | tf_op jit(solution)/shard_map/radiation/pallas_call | solution.py:174
  29.4 1.3 %collective-permute-done.6 = f16[12,2,16,128]{3,2,1,0:T(8,128)(2,1)S(1)} collective-permute-done((f16[12,2,16,128]{3,2,1,0:T(8,128)(2,1)S(1)}, f16[12,2,16,128]{3,2,1,0:T(8,128)(2,1)S(1)}, u32[]{:S(2)}, u32[]{:S(2)}) %collective-permute-start.6) | collective-permute-done | bytes 98336 | tf_op jit(solution)/shard_map/ppermute | solution.py:279
  30.7 0.1 subtract_convert_fusion
  30.9 1.2 %collective-permute-start.9 = (bf16[11,2,16,128]{3,2,1,0:T(8,128)(2,1)S(1)}, bf16[11,2,16,128]{3,2,1,0:T(8,128)(2,1)S(1)}, u32[]{:S(2)}, u32[]{:S(2)}) collective-permute-start(bf16[11,2,16,128]{3,2,1,0:T(8,128)(2,1)S(1)} %pad_maximum_fusion.3.refs_0_), channel_id=1, source_target_pairs={{0,24},{4,28},{8,16},{12,20},{16,8},{20,12},{24,0},{28,4},{1,25},{... | collective-permute-start | bytes 270344 | tf_op jit(solution)/shard_map/ppermute | solution.py:279
  32.1 2.0 %collective-permute-start.8 = (bf16[11,2,16,128]{3,2,1,0:T(8,128)(2,1)S(1)}, bf16[11,2,16,128]{3,2,1,0:T(8,128)(2,1)S(1)}, u32[]{:S(2)}, u32[]{:S(2)}) collective-permute-start(bf16[11,2,16,128]{3,2,1,0:T(8,128)(2,1)S(1)} %pad_maximum_fusion.3.refs_0_), channel_id=1, source_target_pairs={{0,16},{4,20},{8,24},{12,28},{16,0},{20,4},{24,8},{28,12},{1,17},{... | collective-permute-start | bytes 270344 | tf_op jit(solution)/shard_map/ppermute | solution.py:279
  34.2 0.3 collective-permute-start.7
  34.5 3.5 %panel_modes.3 = (bf16[256,1408]{1,0:T(8,128)(2,1)S(1)}, bf16[256,1408]{1,0:T(8,128)(2,1)S(1)}) custom-call(s32[1,1792]{1,0:T(1,128)S(1)} %reshape.85.panel_ref, bf16[1792,2816]{1,0:T(8,128)(2,1)} %modes_ref.7), custom_call_target="tpu_custom_call" | custom-call | flops 1291845632 | bytes 5046272 | tf_op jit(solution)/shard_map/panel_modes/pallas_call | solution.py:114
  38.0 0.8 %collective-permute-done.8.refs_2_ = bf16[11,2,16,128]{3,2,1,0:T(8,128)(2,1)S(1)} collective-permute-done((bf16[11,2,16,128]{3,2,1,0:T(8,128)(2,1)S(1)}, bf16[11,2,16,128]{3,2,1,0:T(8,128)(2,1)S(1)}, u32[]{:S(2)}, u32[]{:S(2)}) %collective-permute-start.8) | collective-permute-done | bytes 90144 | tf_op jit(solution)/shard_map/ppermute | solution.py:279
  38.8 0.3 collective-permute-done.7.refs_1_
  39.1 0.5 collective-permute-start.12
  39.7 0.7 %collective-permute-done.11.refs_5_ = bf16[11,2,16,128]{3,2,1,0:T(8,128)(2,1)S(1)} collective-permute-done((bf16[11,2,16,128]{3,2,1,0:T(8,128)(2,1)S(1)}, bf16[11,2,16,128]{3,2,1,0:T(8,128)(2,1)S(1)}, u32[]{:S(2)}, u32[]{:S(2)}) %collective-permute-start.11) | collective-permute-done | bytes 90144 | tf_op jit(solution)/shard_map/ppermute | solution.py:279
  40.4 0.2 collective-permute-done.12.refs_6_
  40.5 0.4 collective-permute-done.13.refs_7_
  40.9 1.6 %panel_sums.1.refs_0_ = bf16[128,256]{1,0:T(8,128)(2,1)S(1)} custom-call(s32[3]{0:T(128)S(1)} %pad_add_fusion.place_ref, bf16[11,2,16,128]{3,2,1,0:T(8,128)(2,1)S(1)} %pad_maximum_fusion.3.refs_0_, bf16[11,2,16,128]{3,2,1,0:T(8,128)(2,1)S(1)} %collective-permute-done.7.refs_1_, bf16[11,2,16,128]{3,2,1,0:T(8,128)(2,1)S(1)} %collective-permute-done.8.refs_2_, ...), custom_call_target="tpu_custom_call" | custom-call | tf_op jit(solution)/shard_map/panel_sums/pallas_call | solution.py:217
  42.5 3.1 %collective-permute-start.16 = (bf16[128,256]{1,0:T(8,128)(2,1)S(1)}, bf16[128,256]{1,0:T(8,128)(2,1)S(1)}, u32[]{:S(2)}, u32[]{:S(2)}) collective-permute-start(bf16[128,256]{1,0:T(8,128)(2,1)S(1)} %panel_sums.1.refs_0_), channel_id=1, source_target_pairs={{0,3},{1,2},{2,1},{3,0},{4,7},{5,6},{6,5},{7,4},{8,11},{9,10},{10,... | collective-permute-start | bytes 196616 | tf_op jit(solution)/shard_map/ppermute | solution.py:279
  45.7 1.3 %collective-permute-start.14 = (bf16[128,256]{1,0:T(8,128)(2,1)S(1)}, bf16[128,256]{1,0:T(8,128)(2,1)S(1)}, u32[]{:S(2)}, u32[]{:S(2)}) collective-permute-start(bf16[128,256]{1,0:T(8,128)(2,1)S(1)} %panel_sums.1.refs_0_), channel_id=1, source_target_pairs={{0,1},{1,0},{2,3},{3,2},{4,5},{5,4},{6,7},{7,6},{8,9},{9,8},{10,11... | collective-permute-start | bytes 196616 | tf_op jit(solution)/shard_map/ppermute | solution.py:279
  47.0 2.3 %collective-permute-done.16.refs_3_ = bf16[128,256]{1,0:T(8,128)(2,1)S(1)} collective-permute-done((bf16[128,256]{1,0:T(8,128)(2,1)S(1)}, bf16[128,256]{1,0:T(8,128)(2,1)S(1)}, u32[]{:S(2)}, u32[]{:S(2)}) %collective-permute-start.16) | collective-permute-done | bytes 65568 | tf_op jit(solution)/shard_map/ppermute | solution.py:279
  49.3 2.1 %collective-permute-done.15.refs_2_ = bf16[128,256]{1,0:T(8,128)(2,1)S(1)} collective-permute-done((bf16[128,256]{1,0:T(8,128)(2,1)S(1)}, bf16[128,256]{1,0:T(8,128)(2,1)S(1)}, u32[]{:S(2)}, u32[]{:S(2)}) %collective-permute-start.15) | collective-permute-done | bytes 65568 | tf_op jit(solution)/shard_map/ppermute | solution.py:279
  51.4 0.1 collective-permute-done.14.refs_1_
  51.5 1.4 %field_sums.1 = f32[64,128]{1,0:T(8,128)S(1)} custom-call(s32[3]{0:T(128)S(1)} %pad_add_fusion.place_ref, bf16[128,256]{1,0:T(8,128)(2,1)S(1)} %panel_sums.1.refs_0_, bf16[128,256]{1,0:T(8,128)(2,1)S(1)} %collective-permute-done.14.refs_1_, bf16[128,256]{1,0:T(8,128)(2,1)S(1)} %collective-permute-done.15.refs_2_, ...), custom_call_target="tpu_custom_call" | custom-call | tf_op jit(solution)/shard_map/field_sums/pallas_call | solution.py:262
  53.0 1.2 %collective-permute-done.17 = f32[64,128]{1,0:T(8,128)S(1)} collective-permute-done((f32[64,128]{1,0:T(8,128)S(1)}, f32[64,128]{1,0:T(8,128)S(1)}, u32[]{:S(2)}, u32[]{:S(2)}) %collective-permute-start.17) | collective-permute-done | bytes 32800 | tf_op jit(solution)/shard_map/ppermute | solution.py:279
  54.2 1.3 %collective-permute-start.20 = (f32[64,128]{1,0:T(8,128)S(1)}, f32[64,128]{1,0:T(8,128)S(1)}, u32[]{:S(2)}, u32[]{:S(2)}) collective-permute-start(f32[64,128]{1,0:T(8,128)S(1)} %add.90), channel_id=1, source_target_pairs={{0,24},{4,28},{8,16},{12,20},{16,8},{20,12},{24,0},{28,4},{1,25},{... | collective-permute-start | bytes 98312 | tf_op jit(solution)/shard_map/ppermute | solution.py:279
  55.5 1.4 %collective-permute-start.19 = (f32[64,128]{1,0:T(8,128)S(1)}, f32[64,128]{1,0:T(8,128)S(1)}, u32[]{:S(2)}, u32[]{:S(2)}) collective-permute-start(f32[64,128]{1,0:T(8,128)S(1)} %add.90), channel_id=1, source_target_pairs={{0,16},{4,20},{8,24},{12,28},{16,0},{20,4},{24,8},{28,12},{1,17},{... | collective-permute-start | bytes 98312 | tf_op jit(solution)/shard_map/ppermute | solution.py:279
  56.9 0.8 %collective-permute-start.18 = (f32[64,128]{1,0:T(8,128)S(1)}, f32[64,128]{1,0:T(8,128)S(1)}, u32[]{:S(2)}, u32[]{:S(2)}) collective-permute-start(f32[64,128]{1,0:T(8,128)S(1)} %add.90), channel_id=1, source_target_pairs={{0,8},{4,12},{8,0},{12,4},{16,24},{20,28},{24,16},{28,20},{1,9},{5... | collective-permute-start | bytes 98312 | tf_op jit(solution)/shard_map/ppermute | solution.py:279
  57.7 1.3 %collective-permute-done.20 = f32[64,128]{1,0:T(8,128)S(1)} collective-permute-done((f32[64,128]{1,0:T(8,128)S(1)}, f32[64,128]{1,0:T(8,128)S(1)}, u32[]{:S(2)}, u32[]{:S(2)}) %collective-permute-start.20) | collective-permute-done | bytes 32800 | tf_op jit(solution)/shard_map/ppermute | solution.py:279
  59.0 0.4 collective-permute-done.19
  59.4 1.4 %collective-permute-done.18 = f32[64,128]{1,0:T(8,128)S(1)} collective-permute-done((f32[64,128]{1,0:T(8,128)S(1)}, f32[64,128]{1,0:T(8,128)S(1)}, u32[]{:S(2)}, u32[]{:S(2)}) %collective-permute-start.18) | collective-permute-done | bytes 32800 | tf_op jit(solution)/shard_map/ppermute | solution.py:279
  60.8 0.6 %add_add_fusion.1 = f32[64,128]{1,0:T(8,128)} fusion(f32[64,128]{1,0:T(8,128)S(1)} %collective-permute-done.19, f32[64,128]{1,0:T(8,128)S(1)} %collective-permute-done.20, f32[64,128]{1,0:T(8,128)S(1)} %add.90, f32[64,128]{1,0:T(8,128)S(1)} %collective-permute-done.18), kind=kLoop, calls=%fused_computation.18 | loop fusion | flops 24576 | bytes 163840 | tf_op jit(solution)/shard_map/add | solution.py:274
  (40 shorter events, 0.8 us)
Async XLA Ops:
  0.0 1.0 %copy-start.1 = (bf16[1792,128]{1,0:T(8,128)(2,1)S(1)}, bf16[1792,128]{1,0:T(8,128)(2,1)}, u32[]{:S(2)}) copy-start(bf16[1792,128]{1,0:T(8,128)(2,1)} %pressure_ref.1) | copy-start | bytes 1376260
  1.0 7.4 %copy-start.2 = (f32[8]{0:T(128)S(1)}, f32[8]{0:T(128)}, u32[]{:S(2)}) copy-start(f32[8]{0:T(128)} %omega_ref.3) | copy-start | bytes 100
  1.0 7.9 %copy-start.3 = (s32[1792]{0:T(1024)S(1)}, s32[1792]{0:T(1024)}, u32[]{:S(2)}) copy-start(s32[1792]{0:T(1024)} %param.12) | copy-start | bytes 21508
  4.5 4.1 %collective-permute-start = (f32[11,128,128]{2,1,0:T(8,128)S(1)}, f32[11,128,128]{2,1,0:T(8,128)S(1)}, u32[]{:S(2)}, u32[]{:S(2)}) collective-permute-start(f32[11,128,128]{2,1,0:T(8,128)S(1)} %get-tuple-element.44), channel_id=1, source_target_pairs={{0,4},{4,0},{8,12},{12,8},{16,20},{20,16},{24,28},{28,24},{1,5},{5... | collective-permute-start | bytes 2162696 | tf_op jit(solution)/shard_map/ppermute | solution.py:279
  5.0 3.5 %collective-permute-start.1 = (f32[8,128]{1,0:T(8,128)S(1)}, f32[8,128]{1,0:T(8,128)S(1)}, u32[]{:S(2)}, u32[]{:S(2)}) collective-permute-start(f32[8,128]{1,0:T(8,128)S(1)} %get-tuple-element.46), channel_id=1, source_target_pairs={{0,4},{4,0},{8,12},{12,8},{16,20},{20,16},{24,28},{28,24},{1,5},{5... | collective-permute-start | bytes 12296 | tf_op jit(solution)/shard_map/ppermute | solution.py:279
  8.3 11.9 %copy-start.4 = (f32[2816]{0:T(1024)S(1)}, f32[2816]{0:T(1024)}, u32[]{:S(2)}) copy-start(f32[2816]{0:T(1024)} %param.9) | copy-start | bytes 33796
  8.3 11.9 %copy-start.5 = (f32[2816]{0:T(1024)S(1)}, f32[2816]{0:T(1024)}, u32[]{:S(2)}) copy-start(f32[2816]{0:T(1024)} %param.10) | copy-start | bytes 33796
  8.3 11.9 %copy-start = (s32[1024,64]{0,1:T(8,128)S(1)}, s32[1024,64]{0,1:T(8,128)}, u32[]{:S(2)}) copy-start(s32[1024,64]{0,1:T(8,128)} %param.13) | copy-start | bytes 786436
  9.0 8.1 %collective-permute-start.4 = (f16[12,2,16,128]{3,2,1,0:T(8,128)(2,1)S(1)}, f16[12,2,16,128]{3,2,1,0:T(8,128)(2,1)S(1)}, u32[]{:S(2)}, u32[]{:S(2)}) collective-permute-start(f16[12,2,16,128]{3,2,1,0:T(8,128)(2,1)S(1)} %get-tuple-element.87), channel_id=1, source_target_pairs={{0,24},{4,28},{8,16},{12,20},{16,8},{20,12},{24,0},{28,4},{1,25},{... | collective-permute-start | bytes 294920 | tf_op jit(solution)/shard_map/ppermute | solution.py:279
  13.0 5.1 %collective-permute-start.3 = (f16[12,2,16,128]{3,2,1,0:T(8,128)(2,1)S(1)}, f16[12,2,16,128]{3,2,1,0:T(8,128)(2,1)S(1)}, u32[]{:S(2)}, u32[]{:S(2)}) collective-permute-start(f16[12,2,16,128]{3,2,1,0:T(8,128)(2,1)S(1)} %get-tuple-element.88), channel_id=1, source_target_pairs={{0,16},{4,20},{8,24},{12,28},{16,0},{20,4},{24,8},{28,12},{1,17},{... | collective-permute-start | bytes 294920 | tf_op jit(solution)/shard_map/ppermute | solution.py:279
  13.5 4.9 %collective-permute-start.2 = (f16[12,2,16,128]{3,2,1,0:T(8,128)(2,1)S(1)}, f16[12,2,16,128]{3,2,1,0:T(8,128)(2,1)S(1)}, u32[]{:S(2)}, u32[]{:S(2)}) collective-permute-start(f16[12,2,16,128]{3,2,1,0:T(8,128)(2,1)S(1)} %get-tuple-element.89), channel_id=1, source_target_pairs={{0,8},{4,12},{8,0},{12,4},{16,24},{20,28},{24,16},{28,20},{1,9},{5... | collective-permute-start | bytes 294920 | tf_op jit(solution)/shard_map/ppermute | solution.py:279
  18.5 4.8 %collective-permute-start.5 = (f16[12,2,16,128]{3,2,1,0:T(8,128)(2,1)S(1)}, f16[12,2,16,128]{3,2,1,0:T(8,128)(2,1)S(1)}, u32[]{:S(2)}, u32[]{:S(2)}) collective-permute-start(f16[12,2,16,128]{3,2,1,0:T(8,128)(2,1)S(1)} %pad_maximum_fusion.1), channel_id=1, source_target_pairs={{0,1},{1,0},{2,3},{3,2},{4,5},{5,4},{6,7},{7,6},{8,9},{9,8},{10,11... | collective-permute-start | bytes 294920 | tf_op jit(solution)/shard_map/ppermute | solution.py:279
  23.4 7.2 %collective-permute-start.6 = (f16[12,2,16,128]{3,2,1,0:T(8,128)(2,1)S(1)}, f16[12,2,16,128]{3,2,1,0:T(8,128)(2,1)S(1)}, u32[]{:S(2)}, u32[]{:S(2)}) collective-permute-start(f16[12,2,16,128]{3,2,1,0:T(8,128)(2,1)S(1)} %pad_maximum_fusion.2), channel_id=1, source_target_pairs={{0,2},{1,3},{2,0},{3,1},{4,6},{5,7},{6,4},{7,5},{8,10},{9,11},{10,... | collective-permute-start | bytes 294920 | tf_op jit(solution)/shard_map/ppermute | solution.py:279
  30.8 8.8 %collective-permute-start.10 = (bf16[11,2,16,128]{3,2,1,0:T(8,128)(2,1)S(1)}, bf16[11,2,16,128]{3,2,1,0:T(8,128)(2,1)S(1)}, u32[]{:S(2)}, u32[]{:S(2)}) collective-permute-start(bf16[11,2,16,128]{3,2,1,0:T(8,128)(2,1)S(1)} %pad_maximum_fusion.3.refs_0_), channel_id=1, source_target_pairs={{0,4},{4,0},{8,12},{12,8},{16,20},{20,16},{24,28},{28,24},{1,5},{5... | collective-permute-start | bytes 270344 | tf_op jit(solution)/shard_map/ppermute | solution.py:279
  30.9 7.1 %collective-permute-start.9 = (bf16[11,2,16,128]{3,2,1,0:T(8,128)(2,1)S(1)}, bf16[11,2,16,128]{3,2,1,0:T(8,128)(2,1)S(1)}, u32[]{:S(2)}, u32[]{:S(2)}) collective-permute-start(bf16[11,2,16,128]{3,2,1,0:T(8,128)(2,1)S(1)} %pad_maximum_fusion.3.refs_0_), channel_id=1, source_target_pairs={{0,24},{4,28},{8,16},{12,20},{16,8},{20,12},{24,0},{28,4},{1,25},{... | collective-permute-start | bytes 270344 | tf_op jit(solution)/shard_map/ppermute | solution.py:279
  32.1 6.6 %collective-permute-start.8 = (bf16[11,2,16,128]{3,2,1,0:T(8,128)(2,1)S(1)}, bf16[11,2,16,128]{3,2,1,0:T(8,128)(2,1)S(1)}, u32[]{:S(2)}, u32[]{:S(2)}) collective-permute-start(bf16[11,2,16,128]{3,2,1,0:T(8,128)(2,1)S(1)} %pad_maximum_fusion.3.refs_0_), channel_id=1, source_target_pairs={{0,16},{4,20},{8,24},{12,28},{16,0},{20,4},{24,8},{28,12},{1,17},{... | collective-permute-start | bytes 270344 | tf_op jit(solution)/shard_map/ppermute | solution.py:279
  34.2 4.9 %collective-permute-start.7 = (bf16[11,2,16,128]{3,2,1,0:T(8,128)(2,1)S(1)}, bf16[11,2,16,128]{3,2,1,0:T(8,128)(2,1)S(1)}, u32[]{:S(2)}, u32[]{:S(2)}) collective-permute-start(bf16[11,2,16,128]{3,2,1,0:T(8,128)(2,1)S(1)} %pad_maximum_fusion.3.refs_0_), channel_id=1, source_target_pairs={{0,8},{4,12},{8,0},{12,4},{16,24},{20,28},{24,16},{28,20},{1,9},{5... | collective-permute-start | bytes 270344 | tf_op jit(solution)/shard_map/ppermute | solution.py:279
  39.1 1.3 %collective-permute-start.11 = (bf16[11,2,16,128]{3,2,1,0:T(8,128)(2,1)S(1)}, bf16[11,2,16,128]{3,2,1,0:T(8,128)(2,1)S(1)}, u32[]{:S(2)}, u32[]{:S(2)}) collective-permute-start(bf16[11,2,16,128]{3,2,1,0:T(8,128)(2,1)S(1)} %collective-permute-done.7.refs_1_), channel_id=1, source_target_pairs={{0,4},{4,0},{8,12},{12,8},{16,20},{20,16},{24,28},{28,24},{1,5},{5... | collective-permute-start | bytes 270344 | tf_op jit(solution)/shard_map/ppermute | solution.py:279
  39.1 1.4 %collective-permute-start.12 = (bf16[11,2,16,128]{3,2,1,0:T(8,128)(2,1)S(1)}, bf16[11,2,16,128]{3,2,1,0:T(8,128)(2,1)S(1)}, u32[]{:S(2)}, u32[]{:S(2)}) collective-permute-start(bf16[11,2,16,128]{3,2,1,0:T(8,128)(2,1)S(1)} %collective-permute-done.8.refs_2_), channel_id=1, source_target_pairs={{0,4},{4,0},{8,12},{12,8},{16,20},{20,16},{24,28},{28,24},{1,5},{5... | collective-permute-start | bytes 270344 | tf_op jit(solution)/shard_map/ppermute | solution.py:279
  39.6 1.3 %collective-permute-start.13 = (bf16[11,2,16,128]{3,2,1,0:T(8,128)(2,1)S(1)}, bf16[11,2,16,128]{3,2,1,0:T(8,128)(2,1)S(1)}, u32[]{:S(2)}, u32[]{:S(2)}) collective-permute-start(bf16[11,2,16,128]{3,2,1,0:T(8,128)(2,1)S(1)} %collective-permute-done.9.refs_3_), channel_id=1, source_target_pairs={{0,4},{4,0},{8,12},{12,8},{16,20},{20,16},{24,28},{28,24},{1,5},{5... | collective-permute-start | bytes 270344 | tf_op jit(solution)/shard_map/ppermute | solution.py:279
  42.5 6.8 %collective-permute-start.16 = (bf16[128,256]{1,0:T(8,128)(2,1)S(1)}, bf16[128,256]{1,0:T(8,128)(2,1)S(1)}, u32[]{:S(2)}, u32[]{:S(2)}) collective-permute-start(bf16[128,256]{1,0:T(8,128)(2,1)S(1)} %panel_sums.1.refs_0_), channel_id=1, source_target_pairs={{0,3},{1,2},{2,1},{3,0},{4,7},{5,6},{6,5},{7,4},{8,11},{9,10},{10,... | collective-permute-start | bytes 196616 | tf_op jit(solution)/shard_map/ppermute | solution.py:279
  45.7 5.7 %collective-permute-start.15 = (bf16[128,256]{1,0:T(8,128)(2,1)S(1)}, bf16[128,256]{1,0:T(8,128)(2,1)S(1)}, u32[]{:S(2)}, u32[]{:S(2)}) collective-permute-start(bf16[128,256]{1,0:T(8,128)(2,1)S(1)} %panel_sums.1.refs_0_), channel_id=1, source_target_pairs={{0,2},{1,3},{2,0},{3,1},{4,6},{5,7},{6,4},{7,5},{8,10},{9,11},{10,... | collective-permute-start | bytes 196616 | tf_op jit(solution)/shard_map/ppermute | solution.py:279
  45.7 5.9 %collective-permute-start.14 = (bf16[128,256]{1,0:T(8,128)(2,1)S(1)}, bf16[128,256]{1,0:T(8,128)(2,1)S(1)}, u32[]{:S(2)}, u32[]{:S(2)}) collective-permute-start(bf16[128,256]{1,0:T(8,128)(2,1)S(1)} %panel_sums.1.refs_0_), channel_id=1, source_target_pairs={{0,1},{1,0},{2,3},{3,2},{4,5},{5,4},{6,7},{7,6},{8,9},{9,8},{10,11... | collective-permute-start | bytes 196616 | tf_op jit(solution)/shard_map/ppermute | solution.py:279
  52.9 1.3 %collective-permute-start.17 = (f32[64,128]{1,0:T(8,128)S(1)}, f32[64,128]{1,0:T(8,128)S(1)}, u32[]{:S(2)}, u32[]{:S(2)}) collective-permute-start(f32[64,128]{1,0:T(8,128)S(1)} %field_sums.1), channel_id=1, source_target_pairs={{0,4},{4,0},{8,12},{12,8},{16,20},{20,16},{24,28},{28,24},{1,5},{5... | collective-permute-start | bytes 98312 | tf_op jit(solution)/shard_map/ppermute | solution.py:279
  54.2 4.8 %collective-permute-start.20 = (f32[64,128]{1,0:T(8,128)S(1)}, f32[64,128]{1,0:T(8,128)S(1)}, u32[]{:S(2)}, u32[]{:S(2)}) collective-permute-start(f32[64,128]{1,0:T(8,128)S(1)} %add.90), channel_id=1, source_target_pairs={{0,24},{4,28},{8,16},{12,20},{16,8},{20,12},{24,0},{28,4},{1,25},{... | collective-permute-start | bytes 98312 | tf_op jit(solution)/shard_map/ppermute | solution.py:279
  55.5 3.9 %collective-permute-start.19 = (f32[64,128]{1,0:T(8,128)S(1)}, f32[64,128]{1,0:T(8,128)S(1)}, u32[]{:S(2)}, u32[]{:S(2)}) collective-permute-start(f32[64,128]{1,0:T(8,128)S(1)} %add.90), channel_id=1, source_target_pairs={{0,16},{4,20},{8,24},{12,28},{16,0},{20,4},{24,8},{28,12},{1,17},{... | collective-permute-start | bytes 98312 | tf_op jit(solution)/shard_map/ppermute | solution.py:279
  56.9 3.9 %collective-permute-start.18 = (f32[64,128]{1,0:T(8,128)S(1)}, f32[64,128]{1,0:T(8,128)S(1)}, u32[]{:S(2)}, u32[]{:S(2)}) collective-permute-start(f32[64,128]{1,0:T(8,128)S(1)} %add.90), channel_id=1, source_target_pairs={{0,8},{4,12},{8,0},{12,4},{16,24},{20,28},{24,16},{28,20},{1,9},{5... | collective-permute-start | bytes 98312 | tf_op jit(solution)/shard_map/ppermute | solution.py:279

commit v3 on v2

--- a/solution.py
+++ b/solution.py
@@ -53,7 +53,9 @@
 
     def ready():
         load.wait()
-        left_ref[...] = loads_ref[...].T
+        rows = loads_ref.shape[1]
+        for k in range(loads_ref.shape[0]):
+            left_ref[:, k * rows : (k + 1) * rows] = loads_ref[k].T
 
     forces_sums(half_ref, left_ref, modes_ref, out_ref, top_ref, held_ref, sems, ready)
 
@@ -63,7 +65,7 @@
 
 
 def forces_half(half, pressure, modes, first):
-    nodes, columns = pressure.shape if first else pressure.shape[::-1]
+    columns, nodes = (pressure.shape[2], modes.shape[0]) if first else pressure.shape
     width = modes.shape[1] // 2
     vmem, hbm = pl.BlockSpec(memory_space=pltpu.VMEM), pl.BlockSpec(memory_space=pltpu.HBM)
     outs = [
@@ -72,7 +74,7 @@
         jax.ShapeDtypeStruct((columns, nodes), BF16),
     ][: 3 if first else 2]
     scratch = [
-        pltpu.VMEM((nodes, columns), BF16),
+        pltpu.VMEM(pressure.shape, BF16),
         pltpu.VMEM((nodes, width), BF16),
         pltpu.SemaphoreType.DMA,
         pltpu.SemaphoreType.DMA((nodes // row_block(nodes),)),
@@ -91,9 +93,9 @@
     )(half, pressure, modes)
 
 
-def panel_modes_kernel(half, panel_ref, modes_ref, high_ref, low_ref, onehot_ref, held_ref, total_ref, sems):
+def panel_modes_kernel(half_ref, panel_ref, modes_ref, high_ref, low_ref, onehot_ref, held_ref, total_ref, sems):
     width = held_ref.shape[1]
-    rows, copies = start_rows(modes_ref, held_ref, sems, half * width)
+    rows, copies = start_rows(modes_ref, held_ref, sems, pl.multiple_of(half_ref[0] * width, 128))
     panels = lax.broadcasted_iota(jnp.int32, onehot_ref.shape, 0)
     onehot_ref[...] = jnp.where(panels == panel_ref[...], 1.0, 0.0).astype(BF16)
     for k, copy in enumerate(copies):
@@ -112,8 +114,12 @@
     width = count // 2
     blocks = 4 if nodes % 64 == 0 else 1
     return pl.pallas_call(
-        functools.partial(panel_modes_kernel, half),
-        in_specs=[pl.BlockSpec(memory_space=pltpu.VMEM), pl.BlockSpec(memory_space=pltpu.HBM)],
+        panel_modes_kernel,
+        in_specs=[
+            pl.BlockSpec(memory_space=pltpu.SMEM),
+            pl.BlockSpec(memory_space=pltpu.VMEM),
+            pl.BlockSpec(memory_space=pltpu.HBM),
+        ],
         out_specs=[pl.BlockSpec(memory_space=pltpu.VMEM)] * 2,
         out_shape=[jax.ShapeDtypeStruct((PANEL_DEV, width), BF16)] * 2,
         scratch_shapes=[
@@ -127,7 +133,7 @@
             flops=2 * nodes * PANEL_DEV * width, bytes_accessed=2 * nodes * width, transcendentals=0
         ),
         name="panel_modes",
-    )(panel_of.reshape(1, nodes), modes)
+    )(half, panel_of.reshape(1, nodes), modes)
 
 
 def sin_cos(angle):
@@ -189,84 +195,81 @@
     )(omega_force, bins)
 
 
-def panel_sums_kernel(place_ref, *refs):
-    *slots, high0, low0, high1, low1, out_ref, held_ref = refs
-    core, chip = place_ref[0], place_ref[1]
-    count = len(slots) // 2
+def panel_sums_kernel(count, place_ref, *refs):
+    slots, (high_ref, low_ref), before, (out_ref, held_ref) = refs[:count], refs[count : count + 2], refs[count + 2 : -2], refs[-2:]
+    chip = place_ref[1]
     tiles, _, group, lanes = slots[0].shape
-    half = held_ref.shape[1] // 2
-    for side in range(2):
-        for k in range(count):
-            slot = slots[side * count + k]
-            start = 0 if count == 1 else pl.multiple_of((chip ^ k) * group, group)
-            for part in range(2):
-                for t in range(tiles):
-                    held_ref[core ^ side, pl.ds(part * half + start, group), t * lanes : (t + 1) * lanes] = slot[t, part]
-    total = None
-    for side, pair in enumerate(((high0, low0), (high1, low1))):
-        for ref in pair:
-            term = lax.dot_general(held_ref[side], ref[...], NT, preferred_element_type=F32)
-            total = term if total is None else total + term
+    half = held_ref.shape[0] // 2
+    for k, slot in enumerate(slots):
+        start = 0 if count == 1 else pl.multiple_of((chip ^ (count - 1 - k)) * group, group)
+        for part in range(2):
+            for t in range(tiles):
+                held_ref[pl.ds(part * half + start, group), t * lanes : (t + 1) * lanes] = slot[t, part]
+    total = before[0][...] if before else None
+    for ref in (high_ref, low_ref):
+        term = lax.dot_general(held_ref[...], ref[...], NT, preferred_element_type=F32)
+        total = term if total is None else total + term
     out_ref[...] = total.astype(out_ref.dtype)
 
 
-def panel_sums(place, slots, first, second):
-    half = slots[0].shape[2] * (len(slots) // 2)
+def panel_sums(place, slots, pair, *before):
+    half = slots[0].shape[2] * len(slots)
     width = slots[0].shape[0] * slots[0].shape[3]
     vmem = pl.BlockSpec(memory_space=pltpu.VMEM)
     return pl.pallas_call(
-        panel_sums_kernel,
-        in_specs=[pl.BlockSpec(memory_space=pltpu.SMEM)] + [vmem] * (len(slots) + 4),
+        functools.partial(panel_sums_kernel, len(slots)),
+        in_specs=[pl.BlockSpec(memory_space=pltpu.SMEM)] + [vmem] * (len(slots) + 2 + len(before)),
         out_specs=vmem,
-        out_shape=jax.ShapeDtypeStruct((2 * half, PANEL_DEV), BF16),
-        scratch_shapes=[pltpu.VMEM((2, 2 * half, width), BF16)],
+        out_shape=jax.ShapeDtypeStruct((2 * half, PANEL_DEV), BF16 if before else F32),
+        scratch_shapes=[pltpu.VMEM((2 * half, width), BF16)],
         compiler_params=pltpu.CompilerParams(vmem_limit_bytes=16 * MIB),
+        cost_estimate=pl.CostEstimate(
+            flops=8 * half * width * PANEL_DEV, bytes_accessed=8 * width * PANEL_DEV, transcendentals=0
+        ),
         name="panel_sums",
-    )(place, *slots, *first, *second)
-
-
-def field_kernel(freqs, place_ref, *refs):
-    *pieces, high0, low0, high1, low1, out_ref = refs
+    )(place, *slots, *pair, *before)
+
+
+def field_kernel(freqs, order, place_ref, *refs):
+    pieces, kernels, out_ref = refs[: len(order)], refs[len(order) : -1], refs[-1]
     own = place_ref[2]
     columns = pieces[0].shape[0]
     half = columns // 2
     field = out_ref.shape[0]
     wide = 2 * field
-    parts = [None] * 4
-    for k, piece in enumerate(pieces):
+    products = [[None] * (len(kernels) // 2) for _ in range(2)]
+    for k, piece in zip(order, pieces, strict=True):
         rows = pl.ds(pl.multiple_of((own ^ k) * PANEL_DEV, PANEL_DEV), PANEL_DEV)
         for part in range(2):
-            for side, pair in enumerate(((high0, low0), (high1, low1))):
-                for ref in pair:
-                    term = jnp.dot(piece[...], ref[part, rows, :], preferred_element_type=F32)
-                    at = 2 * part + side
-                    parts[at] = term if parts[at] is None else parts[at] + term
+            for at, ref in enumerate(kernels):
+                term = jnp.dot(piece[...], ref[part, rows, :], preferred_element_type=F32)
+                before = products[part][at // 2]
+                products[part][at // 2] = term if before is None else before + term
     row = lax.broadcasted_iota(jnp.int32, (columns, wide), 0)
     freq_of = (row % half) // (half // freqs)
     sums = []
     for part in range(2):
-        picked = None
-        for pair in range(freqs // 2):
-            side, at = divmod(pair, freqs // 4)
-            block = parts[2 * part + side][:, at * wide : (at + 1) * wide]
-            picked = block if picked is None else jnp.where(freq_of // 2 == pair, block, picked)
+        blocks = [p[:, i : i + wide] for p in products[part] for i in range(0, p.shape[1], wide)]
+        picked = blocks[0]
+        for pair in range(1, freqs // 2):
+            picked = jnp.where(freq_of // 2 == pair, blocks[pair], picked)
         sums.append(jnp.where(freq_of % 2 == 1, pltpu.roll(picked, field, 1), picked))
     real = sums[0][:half] - sums[1][half:]
     imag = sums[0][half:] + sums[1][:half]
     out_ref[...] = jnp.concatenate([real, imag], axis=0).T[:field]
 
 
-def field_sums(freqs, field, place, pieces, first, second):
+def field_sums(freqs, field, place, pieces, kernels):
     columns = pieces[0].shape[0]
     vmem = pl.BlockSpec(memory_space=pltpu.VMEM)
     return pl.pallas_call(
-        functools.partial(field_kernel, freqs),
-        in_specs=[pl.BlockSpec(memory_space=pltpu.SMEM)] + [vmem] * (len(pieces) + 4),
+        functools.partial(field_kernel, freqs, tuple(pieces)),
+        in_specs=[pl.BlockSpec(memory_space=pltpu.SMEM)] + [vmem] * (len(pieces) + len(kernels)),
         out_specs=vmem,
         out_shape=jax.ShapeDtypeStruct((field, columns), F32),
         compiler_params=pltpu.CompilerParams(vmem_limit_bytes=24 * MIB),
         name="field_sums",
-    )(place, *pieces, *first, *second)
+    )(place, *pieces.values(), *kernels)
 
 
 def tree(terms):
@@ -279,15 +282,19 @@
     return lax.ppermute(x, axis, [(i, i ^ k) for i in range(size)])
 
 
+def far_first(size):
+    return range(size - 1, 0, -1)
+
+
 def pack(x, shift):
-    scaled = (x * jnp.exp2(shift)).astype(F16)
-    note = jnp.broadcast_to(shift, (1, *x.shape[1:])).astype(F16)
+    scaled = (x * jnp.exp2(shift)).astype(F16).reshape(-1, x.shape[-1])
+    note = jnp.broadcast_to(shift.reshape(1, -1), (8, x.shape[-1])).astype(F16)
     return jnp.concatenate([scaled, note], axis=0)
 
 
-def unpack(y):
-    shift = y[-1:].astype(F32)
-    return y[:-1].astype(F32) * jnp.exp2(-shift), shift
+def unpack(y, shape):
+    shift = y[-8:-7].astype(F32).reshape(1, 1, 1, -1)
+    return y[:-8].reshape(shape).astype(F32) * jnp.exp2(-shift), shift
 
 
 def beside(x, work):
@@ -308,41 +315,41 @@
         core, chip, fld = node % 2, node // 2, lax.axis_index("fld")
         place = jnp.stack([core, chip, fld]).astype(jnp.int32)
 
-        away, away_top, left = forces_half((1 - core).reshape(1), pressure, modes, True)
+        away, away_top, left = forces_half(
+            (1 - core).reshape(1), pressure.reshape(-1, row_block(pressure.shape[0]), columns), modes, True
+        )
         came, came_top = (swap(x, "node", nodes_axis, 1) for x in (away, away_top))
         home, home_top = forces_half(core.reshape(1), left, modes, False)
         total = (home + came).reshape(tiles, 2, half, 128)
         bound = jnp.maximum(home_top[:1] + came_top[:1], 1e-30)
-        shift = jnp.broadcast_to(14.0 - jnp.ceil(jnp.log2(bound)), (1, 2, group, 128))
-
-        packed, panel_known = beside(pack(total, shift[:, :, :1]), panel_of)
-        came = [
-            swap(lax.dynamic_slice_in_dim(packed, (chip ^ k) * group, group, 2), "node", nodes_axis, 2 * k)
-            for k in range(1, chips)
+        shift = (14.0 - jnp.ceil(jnp.log2(bound))).reshape(1, 1, 1, 128)
+
+        share = (tiles, 2, group, 128)
+        sent = [
+            pack(lax.dynamic_slice_in_dim(total, (chip ^ k) * group, group, 2), shift) for k in far_first(chips)
         ]
-        came, first = beside(came, panel_modes(0, panel_known, modes))
-        terms, shifts = [lax.dynamic_slice_in_dim(total, chip * group, group, 2)], [shift]
+        sent, panel_known = beside(sent, panel_of)
+        came = [swap(piece, "node", nodes_axis, 2 * k) for k, piece in zip(far_first(chips), sent, strict=True)]
+        came, first = beside(came, panel_modes(core.reshape(1), panel_known, modes))
+        terms, shifts = [], [shift]
         for piece in came:
-            value, other = unpack(piece)
+            value, other = unpack(piece, share)
             terms.append(value)
             shifts.append(other)
-        forces = tree(terms)
+        forces = tree(terms + [lax.dynamic_slice_in_dim(total, chip * group, group, 2)])
         shift = functools.reduce(jnp.minimum, shifts) - chip_bits
 
         freqs = omega_force.shape[0]
         bins, kernels = dist_bin.T, []
-        steps = field_axis.bit_length() - 1
-        for bit in range(steps):
+        for bit in range(field_axis.bit_length() - 1):
             packed, bins = beside(pack(forces, shift), bins)
             came = swap(packed, "fld", field_axis, 1 << bit)
             if bit < 2:
-                came, kernel = beside(came, radiation(bit * freqs // 2, freqs // 2, omega_force, bins))
-                kernels.append(kernel)
-            value, other = unpack(came)
+                came, kernel = beside(came, radiation(2 * bit, 2, omega_force, bins))
+                kernels.extend(kernel)
+            value, other = unpack(came, share)
             forces = forces + value
             shift = jnp.minimum(shift, other) - 1.0
-        for rest in range(len(kernels), 2):
-            kernels.append(radiation(rest * freqs // 2, freqs // 2, omega_force, bins))
 
         wmod = lax.dynamic_slice_in_dim(omega_mode, core * width, width).reshape(tiles, 1, 128)
         damp = lax.dynamic_slice_in_dim(damping, core * width, width).reshape(tiles, 1, 128)
@@ -358,22 +365,24 @@
         response = jnp.stack([a_real, a_imag], axis=1).astype(BF16)
 
         response, panel_known = beside(response, panel_known)
-        came = [swap(response, "node", nodes_axis, 2 * k) for k in range(1, chips)]
-        came, second = beside(came, panel_modes(1, panel_known, modes))
-        slots = [response, *came]
-        slots += [swap(slot, "node", nodes_axis, 1) for slot in slots]
+        came = [swap(response, "node", nodes_axis, 2 * k) for k in far_first(chips)]
+        came, second = beside(came, panel_modes((1 - core).reshape(1), panel_known, modes))
+        sides = [[*came, response]]
+        sides.append([swap(slot, "node", nodes_axis, 1) for slot in sides[0]])
         if group % 16:
-            order = chip ^ jnp.arange(chips)
-            slots = [
-                jnp.moveaxis(jnp.stack(side)[order], 0, 2).reshape(tiles, 2, half, 128)
-                for side in (slots[:chips], slots[chips:])
+            order = chips - 1 - (chip ^ jnp.arange(chips))
+            sides = [
+                [jnp.moveaxis(jnp.stack(side)[order], 0, 2).reshape(tiles, 2, half, 128)] for side in sides
             ]
-
-        sums = panel_sums(place, slots, first, second)
-        pieces = [sums] + [swap(sums, "fld", field_axis, k) for k in range(1, field_axis)]
-        field = field_sums(freqs, dist_bin.shape[1], place, pieces, *kernels)
+        sums = panel_sums(place, sides[0], first)
+        sums = panel_sums(place, sides[1], second, sums)
+        sums, bins = beside(sums, bins)
+        pieces = {k: swap(sums, "fld", field_axis, k) for k in (2, 3, 1)} | {0: sums}
+        done = sum(x.shape[2] // dist_bin.shape[1] for x in kernels[::2])
+        kernels.extend(radiation(done, freqs - done, omega_force, bins))
+        field = field_sums(freqs, dist_bin.shape[1], place, pieces, kernels)
         field = field + swap(field, "node", nodes_axis, 1)
-        return tree([field] + [swap(field, "node", nodes_axis, 2 * k) for k in range(1, chips)])
+        return tree([swap(field, "node", nodes_axis, 2 * k) for k in far_first(chips)] + [field])
 
     return body
 

time: 61.6 us -> 59.9 us (0.972)
  waiting for transfers between devices: 13.7 us -> 9.9 us
  starting transfers between devices: 21.6 us -> 22.8 us
  Pallas kernels: 22.9 us -> 23.8 us
    ppermute x21, waiting for transfers between devices: 13.7 us -> 9.9 us  [swap(): return lax.ppermute(x, axis, [(i, i ^ k) for i in range(size)])]
    ppermute x21, starting transfers between devices: 21.6 us -> 22.8 us  [swap(): return lax.ppermute(x, axis, [(i, i ^ k) for i in range(size)])]
    pallas_call x4 -> x5, Pallas kernels: 10 us -> 11 us  [the longest x2 7.01 us: panel_modes(): pl.pallas_call(panel_modes_kernel, in_specs=[pl.BlockSpec(memory_space=pl...]
    pallas_call x2 -> x3, Pallas kernels: 6.24 us -> 6.06 us  [radiation(): pl.pallas_call(functools.partial(radiation_kernel, first), grid=(count //...]
  transfers between devices with their start and end apart: 21 -> 21, of which waited for: 15 -> 10; matrix products, arithmetic and copies ran while one was open for 1% -> 1% of each run, Pallas kernels for 27% -> 29%
where the time goes in v3:
time: 59.9 us; the launch traced here: 59.7 us
  Pallas kernels  23.8 us (40%)
  starting transfers between devices  22.8 us (38%)
  waiting for transfers between devices  9.9 us (17%)
  other arithmetic  1.54 us (3%)
  local copies, waits for them, and re-layouts  1.34 us (2%)
    ppermute x21, starting transfers between devices, swap(): return lax.ppermute(x, axis, [(i, i ^ k) for i in range(size)])  22.8 us
    ppermute x21, waiting for transfers between devices, swap(): return lax.ppermute(x, axis, [(i, i ^ k) for i in range(size)])  9.9 us
    pallas_call x2, Pallas kernels, panel_modes(): pl.pallas_call(panel_modes_kernel, in_specs=[pl.BlockSpec(memory_space=pl...  7.01 us
    pallas_call x2, Pallas kernels, forces_half(): pl.pallas_call(first_kernel if first else second_kernel, in_specs=[pl.Blo...  6.66 us
    pallas_call x3, Pallas kernels, radiation(): pl.pallas_call(functools.partial(radiation_kernel, first), grid=(count //...  6.06 us
    pallas_call x2, Pallas kernels, panel_sums(): pl.pallas_call(functools.partial(panel_sums_kernel, len(slots)), in_specs...  2.33 us
    pallas_call x1, Pallas kernels, field_sums(): pl.pallas_call(functools.partial(field_kernel, freqs, tuple(pieces)), in_...  1.7 us
  transfers between devices with their start and end apart: 21, of which 10 were waited for; matrix products, arithmetic and copies ran while one was open for 1% of the time, Pallas kernels for 29%

profile of v3, /device:TPU:0, one launch (start us, length us, event | category | flops | bytes accessed | tf_op | source)
XLA Modules:
  0.0 59.7 jit_solution(18210862933991940830)
XLA Ops:
  0.0 1.0 %copy-done.1 = bf16[1792,128]{1,0:T(8,128)(2,1)S(1)} copy-done((bf16[1792,128]{1,0:T(8,128)(2,1)S(1)}, bf16[1792,128]{1,0:T(8,128)(2,1)}, u32[]{:S(2)}) %copy-start.1) | copy-done | bytes 458776
  1.0 3.5 %forces_half.2 = (f32[11,128,128]{2,1,0:T(8,128)S(1)}, f32[8,128]{1,0:T(8,128)S(1)}, bf16[128,1792]{1,0:T(8,128)(2,1)S(1)}) custom-call(s32[1]{0:T(128)} %bitcast.5.half_ref, bf16[7,256,128]{2,1,0:T(8,128)(2,1)S(1)} %bitcast.51, bf16[1792,2816]{1,0:T(8,128)(2,1)} %modes_ref.7), custom_call_target="tpu_custom_call" | custom-call | flops 645922816 | bytes 5046272 | tf_op jit(solution)/shard_map/forces_half/pallas_call | solution.py:82
  4.5 0.5 collective-permute-start
  5.0 0.1 collective-permute-start.1
  5.1 3.2 %forces_half.3 = (f32[11,128,128]{2,1,0:T(8,128)S(1)}, f32[8,128]{1,0:T(8,128)S(1)}) custom-call(s32[1]{0:T(128)} %bitcast.half_ref, bf16[128,1792]{1,0:T(8,128)(2,1)S(1)} %get-tuple-element.48.left_ref, bf16[1792,2816]{1,0:T(8,128)(2,1)} %modes_ref.7), custom_call_target="tpu_custom_call" | custom-call | flops 645922816 | bytes 5046272 | tf_op jit(solution)/shard_map/forces_half/pallas_call | solution.py:82
  8.5 0.1 reshape.271
  8.6 0.1 add.99
  8.7 0.1 multiply_convert_fusion.2
  8.8 0.1 pad_maximum_fusion
  8.9 3.9 %collective-permute-start.2 = (f16[360,128]{1,0:T(8,128)(2,1)S(1)}, f16[360,128]{1,0:T(8,128)(2,1)S(1)}, u32[]{:S(2)}, u32[]{:S(2)}) collective-permute-start(f16[360,128]{1,0:T(8,128)(2,1)S(1)} %get-tuple-element.53), channel_id=1, source_target_pairs={{0,24},{4,28},{8,16},{12,20},{16,8},{20,12},{24,0},{28,4},{1,25},{... | collective-permute-start | bytes 276488 | tf_op jit(solution)/shard_map/ppermute | solution.py:282
  12.8 0.5 collective-permute-start.3
  13.3 0.1 collective-permute-start.4
  13.5 3.5 %panel_modes.2 = (bf16[256,1408]{1,0:T(8,128)(2,1)S(1)}, bf16[256,1408]{1,0:T(8,128)(2,1)S(1)}) custom-call(s32[1]{0:T(128)} %bitcast.half_ref, s32[1,1792]{1,0:T(1,128)S(1)} %reshape.278.panel_ref, bf16[1792,2816]{1,0:T(8,128)(2,1)} %modes_ref.7), custom_call_target="tpu_custom_call" | custom-call | flops 1291845632 | bytes 5046272 | tf_op jit(solution)/shard_map/panel_modes/pallas_call | solution.py:116
  17.0 0.7 %collective-permute-done.3 = f16[360,128]{1,0:T(8,128)(2,1)S(1)} collective-permute-done((f16[360,128]{1,0:T(8,128)(2,1)S(1)}, f16[360,128]{1,0:T(8,128)(2,1)S(1)}, u32[]{:S(2)}, u32[]{:S(2)}) %collective-permute-start.3) | collective-permute-done | bytes 92192 | tf_op jit(solution)/shard_map/ppermute | solution.py:282
  17.7 0.3 collective-permute-done.4
  18.1 0.1 multiply_convert_fusion.1
  18.2 1.6 %collective-permute-start.5 = (f16[360,128]{1,0:T(8,128)(2,1)S(1)}, f16[360,128]{1,0:T(8,128)(2,1)S(1)}, u32[]{:S(2)}, u32[]{:S(2)}) collective-permute-start(f16[360,128]{1,0:T(8,128)(2,1)S(1)} %pad_maximum_fusion.3), channel_id=1, source_target_pairs={{0,1},{1,0},{2,3},{3,2},{4,5},{5,4},{6,7},{7,6},{8,9},{9,8},{10,11... | collective-permute-start | bytes 276488 | tf_op jit(solution)/shard_map/ppermute | solution.py:282
  19.9 0.1 multiply_bitcast_fusion.1
  19.9 1.5 %radiation.3 = (bf16[2,1024,128]{2,1,0:T(8,128)(2,1)S(1)}, bf16[2,1024,128]{2,1,0:T(8,128)(2,1)S(1)}) custom-call(f32[8]{0:T(128)S(1)} %copy-done.2, s32[64,1024]{1,0:T(8,128)S(1)} %bitcast.48), custom_call_target="tpu_custom_call" | custom-call | flops 5242880 | bytes 524288 | tf_op jit(solution)/shard_map/radiation/pallas_call | solution.py:180
  21.5 1.4 %collective-permute-done.5 = f16[360,128]{1,0:T(8,128)(2,1)S(1)} collective-permute-done((f16[360,128]{1,0:T(8,128)(2,1)S(1)}, f16[360,128]{1,0:T(8,128)(2,1)S(1)}, u32[]{:S(2)}, u32[]{:S(2)}) %collective-permute-start.5) | collective-permute-done | bytes 92192 | tf_op jit(solution)/shard_map/ppermute | solution.py:282
  23.0 2.7 %collective-permute-start.6 = (f16[360,128]{1,0:T(8,128)(2,1)S(1)}, f16[360,128]{1,0:T(8,128)(2,1)S(1)}, u32[]{:S(2)}, u32[]{:S(2)}) collective-permute-start(f16[360,128]{1,0:T(8,128)(2,1)S(1)} %pad_maximum_fusion.4), channel_id=1, source_target_pairs={{0,2},{1,3},{2,0},{3,1},{4,6},{5,7},{6,4},{7,5},{8,10},{9,11},{10,... | collective-permute-start | bytes 276488 | tf_op jit(solution)/shard_map/ppermute | solution.py:282
  25.7 1.5 %radiation.4 = (bf16[2,1024,128]{2,1,0:T(8,128)(2,1)S(1)}, bf16[2,1024,128]{2,1,0:T(8,128)(2,1)S(1)}) custom-call(f32[8]{0:T(128)S(1)} %copy-done.2, s32[64,1024]{1,0:T(8,128)S(1)} %bitcast.49), custom_call_target="tpu_custom_call" | custom-call | flops 5242880 | bytes 524288 | tf_op jit(solution)/shard_map/radiation/pallas_call | solution.py:180
  27.2 1.3 %collective-permute-done.6 = f16[360,128]{1,0:T(8,128)(2,1)S(1)} collective-permute-done((f16[360,128]{1,0:T(8,128)(2,1)S(1)}, f16[360,128]{1,0:T(8,128)(2,1)S(1)}, u32[]{:S(2)}, u32[]{:S(2)}) %collective-permute-start.6) | collective-permute-done | bytes 92192 | tf_op jit(solution)/shard_map/ppermute | solution.py:282
  28.6 0.1 subtract_convert_fusion
  28.7 2.0 %collective-permute-start.7 = (bf16[11,2,16,128]{3,2,1,0:T(8,128)(2,1)S(1)}, bf16[11,2,16,128]{3,2,1,0:T(8,128)(2,1)S(1)}, u32[]{:S(2)}, u32[]{:S(2)}) collective-permute-start(bf16[11,2,16,128]{3,2,1,0:T(8,128)(2,1)S(1)} %pad_maximum_fusion.5.refs_3_), channel_id=1, source_target_pairs={{0,24},{4,28},{8,16},{12,20},{16,8},{20,12},{24,0},{28,4},{1,25},{... | collective-permute-start | bytes 270344 | tf_op jit(solution)/shard_map/ppermute | solution.py:282
  30.7 1.1 %collective-permute-start.8 = (bf16[11,2,16,128]{3,2,1,0:T(8,128)(2,1)S(1)}, bf16[11,2,16,128]{3,2,1,0:T(8,128)(2,1)S(1)}, u32[]{:S(2)}, u32[]{:S(2)}) collective-permute-start(bf16[11,2,16,128]{3,2,1,0:T(8,128)(2,1)S(1)} %pad_maximum_fusion.5.refs_3_), channel_id=1, source_target_pairs={{0,16},{4,20},{8,24},{12,28},{16,0},{20,4},{24,8},{28,12},{1,17},{... | collective-permute-start | bytes 270344 | tf_op jit(solution)/shard_map/ppermute | solution.py:282
  31.8 1.2 %collective-permute-start.9 = (bf16[11,2,16,128]{3,2,1,0:T(8,128)(2,1)S(1)}, bf16[11,2,16,128]{3,2,1,0:T(8,128)(2,1)S(1)}, u32[]{:S(2)}, u32[]{:S(2)}) collective-permute-start(bf16[11,2,16,128]{3,2,1,0:T(8,128)(2,1)S(1)} %pad_maximum_fusion.5.refs_3_), channel_id=1, source_target_pairs={{0,8},{4,12},{8,0},{12,4},{16,24},{20,28},{24,16},{28,20},{1,9},{5... | collective-permute-start | bytes 270344 | tf_op jit(solution)/shard_map/ppermute | solution.py:282
  33.0 3.5 %panel_modes.3 = (bf16[256,1408]{1,0:T(8,128)(2,1)S(1)}, bf16[256,1408]{1,0:T(8,128)(2,1)S(1)}) custom-call(s32[1]{0:T(128)} %bitcast.5.half_ref, s32[1,1792]{1,0:T(1,128)S(1)} %reshape.282.panel_ref, bf16[1792,2816]{1,0:T(8,128)(2,1)} %modes_ref.7), custom_call_target="tpu_custom_call" | custom-call | flops 1291845632 | bytes 5046272 | tf_op jit(solution)/shard_map/panel_modes/pallas_call | solution.py:116
  36.5 0.6 collective-permute-start.10
  37.1 0.1 collective-permute-start.11
  37.1 0.4 collective-permute-start.12
  37.7 1.2 %panel_sums.2.refs_6_ = f32[128,256]{1,0:T(8,128)S(1)} custom-call(s32[3]{0:T(128)S(1)} %pad_add_fusion.place_ref, bf16[11,2,16,128]{3,2,1,0:T(8,128)(2,1)S(1)} %collective-permute-done.7.refs_0_, bf16[11,2,16,128]{3,2,1,0:T(8,128)(2,1)S(1)} %collective-permute-done.8.refs_1_, bf16[11,2,16,128]{3,2,1,0:T(8,128)(2,1)S(1)} %collective-permute-done.9.refs_2_, ...), custom_call_target="tpu_custom_call" | custom-call | flops 184549376 | bytes 2883584 | tf_op jit(solution)/shard_map/panel_sums/pallas_call | solution.py:219
  38.9 1.2 %panel_sums.3.refs_3_ = bf16[128,256]{1,0:T(8,128)(2,1)S(1)} custom-call(s32[3]{0:T(128)S(1)} %pad_add_fusion.place_ref, bf16[11,2,16,128]{3,2,1,0:T(8,128)(2,1)S(1)} %collective-permute-done.10.refs_0_, bf16[11,2,16,128]{3,2,1,0:T(8,128)(2,1)S(1)} %collective-permute-done.11.refs_1_, bf16[11,2,16,128]{3,2,1,0:T(8,128)(2,1)S(1)} %collective-permute-done.12.refs_2_, ...), custom_call_target="tpu_custom_call" | custom-call | flops 184549376 | bytes 2883584 | tf_op jit(solution)/shard_map/panel_sums/pallas_call | solution.py:219
  40.0 2.1 %collective-permute-start.14 = (bf16[128,256]{1,0:T(8,128)(2,1)S(1)}, bf16[128,256]{1,0:T(8,128)(2,1)S(1)}, u32[]{:S(2)}, u32[]{:S(2)}) collective-permute-start(bf16[128,256]{1,0:T(8,128)(2,1)S(1)} %panel_sums.3.refs_3_), channel_id=1, source_target_pairs={{0,2},{1,3},{2,0},{3,1},{4,6},{5,7},{6,4},{7,5},{8,10},{9,11},{10,... | collective-permute-start | bytes 196616 | tf_op jit(solution)/shard_map/ppermute | solution.py:282
  42.1 1.9 %collective-permute-start.15 = (bf16[128,256]{1,0:T(8,128)(2,1)S(1)}, bf16[128,256]{1,0:T(8,128)(2,1)S(1)}, u32[]{:S(2)}, u32[]{:S(2)}) collective-permute-start(bf16[128,256]{1,0:T(8,128)(2,1)S(1)} %panel_sums.3.refs_3_), channel_id=1, source_target_pairs={{0,3},{1,2},{2,1},{3,0},{4,7},{5,6},{6,5},{7,4},{8,11},{9,10},{10,... | collective-permute-start | bytes 196616 | tf_op jit(solution)/shard_map/ppermute | solution.py:282
  44.0 0.5 collective-permute-start.16
  44.5 3.0 %radiation.5 = (bf16[2,1024,256]{2,1,0:T(8,128)(2,1)S(1)}, bf16[2,1024,256]{2,1,0:T(8,128)(2,1)S(1)}) custom-call(f32[8]{0:T(128)S(1)} %copy-done.2, s32[64,1024]{1,0:T(8,128)S(1)} %bitcast.50), custom_call_target="tpu_custom_call" | custom-call | flops 10485760 | bytes 1048576 | tf_op jit(solution)/shard_map/radiation/pallas_call | solution.py:180
  47.5 1.1 %collective-permute-done.15.refs_1_ = bf16[128,256]{1,0:T(8,128)(2,1)S(1)} collective-permute-done((bf16[128,256]{1,0:T(8,128)(2,1)S(1)}, bf16[128,256]{1,0:T(8,128)(2,1)S(1)}, u32[]{:S(2)}, u32[]{:S(2)}) %collective-permute-start.15) | collective-permute-done | bytes 65568 | tf_op jit(solution)/shard_map/ppermute | solution.py:282
  48.6 0.9 %collective-permute-done.16.refs_2_ = bf16[128,256]{1,0:T(8,128)(2,1)S(1)} collective-permute-done((bf16[128,256]{1,0:T(8,128)(2,1)S(1)}, bf16[128,256]{1,0:T(8,128)(2,1)S(1)}, u32[]{:S(2)}, u32[]{:S(2)}) %collective-permute-start.16) | collective-permute-done | bytes 65568 | tf_op jit(solution)/shard_map/ppermute | solution.py:282
  49.5 1.7 %field_sums.1 = f32[64,128]{1,0:T(8,128)S(1)} custom-call(s32[3]{0:T(128)S(1)} %pad_add_fusion.place_ref, bf16[128,256]{1,0:T(8,128)(2,1)S(1)} %collective-permute-done.14.refs_0_, bf16[128,256]{1,0:T(8,128)(2,1)S(1)} %collective-permute-done.15.refs_1_, bf16[128,256]{1,0:T(8,128)(2,1)S(1)} %collective-permute-done.16.refs_2_, ...), custom_call_target="tpu_custom_call" | custom-call | tf_op jit(solution)/shard_map/field_sums/pallas_call | solution.py:265
  51.3 1.2 %collective-permute-done.17 = f32[64,128]{1,0:T(8,128)S(1)} collective-permute-done((f32[64,128]{1,0:T(8,128)S(1)}, f32[64,128]{1,0:T(8,128)S(1)}, u32[]{:S(2)}, u32[]{:S(2)}) %collective-permute-start.17) | collective-permute-done | bytes 32800 | tf_op jit(solution)/shard_map/ppermute | solution.py:282
  52.5 2.1 %collective-permute-start.18 = (f32[64,128]{1,0:T(8,128)S(1)}, f32[64,128]{1,0:T(8,128)S(1)}, u32[]{:S(2)}, u32[]{:S(2)}) collective-permute-start(f32[64,128]{1,0:T(8,128)S(1)} %add.110), channel_id=1, source_target_pairs={{0,24},{4,28},{8,16},{12,20},{16,8},{20,12},{24,0},{28,4},{1,25},{... | collective-permute-start | bytes 98312 | tf_op jit(solution)/shard_map/ppermute | solution.py:282
  54.5 0.6 %collective-permute-start.19 = (f32[64,128]{1,0:T(8,128)S(1)}, f32[64,128]{1,0:T(8,128)S(1)}, u32[]{:S(2)}, u32[]{:S(2)}) collective-permute-start(f32[64,128]{1,0:T(8,128)S(1)} %add.110), channel_id=1, source_target_pairs={{0,16},{4,20},{8,24},{12,28},{16,0},{20,4},{24,8},{28,12},{1,17},{... | collective-permute-start | bytes 98312 | tf_op jit(solution)/shard_map/ppermute | solution.py:282
  55.2 0.8 %collective-permute-start.20 = (f32[64,128]{1,0:T(8,128)S(1)}, f32[64,128]{1,0:T(8,128)S(1)}, u32[]{:S(2)}, u32[]{:S(2)}) collective-permute-start(f32[64,128]{1,0:T(8,128)S(1)} %add.110), channel_id=1, source_target_pairs={{0,8},{4,12},{8,0},{12,4},{16,24},{20,28},{24,16},{28,20},{1,9},{5... | collective-permute-start | bytes 98312 | tf_op jit(solution)/shard_map/ppermute | solution.py:282
  56.0 1.4 %collective-permute-done.18 = f32[64,128]{1,0:T(8,128)S(1)} collective-permute-done((f32[64,128]{1,0:T(8,128)S(1)}, f32[64,128]{1,0:T(8,128)S(1)}, u32[]{:S(2)}, u32[]{:S(2)}) %collective-permute-start.18) | collective-permute-done | bytes 32800 | tf_op jit(solution)/shard_map/ppermute | solution.py:282
  57.3 1.2 %collective-permute-done.19 = f32[64,128]{1,0:T(8,128)S(1)} collective-permute-done((f32[64,128]{1,0:T(8,128)S(1)}, f32[64,128]{1,0:T(8,128)S(1)}, u32[]{:S(2)}, u32[]{:S(2)}) %collective-permute-start.19) | collective-permute-done | bytes 32800 | tf_op jit(solution)/shard_map/ppermute | solution.py:282
  58.5 0.6 %collective-permute-done.20 = f32[64,128]{1,0:T(8,128)S(1)} collective-permute-done((f32[64,128]{1,0:T(8,128)S(1)}, f32[64,128]{1,0:T(8,128)S(1)}, u32[]{:S(2)}, u32[]{:S(2)}) %collective-permute-start.20) | collective-permute-done | bytes 32800 | tf_op jit(solution)/shard_map/ppermute | solution.py:282
  59.1 0.6 %add_add_fusion = f32[64,128]{1,0:T(8,128)} fusion(f32[64,128]{1,0:T(8,128)S(1)} %collective-permute-done.20, f32[64,128]{1,0:T(8,128)S(1)} %add.110, f32[64,128]{1,0:T(8,128)S(1)} %collective-permute-done.18, f32[64,128]{1,0:T(8,128)S(1)} %collective-permute-done.19), kind=kLoop, calls=%fused_computation.29 | loop fusion | flops 24576 | bytes 163840 | tf_op jit(solution)/shard_map/add | solution.py:277
  (49 shorter events, 0.7 us)
Async XLA Ops:
  0.0 1.0 %copy-start.1 = (bf16[1792,128]{1,0:T(8,128)(2,1)S(1)}, bf16[1792,128]{1,0:T(8,128)(2,1)}, u32[]{:S(2)}) copy-start(bf16[1792,128]{1,0:T(8,128)(2,1)} %param.7) | copy-start | bytes 1376260
  1.0 7.4 %copy-start.2 = (f32[8]{0:T(128)S(1)}, f32[8]{0:T(128)}, u32[]{:S(2)}) copy-start(f32[8]{0:T(128)} %omega_ref.5) | copy-start | bytes 100
  1.0 7.8 %copy-start.3 = (s32[1792]{0:T(1024)S(1)}, s32[1792]{0:T(1024)}, u32[]{:S(2)}) copy-start(s32[1792]{0:T(1024)} %param.12) | copy-start | bytes 21508
  4.5 4.1 %collective-permute-start = (f32[11,128,128]{2,1,0:T(8,128)S(1)}, f32[11,128,128]{2,1,0:T(8,128)S(1)}, u32[]{:S(2)}, u32[]{:S(2)}) collective-permute-start(f32[11,128,128]{2,1,0:T(8,128)S(1)} %get-tuple-element.50), channel_id=1, source_target_pairs={{0,4},{4,0},{8,12},{12,8},{16,20},{20,16},{24,28},{28,24},{1,5},{5... | collective-permute-start | bytes 2162696 | tf_op jit(solution)/shard_map/ppermute | solution.py:282
  5.0 3.5 %collective-permute-start.1 = (f32[8,128]{1,0:T(8,128)S(1)}, f32[8,128]{1,0:T(8,128)S(1)}, u32[]{:S(2)}, u32[]{:S(2)}) collective-permute-start(f32[8,128]{1,0:T(8,128)S(1)} %get-tuple-element.52), channel_id=1, source_target_pairs={{0,4},{4,0},{8,12},{12,8},{16,20},{20,16},{24,28},{28,24},{1,5},{5... | collective-permute-start | bytes 12296 | tf_op jit(solution)/shard_map/ppermute | solution.py:282
  8.3 11.6 %copy-start.4 = (f32[2816]{0:T(1024)S(1)}, f32[2816]{0:T(1024)}, u32[]{:S(2)}) copy-start(f32[2816]{0:T(1024)} %param.9) | copy-start | bytes 33796
  8.3 11.6 %copy-start.5 = (f32[2816]{0:T(1024)S(1)}, f32[2816]{0:T(1024)}, u32[]{:S(2)}) copy-start(f32[2816]{0:T(1024)} %param.10) | copy-start | bytes 33796
  8.3 11.6 %copy-start = (s32[1024,64]{0,1:T(8,128)S(1)}, s32[1024,64]{0,1:T(8,128)}, u32[]{:S(2)}) copy-start(s32[1024,64]{0,1:T(8,128)} %param.13) | copy-start | bytes 786436
  8.9 8.1 %collective-permute-start.2 = (f16[360,128]{1,0:T(8,128)(2,1)S(1)}, f16[360,128]{1,0:T(8,128)(2,1)S(1)}, u32[]{:S(2)}, u32[]{:S(2)}) collective-permute-start(f16[360,128]{1,0:T(8,128)(2,1)S(1)} %get-tuple-element.53), channel_id=1, source_target_pairs={{0,24},{4,28},{8,16},{12,20},{16,8},{20,12},{24,0},{28,4},{1,25},{... | collective-permute-start | bytes 276488 | tf_op jit(solution)/shard_map/ppermute | solution.py:282
  12.8 4.9 %collective-permute-start.3 = (f16[360,128]{1,0:T(8,128)(2,1)S(1)}, f16[360,128]{1,0:T(8,128)(2,1)S(1)}, u32[]{:S(2)}, u32[]{:S(2)}) collective-permute-start(f16[360,128]{1,0:T(8,128)(2,1)S(1)} %get-tuple-element.54), channel_id=1, source_target_pairs={{0,16},{4,20},{8,24},{12,28},{16,0},{20,4},{24,8},{28,12},{1,17},{... | collective-permute-start | bytes 276488 | tf_op jit(solution)/shard_map/ppermute | solution.py:282
  13.3 4.6 %collective-permute-start.4 = (f16[360,128]{1,0:T(8,128)(2,1)S(1)}, f16[360,128]{1,0:T(8,128)(2,1)S(1)}, u32[]{:S(2)}, u32[]{:S(2)}) collective-permute-start(f16[360,128]{1,0:T(8,128)(2,1)S(1)} %get-tuple-element.55), channel_id=1, source_target_pairs={{0,8},{4,12},{8,0},{12,4},{16,24},{20,28},{24,16},{28,20},{1,9},{5... | collective-permute-start | bytes 276488 | tf_op jit(solution)/shard_map/ppermute | solution.py:282
  18.2 4.6 %collective-permute-start.5 = (f16[360,128]{1,0:T(8,128)(2,1)S(1)}, f16[360,128]{1,0:T(8,128)(2,1)S(1)}, u32[]{:S(2)}, u32[]{:S(2)}) collective-permute-start(f16[360,128]{1,0:T(8,128)(2,1)S(1)} %pad_maximum_fusion.3), channel_id=1, source_target_pairs={{0,1},{1,0},{2,3},{3,2},{4,5},{5,4},{6,7},{7,6},{8,9},{9,8},{10,11... | collective-permute-start | bytes 276488 | tf_op jit(solution)/shard_map/ppermute | solution.py:282
  23.0 5.5 %collective-permute-start.6 = (f16[360,128]{1,0:T(8,128)(2,1)S(1)}, f16[360,128]{1,0:T(8,128)(2,1)S(1)}, u32[]{:S(2)}, u32[]{:S(2)}) collective-permute-start(f16[360,128]{1,0:T(8,128)(2,1)S(1)} %pad_maximum_fusion.4), channel_id=1, source_target_pairs={{0,2},{1,3},{2,0},{3,1},{4,6},{5,7},{6,4},{7,5},{8,10},{9,11},{10,... | collective-permute-start | bytes 276488 | tf_op jit(solution)/shard_map/ppermute | solution.py:282
  28.7 7.8 %collective-permute-start.7 = (bf16[11,2,16,128]{3,2,1,0:T(8,128)(2,1)S(1)}, bf16[11,2,16,128]{3,2,1,0:T(8,128)(2,1)S(1)}, u32[]{:S(2)}, u32[]{:S(2)}) collective-permute-start(bf16[11,2,16,128]{3,2,1,0:T(8,128)(2,1)S(1)} %pad_maximum_fusion.5.refs_3_), channel_id=1, source_target_pairs={{0,24},{4,28},{8,16},{12,20},{16,8},{20,12},{24,0},{28,4},{1,25},{... | collective-permute-start | bytes 270344 | tf_op jit(solution)/shard_map/ppermute | solution.py:282
  30.7 5.8 %collective-permute-start.8 = (bf16[11,2,16,128]{3,2,1,0:T(8,128)(2,1)S(1)}, bf16[11,2,16,128]{3,2,1,0:T(8,128)(2,1)S(1)}, u32[]{:S(2)}, u32[]{:S(2)}) collective-permute-start(bf16[11,2,16,128]{3,2,1,0:T(8,128)(2,1)S(1)} %pad_maximum_fusion.5.refs_3_), channel_id=1, source_target_pairs={{0,16},{4,20},{8,24},{12,28},{16,0},{20,4},{24,8},{28,12},{1,17},{... | collective-permute-start | bytes 270344 | tf_op jit(solution)/shard_map/ppermute | solution.py:282
  31.8 4.7 %collective-permute-start.9 = (bf16[11,2,16,128]{3,2,1,0:T(8,128)(2,1)S(1)}, bf16[11,2,16,128]{3,2,1,0:T(8,128)(2,1)S(1)}, u32[]{:S(2)}, u32[]{:S(2)}) collective-permute-start(bf16[11,2,16,128]{3,2,1,0:T(8,128)(2,1)S(1)} %pad_maximum_fusion.5.refs_3_), channel_id=1, source_target_pairs={{0,8},{4,12},{8,0},{12,4},{16,24},{20,28},{24,16},{28,20},{1,9},{5... | collective-permute-start | bytes 270344 | tf_op jit(solution)/shard_map/ppermute | solution.py:282
  32.9 5.9 %collective-permute-start.13 = (bf16[11,2,16,128]{3,2,1,0:T(8,128)(2,1)S(1)}, bf16[11,2,16,128]{3,2,1,0:T(8,128)(2,1)S(1)}, u32[]{:S(2)}, u32[]{:S(2)}) collective-permute-start(bf16[11,2,16,128]{3,2,1,0:T(8,128)(2,1)S(1)} %pad_maximum_fusion.5.refs_3_), channel_id=1, source_target_pairs={{0,4},{4,0},{8,12},{12,8},{16,20},{20,16},{24,28},{28,24},{1,5},{5... | collective-permute-start | bytes 270344 | tf_op jit(solution)/shard_map/ppermute | solution.py:282
  36.5 2.3 %collective-permute-start.10 = (bf16[11,2,16,128]{3,2,1,0:T(8,128)(2,1)S(1)}, bf16[11,2,16,128]{3,2,1,0:T(8,128)(2,1)S(1)}, u32[]{:S(2)}, u32[]{:S(2)}) collective-permute-start(bf16[11,2,16,128]{3,2,1,0:T(8,128)(2,1)S(1)} %collective-permute-done.7.refs_0_), channel_id=1, source_target_pairs={{0,4},{4,0},{8,12},{12,8},{16,20},{20,16},{24,28},{28,24},{1,5},{5... | collective-permute-start | bytes 270344 | tf_op jit(solution)/shard_map/ppermute | solution.py:282
  37.1 1.8 %collective-permute-start.11 = (bf16[11,2,16,128]{3,2,1,0:T(8,128)(2,1)S(1)}, bf16[11,2,16,128]{3,2,1,0:T(8,128)(2,1)S(1)}, u32[]{:S(2)}, u32[]{:S(2)}) collective-permute-start(bf16[11,2,16,128]{3,2,1,0:T(8,128)(2,1)S(1)} %collective-permute-done.8.refs_1_), channel_id=1, source_target_pairs={{0,4},{4,0},{8,12},{12,8},{16,20},{20,16},{24,28},{28,24},{1,5},{5... | collective-permute-start | bytes 270344 | tf_op jit(solution)/shard_map/ppermute | solution.py:282
  37.1 1.7 %collective-permute-start.12 = (bf16[11,2,16,128]{3,2,1,0:T(8,128)(2,1)S(1)}, bf16[11,2,16,128]{3,2,1,0:T(8,128)(2,1)S(1)}, u32[]{:S(2)}, u32[]{:S(2)}) collective-permute-start(bf16[11,2,16,128]{3,2,1,0:T(8,128)(2,1)S(1)} %collective-permute-done.9.refs_2_), channel_id=1, source_target_pairs={{0,4},{4,0},{8,12},{12,8},{16,20},{20,16},{24,28},{28,24},{1,5},{5... | collective-permute-start | bytes 270344 | tf_op jit(solution)/shard_map/ppermute | solution.py:282
  40.0 7.5 %collective-permute-start.14 = (bf16[128,256]{1,0:T(8,128)(2,1)S(1)}, bf16[128,256]{1,0:T(8,128)(2,1)S(1)}, u32[]{:S(2)}, u32[]{:S(2)}) collective-permute-start(bf16[128,256]{1,0:T(8,128)(2,1)S(1)} %panel_sums.3.refs_3_), channel_id=1, source_target_pairs={{0,2},{1,3},{2,0},{3,1},{4,6},{5,7},{6,4},{7,5},{8,10},{9,11},{10,... | collective-permute-start | bytes 196616 | tf_op jit(solution)/shard_map/ppermute | solution.py:282
  42.1 6.5 %collective-permute-start.15 = (bf16[128,256]{1,0:T(8,128)(2,1)S(1)}, bf16[128,256]{1,0:T(8,128)(2,1)S(1)}, u32[]{:S(2)}, u32[]{:S(2)}) collective-permute-start(bf16[128,256]{1,0:T(8,128)(2,1)S(1)} %panel_sums.3.refs_3_), channel_id=1, source_target_pairs={{0,3},{1,2},{2,1},{3,0},{4,7},{5,6},{6,5},{7,4},{8,11},{9,10},{10,... | collective-permute-start | bytes 196616 | tf_op jit(solution)/shard_map/ppermute | solution.py:282
  44.0 5.5 %collective-permute-start.16 = (bf16[128,256]{1,0:T(8,128)(2,1)S(1)}, bf16[128,256]{1,0:T(8,128)(2,1)S(1)}, u32[]{:S(2)}, u32[]{:S(2)}) collective-permute-start(bf16[128,256]{1,0:T(8,128)(2,1)S(1)} %panel_sums.3.refs_3_), channel_id=1, source_target_pairs={{0,1},{1,0},{2,3},{3,2},{4,5},{5,4},{6,7},{7,6},{8,9},{9,8},{10,11... | collective-permute-start | bytes 196616 | tf_op jit(solution)/shard_map/ppermute | solution.py:282
  51.2 1.3 %collective-permute-start.17 = (f32[64,128]{1,0:T(8,128)S(1)}, f32[64,128]{1,0:T(8,128)S(1)}, u32[]{:S(2)}, u32[]{:S(2)}) collective-permute-start(f32[64,128]{1,0:T(8,128)S(1)} %field_sums.1), channel_id=1, source_target_pairs={{0,4},{4,0},{8,12},{12,8},{16,20},{20,16},{24,28},{28,24},{1,5},{5... | collective-permute-start | bytes 98312 | tf_op jit(solution)/shard_map/ppermute | solution.py:282
  52.5 4.8 %collective-permute-start.18 = (f32[64,128]{1,0:T(8,128)S(1)}, f32[64,128]{1,0:T(8,128)S(1)}, u32[]{:S(2)}, u32[]{:S(2)}) collective-permute-start(f32[64,128]{1,0:T(8,128)S(1)} %add.110), channel_id=1, source_target_pairs={{0,24},{4,28},{8,16},{12,20},{16,8},{20,12},{24,0},{28,4},{1,25},{... | collective-permute-start | bytes 98312 | tf_op jit(solution)/shard_map/ppermute | solution.py:282
  54.5 3.9 %collective-permute-start.19 = (f32[64,128]{1,0:T(8,128)S(1)}, f32[64,128]{1,0:T(8,128)S(1)}, u32[]{:S(2)}, u32[]{:S(2)}) collective-permute-start(f32[64,128]{1,0:T(8,128)S(1)} %add.110), channel_id=1, source_target_pairs={{0,16},{4,20},{8,24},{12,28},{16,0},{20,4},{24,8},{28,12},{1,17},{... | collective-permute-start | bytes 98312 | tf_op jit(solution)/shard_map/ppermute | solution.py:282
  55.2 3.9 %collective-permute-start.20 = (f32[64,128]{1,0:T(8,128)S(1)}, f32[64,128]{1,0:T(8,128)S(1)}, u32[]{:S(2)}, u32[]{:S(2)}) collective-permute-start(f32[64,128]{1,0:T(8,128)S(1)} %add.110), channel_id=1, source_target_pairs={{0,8},{4,12},{8,0},{12,4},{16,24},{20,28},{24,16},{28,20},{1,9},{5... | collective-permute-start | bytes 98312 | tf_op jit(solution)/shard_map/ppermute | solution.py:282

commit v4 on v3

--- a/solution.py
+++ b/solution.py
@@ -33,15 +33,13 @@
     return rows, copies
 
 
-def forces_sums(half_ref, left_ref, modes_ref, out_ref, top_ref, held_ref, sems, ready):
-    width = held_ref.shape[1]
-    rows, copies = start_rows(modes_ref, held_ref, sems, pl.multiple_of(half_ref[0] * width, 128))
-    ready()
-    for k, copy in enumerate(copies):
-        copy.wait()
+def forces_sums(left_ref, block_of, copies, rows, out_ref, top_ref):
+    for k in range(left_ref.shape[1] // rows):
+        if copies:
+            copies[k].wait()
         block = slice(k * rows, (k + 1) * rows)
-        part = jnp.dot(left_ref[:, block], held_ref[block, :], preferred_element_type=F32)
-        for t in range(width // 128):
+        part = jnp.dot(left_ref[:, block], block_of(block), preferred_element_type=F32)
+        for t in range(out_ref.shape[0]):
             tile = part[:, t * 128 : (t + 1) * 128]
             out_ref[t] = tile if k == 0 else out_ref[t] + tile
     top_ref[...] = jnp.full(top_ref.shape, jnp.max(jnp.abs(out_ref[...])), F32)
@@ -50,18 +48,19 @@
 def first_kernel(half_ref, pressure_ref, modes_ref, out_ref, top_ref, left_ref, loads_ref, held_ref, sem, sems):
     load = pltpu.make_async_copy(pressure_ref, loads_ref, sem)
     load.start()
-
-    def ready():
-        load.wait()
-        rows = loads_ref.shape[1]
-        for k in range(loads_ref.shape[0]):
-            left_ref[:, k * rows : (k + 1) * rows] = loads_ref[k].T
-
-    forces_sums(half_ref, left_ref, modes_ref, out_ref, top_ref, held_ref, sems, ready)
-
-
-def second_kernel(half_ref, left_ref, modes_ref, out_ref, top_ref, held_ref, sems):
-    forces_sums(half_ref, left_ref, modes_ref, out_ref, top_ref, held_ref, sems, lambda: None)
+    width = held_ref.shape[1]
+    rows, copies = start_rows(modes_ref, held_ref, sems, pl.multiple_of(half_ref[0] * width, 128))
+    load.wait()
+    for k in range(loads_ref.shape[0]):
+        part = loads_ref.shape[1]
+        left_ref[:, k * part : (k + 1) * part] = loads_ref[k].T
+    forces_sums(left_ref, lambda block: held_ref[block, :], copies, rows, out_ref, top_ref)
+
+
+def second_kernel(half_ref, left_ref, modes_ref, out_ref, top_ref):
+    width = modes_ref.shape[1] // 2
+    columns = pl.ds(pl.multiple_of(half_ref[0] * width, 128), width)
+    forces_sums(left_ref, lambda block: modes_ref[block, columns], None, row_block(left_ref.shape[1]), out_ref, top_ref)
 
 
 def forces_half(half, pressure, modes, first):
@@ -79,13 +78,15 @@
         pltpu.SemaphoreType.DMA,
         pltpu.SemaphoreType.DMA((nodes // row_block(nodes),)),
     ]
+    if first:
+        pressure, modes = (pltpu.with_memory_space_constraint(x, pltpu.HBM) for x in (pressure, modes))
     return pl.pallas_call(
         first_kernel if first else second_kernel,
-        in_specs=[pl.BlockSpec(memory_space=pltpu.SMEM), hbm if first else vmem, hbm],
+        in_specs=[pl.BlockSpec(memory_space=pltpu.SMEM)] + ([hbm, hbm] if first else [vmem, vmem]),
         out_specs=[vmem] * len(outs),
         out_shape=outs,
-        scratch_shapes=scratch if first else scratch[1::2],
-        compiler_params=pltpu.CompilerParams(vmem_limit_bytes=51 * MIB),
+        scratch_shapes=scratch if first else [],
+        compiler_params=pltpu.CompilerParams(vmem_limit_bytes=16 * MIB),
         cost_estimate=pl.CostEstimate(
             flops=2 * nodes * columns * width, bytes_accessed=2 * nodes * width, transcendentals=0
         ),
@@ -128,12 +129,12 @@
             pltpu.VMEM((PANEL_DEV, width), F32),
             pltpu.SemaphoreType.DMA((blocks,)),
         ],
-        compiler_params=pltpu.CompilerParams(vmem_limit_bytes=51 * MIB),
+        compiler_params=pltpu.CompilerParams(vmem_limit_bytes=16 * MIB),
         cost_estimate=pl.CostEstimate(
             flops=2 * nodes * PANEL_DEV * width, bytes_accessed=2 * nodes * width, transcendentals=0
         ),
         name="panel_modes",
-    )(half, panel_of.reshape(1, nodes), modes)
+    )(half, panel_of.reshape(1, nodes), pltpu.with_memory_space_constraint(modes, pltpu.HBM))
 
 
 def sin_cos(angle):
@@ -319,7 +320,8 @@
             (1 - core).reshape(1), pressure.reshape(-1, row_block(pressure.shape[0]), columns), modes, True
         )
         came, came_top = (swap(x, "node", nodes_axis, 1) for x in (away, away_top))
-        home, home_top = forces_half(core.reshape(1), left, modes, False)
+        near = pltpu.with_memory_space_constraint(modes, pltpu.VMEM)
+        home, home_top = forces_half(core.reshape(1), left, near, False)
         total = (home + came).reshape(tiles, 2, half, 128)
         bound = jnp.maximum(home_top[:1] + came_top[:1], 1e-30)
         shift = (14.0 - jnp.ceil(jnp.log2(bound))).reshape(1, 1, 1, 128)

time: 59.9 us -> 58.4 us (0.975)
  Pallas kernels: 23.8 us -> 22.8 us
  local copies, waits for them, and re-layouts: 1.34 us -> 0.5 us
    pallas_call x2, Pallas kernels: 6.66 us -> 5.75 us  [forces_half(): pl.pallas_call(first_kernel if first else second_kernel, in_specs=[pl.Blo...]
    unnamed x12, local copies, waits for them, and re-layouts: 1.04 us -> 0.2 us
  transfers between devices with their start and end apart: 21 -> 21, of which waited for: 10 -> 11; matrix products, arithmetic and copies ran while one was open for 1% -> 1% of each run, Pallas kernels for 29% -> 26%
where the time goes in v4:
time: 58.4 us; the launch traced here: 58.2 us
  Pallas kernels  22.8 us (39%)
  starting transfers between devices  22.7 us (39%)
  waiting for transfers between devices  10.2 us (17%)
  other arithmetic  1.54 us (3%)
    ppermute x21, starting transfers between devices, swap(): return lax.ppermute(x, axis, [(i, i ^ k) for i in range(size)])  22.7 us
    ppermute x21, waiting for transfers between devices, swap(): return lax.ppermute(x, axis, [(i, i ^ k) for i in range(size)])  10.2 us
    pallas_call x2, Pallas kernels, panel_modes(): pl.pallas_call(panel_modes_kernel, in_specs=[pl.BlockSpec(memory_space=pl...  7.01 us
    pallas_call x3, Pallas kernels, radiation(): pl.pallas_call(functools.partial(radiation_kernel, first), grid=(count //...  6.06 us
    pallas_call x2, Pallas kernels, forces_half(): pl.pallas_call(first_kernel if first else second_kernel, in_specs=[pl.Blo...  5.75 us
    pallas_call x2, Pallas kernels, panel_sums(): pl.pallas_call(functools.partial(panel_sums_kernel, len(slots)), in_specs...  2.33 us
    pallas_call x1, Pallas kernels, field_sums(): pl.pallas_call(functools.partial(field_kernel, freqs, tuple(pieces)), in_...  1.66 us
  transfers between devices with their start and end apart: 21, of which 11 were waited for; matrix products, arithmetic and copies ran while one was open for 1% of the time, Pallas kernels for 26%

profile of v4, /device:TPU:0, one launch (start us, length us, event | category | flops | bytes accessed | tf_op | source)
XLA Modules:
  0.0 58.2 jit_solution(15208618887227338720)
XLA Ops:
  0.0 4.7 %forces_half.2 = (f32[11,128,128]{2,1,0:T(8,128)S(1)}, f32[8,128]{1,0:T(8,128)S(1)}, bf16[128,1792]{1,0:T(8,128)(2,1)S(1)}) custom-call(s32[1]{0:T(128)} %bitcast.5.half_ref, bf16[7,256,128]{2,1,0:T(8,128)(2,1)} %bitcast.55, bf16[1792,2816]{1,0:T(8,128)(2,1)} %modes_ref.7), custom_call_target="tpu_custom_call" | custom-call | flops 645922816 | bytes 5046272 | tf_op jit(solution)/shard_map/forces_half/pallas_call | solution.py:83
  4.7 0.5 collective-permute-start
  5.3 0.1 collective-permute-start.1
  5.3 0.2 copy-done
  5.5 1.0 %forces_half.3 = (f32[11,128,128]{2,1,0:T(8,128)S(1)}, f32[8,128]{1,0:T(8,128)S(1)}) custom-call(s32[1]{0:T(128)} %bitcast.half_ref, bf16[128,1792]{1,0:T(8,128)(2,1)S(1)} %get-tuple-element.48.left_ref, bf16[1792,2816]{1,0:T(8,128)(2,1)S(1)} %copy-done), custom_call_target="tpu_custom_call" | custom-call | flops 645922816 | bytes 5046272 | tf_op jit(solution)/shard_map/forces_half/pallas_call | solution.py:83
  6.7 0.1 reshape.271
  6.8 0.3 collective-permute-done.1
  7.1 0.1 add.99
  7.3 0.1 pad_maximum_fusion
  7.4 3.9 %collective-permute-start.2 = (f16[360,128]{1,0:T(8,128)(2,1)S(1)}, f16[360,128]{1,0:T(8,128)(2,1)S(1)}, u32[]{:S(2)}, u32[]{:S(2)}) collective-permute-start(f16[360,128]{1,0:T(8,128)(2,1)S(1)} %get-tuple-element.53), channel_id=1, source_target_pairs={{0,24},{4,28},{8,16},{12,20},{16,8},{20,12},{24,0},{28,4},{1,25},{... | collective-permute-start | bytes 276488 | tf_op jit(solution)/shard_map/ppermute | solution.py:283
  11.3 0.5 collective-permute-start.3
  11.8 0.1 collective-permute-start.4
  11.9 3.5 %panel_modes.2 = (bf16[256,1408]{1,0:T(8,128)(2,1)S(1)}, bf16[256,1408]{1,0:T(8,128)(2,1)S(1)}) custom-call(s32[1]{0:T(128)} %bitcast.half_ref, s32[1,1792]{1,0:T(1,128)S(1)} %reshape.278.panel_ref, bf16[1792,2816]{1,0:T(8,128)(2,1)} %modes_ref.7), custom_call_target="tpu_custom_call" | custom-call | flops 1291845632 | bytes 5046272 | tf_op jit(solution)/shard_map/panel_modes/pallas_call | solution.py:117
  15.5 0.8 %collective-permute-done.3 = f16[360,128]{1,0:T(8,128)(2,1)S(1)} collective-permute-done((f16[360,128]{1,0:T(8,128)(2,1)S(1)}, f16[360,128]{1,0:T(8,128)(2,1)S(1)}, u32[]{:S(2)}, u32[]{:S(2)}) %collective-permute-start.3) | collective-permute-done | bytes 92192 | tf_op jit(solution)/shard_map/ppermute | solution.py:283
  16.2 0.3 collective-permute-done.4
  16.6 0.1 multiply_convert_fusion.1
  16.8 1.6 %collective-permute-start.5 = (f16[360,128]{1,0:T(8,128)(2,1)S(1)}, f16[360,128]{1,0:T(8,128)(2,1)S(1)}, u32[]{:S(2)}, u32[]{:S(2)}) collective-permute-start(f16[360,128]{1,0:T(8,128)(2,1)S(1)} %pad_maximum_fusion.3), channel_id=1, source_target_pairs={{0,1},{1,0},{2,3},{3,2},{4,5},{5,4},{6,7},{7,6},{8,9},{9,8},{10,11... | collective-permute-start | bytes 276488 | tf_op jit(solution)/shard_map/ppermute | solution.py:283
  18.4 0.1 multiply_bitcast_fusion.1
  18.5 1.5 %radiation.3 = (bf16[2,1024,128]{2,1,0:T(8,128)(2,1)S(1)}, bf16[2,1024,128]{2,1,0:T(8,128)(2,1)S(1)}) custom-call(f32[8]{0:T(128)S(1)} %copy-done.2, s32[64,1024]{1,0:T(8,128)S(1)} %bitcast.48), custom_call_target="tpu_custom_call" | custom-call | flops 5242880 | bytes 524288 | tf_op jit(solution)/shard_map/radiation/pallas_call | solution.py:181
  20.0 1.4 %collective-permute-done.5 = f16[360,128]{1,0:T(8,128)(2,1)S(1)} collective-permute-done((f16[360,128]{1,0:T(8,128)(2,1)S(1)}, f16[360,128]{1,0:T(8,128)(2,1)S(1)}, u32[]{:S(2)}, u32[]{:S(2)}) %collective-permute-start.5) | collective-permute-done | bytes 92192 | tf_op jit(solution)/shard_map/ppermute | solution.py:283
  21.5 2.7 %collective-permute-start.6 = (f16[360,128]{1,0:T(8,128)(2,1)S(1)}, f16[360,128]{1,0:T(8,128)(2,1)S(1)}, u32[]{:S(2)}, u32[]{:S(2)}) collective-permute-start(f16[360,128]{1,0:T(8,128)(2,1)S(1)} %pad_maximum_fusion.4), channel_id=1, source_target_pairs={{0,2},{1,3},{2,0},{3,1},{4,6},{5,7},{6,4},{7,5},{8,10},{9,11},{10,... | collective-permute-start | bytes 276488 | tf_op jit(solution)/shard_map/ppermute | solution.py:283
  24.3 1.5 %radiation.4 = (bf16[2,1024,128]{2,1,0:T(8,128)(2,1)S(1)}, bf16[2,1024,128]{2,1,0:T(8,128)(2,1)S(1)}) custom-call(f32[8]{0:T(128)S(1)} %copy-done.2, s32[64,1024]{1,0:T(8,128)S(1)} %bitcast.49), custom_call_target="tpu_custom_call" | custom-call | flops 5242880 | bytes 524288 | tf_op jit(solution)/shard_map/radiation/pallas_call | solution.py:181
  25.8 1.3 %collective-permute-done.6 = f16[360,128]{1,0:T(8,128)(2,1)S(1)} collective-permute-done((f16[360,128]{1,0:T(8,128)(2,1)S(1)}, f16[360,128]{1,0:T(8,128)(2,1)S(1)}, u32[]{:S(2)}, u32[]{:S(2)}) %collective-permute-start.6) | collective-permute-done | bytes 92192 | tf_op jit(solution)/shard_map/ppermute | solution.py:283
  27.1 0.1 subtract_convert_fusion
  27.3 1.9 %collective-permute-start.7 = (bf16[11,2,16,128]{3,2,1,0:T(8,128)(2,1)S(1)}, bf16[11,2,16,128]{3,2,1,0:T(8,128)(2,1)S(1)}, u32[]{:S(2)}, u32[]{:S(2)}) collective-permute-start(bf16[11,2,16,128]{3,2,1,0:T(8,128)(2,1)S(1)} %pad_maximum_fusion.5.refs_3_), channel_id=1, source_target_pairs={{0,24},{4,28},{8,16},{12,20},{16,8},{20,12},{24,0},{28,4},{1,25},{... | collective-permute-start | bytes 270344 | tf_op jit(solution)/shard_map/ppermute | solution.py:283
  29.2 1.2 %collective-permute-start.8 = (bf16[11,2,16,128]{3,2,1,0:T(8,128)(2,1)S(1)}, bf16[11,2,16,128]{3,2,1,0:T(8,128)(2,1)S(1)}, u32[]{:S(2)}, u32[]{:S(2)}) collective-permute-start(bf16[11,2,16,128]{3,2,1,0:T(8,128)(2,1)S(1)} %pad_maximum_fusion.5.refs_3_), channel_id=1, source_target_pairs={{0,16},{4,20},{8,24},{12,28},{16,0},{20,4},{24,8},{28,12},{1,17},{... | collective-permute-start | bytes 270344 | tf_op jit(solution)/shard_map/ppermute | solution.py:283
  30.3 1.2 %collective-permute-start.9 = (bf16[11,2,16,128]{3,2,1,0:T(8,128)(2,1)S(1)}, bf16[11,2,16,128]{3,2,1,0:T(8,128)(2,1)S(1)}, u32[]{:S(2)}, u32[]{:S(2)}) collective-permute-start(bf16[11,2,16,128]{3,2,1,0:T(8,128)(2,1)S(1)} %pad_maximum_fusion.5.refs_3_), channel_id=1, source_target_pairs={{0,8},{4,12},{8,0},{12,4},{16,24},{20,28},{24,16},{28,20},{1,9},{5... | collective-permute-start | bytes 270344 | tf_op jit(solution)/shard_map/ppermute | solution.py:283
  31.5 3.5 %panel_modes.3 = (bf16[256,1408]{1,0:T(8,128)(2,1)S(1)}, bf16[256,1408]{1,0:T(8,128)(2,1)S(1)}) custom-call(s32[1]{0:T(128)} %bitcast.5.half_ref, s32[1,1792]{1,0:T(1,128)S(1)} %reshape.282.panel_ref, bf16[1792,2816]{1,0:T(8,128)(2,1)} %modes_ref.7), custom_call_target="tpu_custom_call" | custom-call | flops 1291845632 | bytes 5046272 | tf_op jit(solution)/shard_map/panel_modes/pallas_call | solution.py:117
  35.1 0.6 collective-permute-start.10
  35.6 0.1 collective-permute-start.11
  35.7 0.4 collective-permute-start.12
  36.2 1.2 %panel_sums.2.refs_6_ = f32[128,256]{1,0:T(8,128)S(1)} custom-call(s32[3]{0:T(128)S(1)} %pad_add_fusion.place_ref, bf16[11,2,16,128]{3,2,1,0:T(8,128)(2,1)S(1)} %collective-permute-done.7.refs_0_, bf16[11,2,16,128]{3,2,1,0:T(8,128)(2,1)S(1)} %collective-permute-done.8.refs_1_, bf16[11,2,16,128]{3,2,1,0:T(8,128)(2,1)S(1)} %collective-permute-done.9.refs_2_, ...), custom_call_target="tpu_custom_call" | custom-call | flops 184549376 | bytes 2883584 | tf_op jit(solution)/shard_map/panel_sums/pallas_call | solution.py:220
  37.4 1.2 %panel_sums.3.refs_3_ = bf16[128,256]{1,0:T(8,128)(2,1)S(1)} custom-call(s32[3]{0:T(128)S(1)} %pad_add_fusion.place_ref, bf16[11,2,16,128]{3,2,1,0:T(8,128)(2,1)S(1)} %collective-permute-done.10.refs_0_, bf16[11,2,16,128]{3,2,1,0:T(8,128)(2,1)S(1)} %collective-permute-done.11.refs_1_, bf16[11,2,16,128]{3,2,1,0:T(8,128)(2,1)S(1)} %collective-permute-done.12.refs_2_, ...), custom_call_target="tpu_custom_call" | custom-call | flops 184549376 | bytes 2883584 | tf_op jit(solution)/shard_map/panel_sums/pallas_call | solution.py:220
  38.6 2.1 %collective-permute-start.14 = (bf16[128,256]{1,0:T(8,128)(2,1)S(1)}, bf16[128,256]{1,0:T(8,128)(2,1)S(1)}, u32[]{:S(2)}, u32[]{:S(2)}) collective-permute-start(bf16[128,256]{1,0:T(8,128)(2,1)S(1)} %panel_sums.3.refs_3_), channel_id=1, source_target_pairs={{0,2},{1,3},{2,0},{3,1},{4,6},{5,7},{6,4},{7,5},{8,10},{9,11},{10,... | collective-permute-start | bytes 196616 | tf_op jit(solution)/shard_map/ppermute | solution.py:283
  40.7 1.9 %collective-permute-start.15 = (bf16[128,256]{1,0:T(8,128)(2,1)S(1)}, bf16[128,256]{1,0:T(8,128)(2,1)S(1)}, u32[]{:S(2)}, u32[]{:S(2)}) collective-permute-start(bf16[128,256]{1,0:T(8,128)(2,1)S(1)} %panel_sums.3.refs_3_), channel_id=1, source_target_pairs={{0,3},{1,2},{2,1},{3,0},{4,7},{5,6},{6,5},{7,4},{8,11},{9,10},{10,... | collective-permute-start | bytes 196616 | tf_op jit(solution)/shard_map/ppermute | solution.py:283
  42.6 0.5 collective-permute-start.16
  43.0 3.0 %radiation.5 = (bf16[2,1024,256]{2,1,0:T(8,128)(2,1)S(1)}, bf16[2,1024,256]{2,1,0:T(8,128)(2,1)S(1)}) custom-call(f32[8]{0:T(128)S(1)} %copy-done.2, s32[64,1024]{1,0:T(8,128)S(1)} %bitcast.50), custom_call_target="tpu_custom_call" | custom-call | flops 10485760 | bytes 1048576 | tf_op jit(solution)/shard_map/radiation/pallas_call | solution.py:181
  46.1 1.1 %collective-permute-done.15.refs_1_ = bf16[128,256]{1,0:T(8,128)(2,1)S(1)} collective-permute-done((bf16[128,256]{1,0:T(8,128)(2,1)S(1)}, bf16[128,256]{1,0:T(8,128)(2,1)S(1)}, u32[]{:S(2)}, u32[]{:S(2)}) %collective-permute-start.15) | collective-permute-done | bytes 65568 | tf_op jit(solution)/shard_map/ppermute | solution.py:283
  47.2 0.9 %collective-permute-done.16.refs_2_ = bf16[128,256]{1,0:T(8,128)(2,1)S(1)} collective-permute-done((bf16[128,256]{1,0:T(8,128)(2,1)S(1)}, bf16[128,256]{1,0:T(8,128)(2,1)S(1)}, u32[]{:S(2)}, u32[]{:S(2)}) %collective-permute-start.16) | collective-permute-done | bytes 65568 | tf_op jit(solution)/shard_map/ppermute | solution.py:283
  48.1 1.7 %field_sums.1 = f32[64,128]{1,0:T(8,128)S(1)} custom-call(s32[3]{0:T(128)S(1)} %pad_add_fusion.place_ref, bf16[128,256]{1,0:T(8,128)(2,1)S(1)} %collective-permute-done.14.refs_0_, bf16[128,256]{1,0:T(8,128)(2,1)S(1)} %collective-permute-done.15.refs_1_, bf16[128,256]{1,0:T(8,128)(2,1)S(1)} %collective-permute-done.16.refs_2_, ...), custom_call_target="tpu_custom_call" | custom-call | tf_op jit(solution)/shard_map/field_sums/pallas_call | solution.py:266
  49.8 1.2 %collective-permute-done.17 = f32[64,128]{1,0:T(8,128)S(1)} collective-permute-done((f32[64,128]{1,0:T(8,128)S(1)}, f32[64,128]{1,0:T(8,128)S(1)}, u32[]{:S(2)}, u32[]{:S(2)}) %collective-permute-start.17) | collective-permute-done | bytes 32800 | tf_op jit(solution)/shard_map/ppermute | solution.py:283
  51.0 2.1 %collective-permute-start.18 = (f32[64,128]{1,0:T(8,128)S(1)}, f32[64,128]{1,0:T(8,128)S(1)}, u32[]{:S(2)}, u32[]{:S(2)}) collective-permute-start(f32[64,128]{1,0:T(8,128)S(1)} %add.110), channel_id=1, source_target_pairs={{0,24},{4,28},{8,16},{12,20},{16,8},{20,12},{24,0},{28,4},{1,25},{... | collective-permute-start | bytes 98312 | tf_op jit(solution)/shard_map/ppermute | solution.py:283
  53.1 0.6 %collective-permute-start.19 = (f32[64,128]{1,0:T(8,128)S(1)}, f32[64,128]{1,0:T(8,128)S(1)}, u32[]{:S(2)}, u32[]{:S(2)}) collective-permute-start(f32[64,128]{1,0:T(8,128)S(1)} %add.110), channel_id=1, source_target_pairs={{0,16},{4,20},{8,24},{12,28},{16,0},{20,4},{24,8},{28,12},{1,17},{... | collective-permute-start | bytes 98312 | tf_op jit(solution)/shard_map/ppermute | solution.py:283
  53.7 0.8 %collective-permute-start.20 = (f32[64,128]{1,0:T(8,128)S(1)}, f32[64,128]{1,0:T(8,128)S(1)}, u32[]{:S(2)}, u32[]{:S(2)}) collective-permute-start(f32[64,128]{1,0:T(8,128)S(1)} %add.110), channel_id=1, source_target_pairs={{0,8},{4,12},{8,0},{12,4},{16,24},{20,28},{24,16},{28,20},{1,9},{5... | collective-permute-start | bytes 98312 | tf_op jit(solution)/shard_map/ppermute | solution.py:283
  54.5 1.4 %collective-permute-done.18 = f32[64,128]{1,0:T(8,128)S(1)} collective-permute-done((f32[64,128]{1,0:T(8,128)S(1)}, f32[64,128]{1,0:T(8,128)S(1)}, u32[]{:S(2)}, u32[]{:S(2)}) %collective-permute-start.18) | collective-permute-done | bytes 32800 | tf_op jit(solution)/shard_map/ppermute | solution.py:283
  55.8 1.1 %collective-permute-done.19 = f32[64,128]{1,0:T(8,128)S(1)} collective-permute-done((f32[64,128]{1,0:T(8,128)S(1)}, f32[64,128]{1,0:T(8,128)S(1)}, u32[]{:S(2)}, u32[]{:S(2)}) %collective-permute-start.19) | collective-permute-done | bytes 32800 | tf_op jit(solution)/shard_map/ppermute | solution.py:283
  57.0 0.6 %collective-permute-done.20 = f32[64,128]{1,0:T(8,128)S(1)} collective-permute-done((f32[64,128]{1,0:T(8,128)S(1)}, f32[64,128]{1,0:T(8,128)S(1)}, u32[]{:S(2)}, u32[]{:S(2)}) %collective-permute-start.20) | collective-permute-done | bytes 32800 | tf_op jit(solution)/shard_map/ppermute | solution.py:283
  57.6 0.6 %add_add_fusion = f32[64,128]{1,0:T(8,128)} fusion(f32[64,128]{1,0:T(8,128)S(1)} %collective-permute-done.20, f32[64,128]{1,0:T(8,128)S(1)} %add.110, f32[64,128]{1,0:T(8,128)S(1)} %collective-permute-done.18, f32[64,128]{1,0:T(8,128)S(1)} %collective-permute-done.19), kind=kLoop, calls=%fused_computation.29 | loop fusion | flops 24576 | bytes 163840 | tf_op jit(solution)/shard_map/add | solution.py:278
  (49 shorter events, 0.8 us)
Async XLA Ops:
  0.0 5.5 %copy-start = (bf16[1792,2816]{1,0:T(8,128)(2,1)S(1)}, bf16[1792,2816]{1,0:T(8,128)(2,1)}, u32[]{:S(2)}) copy-start(bf16[1792,2816]{1,0:T(8,128)(2,1)} %modes_ref.7) | copy-start | bytes 30277636
  0.0 6.6 %copy-start.2 = (f32[8]{0:T(128)S(1)}, f32[8]{0:T(128)}, u32[]{:S(2)}) copy-start(f32[8]{0:T(128)} %omega_ref.5) | copy-start | bytes 100
  0.0 7.4 %copy-start.3 = (s32[1792]{0:T(1024)S(1)}, s32[1792]{0:T(1024)}, u32[]{:S(2)}) copy-start(s32[1792]{0:T(1024)} %param.12) | copy-start | bytes 21508
  4.7 2.4 %collective-permute-start = (f32[11,128,128]{2,1,0:T(8,128)S(1)}, f32[11,128,128]{2,1,0:T(8,128)S(1)}, u32[]{:S(2)}, u32[]{:S(2)}) collective-permute-start(f32[11,128,128]{2,1,0:T(8,128)S(1)} %get-tuple-element.50), channel_id=1, source_target_pairs={{0,4},{4,0},{8,12},{12,8},{16,20},{20,16},{24,28},{28,24},{1,5},{5... | collective-permute-start | bytes 2162696 | tf_op jit(solution)/shard_map/ppermute | solution.py:283
  5.3 1.8 %collective-permute-start.1 = (f32[8,128]{1,0:T(8,128)S(1)}, f32[8,128]{1,0:T(8,128)S(1)}, u32[]{:S(2)}, u32[]{:S(2)}) collective-permute-start(f32[8,128]{1,0:T(8,128)S(1)} %get-tuple-element.52), channel_id=1, source_target_pairs={{0,4},{4,0},{8,12},{12,8},{16,20},{20,16},{24,28},{28,24},{1,5},{5... | collective-permute-start | bytes 12296 | tf_op jit(solution)/shard_map/ppermute | solution.py:283
  6.6 11.9 %copy-start.4 = (f32[2816]{0:T(1024)S(1)}, f32[2816]{0:T(1024)}, u32[]{:S(2)}) copy-start(f32[2816]{0:T(1024)} %param.9) | copy-start | bytes 33796
  6.6 11.8 %copy-start.5 = (f32[2816]{0:T(1024)S(1)}, f32[2816]{0:T(1024)}, u32[]{:S(2)}) copy-start(f32[2816]{0:T(1024)} %param.10) | copy-start | bytes 33796
  6.6 11.9 %copy-start.1 = (s32[1024,64]{0,1:T(8,128)S(1)}, s32[1024,64]{0,1:T(8,128)}, u32[]{:S(2)}) copy-start(s32[1024,64]{0,1:T(8,128)} %param.13) | copy-start | bytes 786436
  7.4 8.0 %collective-permute-start.2 = (f16[360,128]{1,0:T(8,128)(2,1)S(1)}, f16[360,128]{1,0:T(8,128)(2,1)S(1)}, u32[]{:S(2)}, u32[]{:S(2)}) collective-permute-start(f16[360,128]{1,0:T(8,128)(2,1)S(1)} %get-tuple-element.53), channel_id=1, source_target_pairs={{0,24},{4,28},{8,16},{12,20},{16,8},{20,12},{24,0},{28,4},{1,25},{... | collective-permute-start | bytes 276488 | tf_op jit(solution)/shard_map/ppermute | solution.py:283
  11.3 4.9 %collective-permute-start.3 = (f16[360,128]{1,0:T(8,128)(2,1)S(1)}, f16[360,128]{1,0:T(8,128)(2,1)S(1)}, u32[]{:S(2)}, u32[]{:S(2)}) collective-permute-start(f16[360,128]{1,0:T(8,128)(2,1)S(1)} %get-tuple-element.54), channel_id=1, source_target_pairs={{0,16},{4,20},{8,24},{12,28},{16,0},{20,4},{24,8},{28,12},{1,17},{... | collective-permute-start | bytes 276488 | tf_op jit(solution)/shard_map/ppermute | solution.py:283
  11.8 4.7 %collective-permute-start.4 = (f16[360,128]{1,0:T(8,128)(2,1)S(1)}, f16[360,128]{1,0:T(8,128)(2,1)S(1)}, u32[]{:S(2)}, u32[]{:S(2)}) collective-permute-start(f16[360,128]{1,0:T(8,128)(2,1)S(1)} %get-tuple-element.55), channel_id=1, source_target_pairs={{0,8},{4,12},{8,0},{12,4},{16,24},{20,28},{24,16},{28,20},{1,9},{5... | collective-permute-start | bytes 276488 | tf_op jit(solution)/shard_map/ppermute | solution.py:283
  16.8 4.6 %collective-permute-start.5 = (f16[360,128]{1,0:T(8,128)(2,1)S(1)}, f16[360,128]{1,0:T(8,128)(2,1)S(1)}, u32[]{:S(2)}, u32[]{:S(2)}) collective-permute-start(f16[360,128]{1,0:T(8,128)(2,1)S(1)} %pad_maximum_fusion.3), channel_id=1, source_target_pairs={{0,1},{1,0},{2,3},{3,2},{4,5},{5,4},{6,7},{7,6},{8,9},{9,8},{10,11... | collective-permute-start | bytes 276488 | tf_op jit(solution)/shard_map/ppermute | solution.py:283
  21.5 5.5 %collective-permute-start.6 = (f16[360,128]{1,0:T(8,128)(2,1)S(1)}, f16[360,128]{1,0:T(8,128)(2,1)S(1)}, u32[]{:S(2)}, u32[]{:S(2)}) collective-permute-start(f16[360,128]{1,0:T(8,128)(2,1)S(1)} %pad_maximum_fusion.4), channel_id=1, source_target_pairs={{0,2},{1,3},{2,0},{3,1},{4,6},{5,7},{6,4},{7,5},{8,10},{9,11},{10,... | collective-permute-start | bytes 276488 | tf_op jit(solution)/shard_map/ppermute | solution.py:283
  27.3 7.8 %collective-permute-start.7 = (bf16[11,2,16,128]{3,2,1,0:T(8,128)(2,1)S(1)}, bf16[11,2,16,128]{3,2,1,0:T(8,128)(2,1)S(1)}, u32[]{:S(2)}, u32[]{:S(2)}) collective-permute-start(bf16[11,2,16,128]{3,2,1,0:T(8,128)(2,1)S(1)} %pad_maximum_fusion.5.refs_3_), channel_id=1, source_target_pairs={{0,24},{4,28},{8,16},{12,20},{16,8},{20,12},{24,0},{28,4},{1,25},{... | collective-permute-start | bytes 270344 | tf_op jit(solution)/shard_map/ppermute | solution.py:283
  29.2 5.9 %collective-permute-start.8 = (bf16[11,2,16,128]{3,2,1,0:T(8,128)(2,1)S(1)}, bf16[11,2,16,128]{3,2,1,0:T(8,128)(2,1)S(1)}, u32[]{:S(2)}, u32[]{:S(2)}) collective-permute-start(bf16[11,2,16,128]{3,2,1,0:T(8,128)(2,1)S(1)} %pad_maximum_fusion.5.refs_3_), channel_id=1, source_target_pairs={{0,16},{4,20},{8,24},{12,28},{16,0},{20,4},{24,8},{28,12},{1,17},{... | collective-permute-start | bytes 270344 | tf_op jit(solution)/shard_map/ppermute | solution.py:283
  30.3 4.7 %collective-permute-start.9 = (bf16[11,2,16,128]{3,2,1,0:T(8,128)(2,1)S(1)}, bf16[11,2,16,128]{3,2,1,0:T(8,128)(2,1)S(1)}, u32[]{:S(2)}, u32[]{:S(2)}) collective-permute-start(bf16[11,2,16,128]{3,2,1,0:T(8,128)(2,1)S(1)} %pad_maximum_fusion.5.refs_3_), channel_id=1, source_target_pairs={{0,8},{4,12},{8,0},{12,4},{16,24},{20,28},{24,16},{28,20},{1,9},{5... | collective-permute-start | bytes 270344 | tf_op jit(solution)/shard_map/ppermute | solution.py:283
  31.5 5.9 %collective-permute-start.13 = (bf16[11,2,16,128]{3,2,1,0:T(8,128)(2,1)S(1)}, bf16[11,2,16,128]{3,2,1,0:T(8,128)(2,1)S(1)}, u32[]{:S(2)}, u32[]{:S(2)}) collective-permute-start(bf16[11,2,16,128]{3,2,1,0:T(8,128)(2,1)S(1)} %pad_maximum_fusion.5.refs_3_), channel_id=1, source_target_pairs={{0,4},{4,0},{8,12},{12,8},{16,20},{20,16},{24,28},{28,24},{1,5},{5... | collective-permute-start | bytes 270344 | tf_op jit(solution)/shard_map/ppermute | solution.py:283
  35.1 2.3 %collective-permute-start.10 = (bf16[11,2,16,128]{3,2,1,0:T(8,128)(2,1)S(1)}, bf16[11,2,16,128]{3,2,1,0:T(8,128)(2,1)S(1)}, u32[]{:S(2)}, u32[]{:S(2)}) collective-permute-start(bf16[11,2,16,128]{3,2,1,0:T(8,128)(2,1)S(1)} %collective-permute-done.7.refs_0_), channel_id=1, source_target_pairs={{0,4},{4,0},{8,12},{12,8},{16,20},{20,16},{24,28},{28,24},{1,5},{5... | collective-permute-start | bytes 270344 | tf_op jit(solution)/shard_map/ppermute | solution.py:283
  35.6 1.8 %collective-permute-start.11 = (bf16[11,2,16,128]{3,2,1,0:T(8,128)(2,1)S(1)}, bf16[11,2,16,128]{3,2,1,0:T(8,128)(2,1)S(1)}, u32[]{:S(2)}, u32[]{:S(2)}) collective-permute-start(bf16[11,2,16,128]{3,2,1,0:T(8,128)(2,1)S(1)} %collective-permute-done.8.refs_1_), channel_id=1, source_target_pairs={{0,4},{4,0},{8,12},{12,8},{16,20},{20,16},{24,28},{28,24},{1,5},{5... | collective-permute-start | bytes 270344 | tf_op jit(solution)/shard_map/ppermute | solution.py:283
  35.7 1.7 %collective-permute-start.12 = (bf16[11,2,16,128]{3,2,1,0:T(8,128)(2,1)S(1)}, bf16[11,2,16,128]{3,2,1,0:T(8,128)(2,1)S(1)}, u32[]{:S(2)}, u32[]{:S(2)}) collective-permute-start(bf16[11,2,16,128]{3,2,1,0:T(8,128)(2,1)S(1)} %collective-permute-done.9.refs_2_), channel_id=1, source_target_pairs={{0,4},{4,0},{8,12},{12,8},{16,20},{20,16},{24,28},{28,24},{1,5},{5... | collective-permute-start | bytes 270344 | tf_op jit(solution)/shard_map/ppermute | solution.py:283
  38.6 7.5 %collective-permute-start.14 = (bf16[128,256]{1,0:T(8,128)(2,1)S(1)}, bf16[128,256]{1,0:T(8,128)(2,1)S(1)}, u32[]{:S(2)}, u32[]{:S(2)}) collective-permute-start(bf16[128,256]{1,0:T(8,128)(2,1)S(1)} %panel_sums.3.refs_3_), channel_id=1, source_target_pairs={{0,2},{1,3},{2,0},{3,1},{4,6},{5,7},{6,4},{7,5},{8,10},{9,11},{10,... | collective-permute-start | bytes 196616 | tf_op jit(solution)/shard_map/ppermute | solution.py:283
  40.7 6.5 %collective-permute-start.15 = (bf16[128,256]{1,0:T(8,128)(2,1)S(1)}, bf16[128,256]{1,0:T(8,128)(2,1)S(1)}, u32[]{:S(2)}, u32[]{:S(2)}) collective-permute-start(bf16[128,256]{1,0:T(8,128)(2,1)S(1)} %panel_sums.3.refs_3_), channel_id=1, source_target_pairs={{0,3},{1,2},{2,1},{3,0},{4,7},{5,6},{6,5},{7,4},{8,11},{9,10},{10,... | collective-permute-start | bytes 196616 | tf_op jit(solution)/shard_map/ppermute | solution.py:283
  42.6 5.5 %collective-permute-start.16 = (bf16[128,256]{1,0:T(8,128)(2,1)S(1)}, bf16[128,256]{1,0:T(8,128)(2,1)S(1)}, u32[]{:S(2)}, u32[]{:S(2)}) collective-permute-start(bf16[128,256]{1,0:T(8,128)(2,1)S(1)} %panel_sums.3.refs_3_), channel_id=1, source_target_pairs={{0,1},{1,0},{2,3},{3,2},{4,5},{5,4},{6,7},{7,6},{8,9},{9,8},{10,11... | collective-permute-start | bytes 196616 | tf_op jit(solution)/shard_map/ppermute | solution.py:283
  49.7 1.3 %collective-permute-start.17 = (f32[64,128]{1,0:T(8,128)S(1)}, f32[64,128]{1,0:T(8,128)S(1)}, u32[]{:S(2)}, u32[]{:S(2)}) collective-permute-start(f32[64,128]{1,0:T(8,128)S(1)} %field_sums.1), channel_id=1, source_target_pairs={{0,4},{4,0},{8,12},{12,8},{16,20},{20,16},{24,28},{28,24},{1,5},{5... | collective-permute-start | bytes 98312 | tf_op jit(solution)/shard_map/ppermute | solution.py:283
  51.0 4.8 %collective-permute-start.18 = (f32[64,128]{1,0:T(8,128)S(1)}, f32[64,128]{1,0:T(8,128)S(1)}, u32[]{:S(2)}, u32[]{:S(2)}) collective-permute-start(f32[64,128]{1,0:T(8,128)S(1)} %add.110), channel_id=1, source_target_pairs={{0,24},{4,28},{8,16},{12,20},{16,8},{20,12},{24,0},{28,4},{1,25},{... | collective-permute-start | bytes 98312 | tf_op jit(solution)/shard_map/ppermute | solution.py:283
  53.1 3.9 %collective-permute-start.19 = (f32[64,128]{1,0:T(8,128)S(1)}, f32[64,128]{1,0:T(8,128)S(1)}, u32[]{:S(2)}, u32[]{:S(2)}) collective-permute-start(f32[64,128]{1,0:T(8,128)S(1)} %add.110), channel_id=1, source_target_pairs={{0,16},{4,20},{8,24},{12,28},{16,0},{20,4},{24,8},{28,12},{1,17},{... | collective-permute-start | bytes 98312 | tf_op jit(solution)/shard_map/ppermute | solution.py:283
  53.7 3.9 %collective-permute-start.20 = (f32[64,128]{1,0:T(8,128)S(1)}, f32[64,128]{1,0:T(8,128)S(1)}, u32[]{:S(2)}, u32[]{:S(2)}) collective-permute-start(f32[64,128]{1,0:T(8,128)S(1)} %add.110), channel_id=1, source_target_pairs={{0,8},{4,12},{8,0},{12,4},{16,24},{20,28},{24,16},{28,20},{1,9},{5... | collective-permute-start | bytes 98312 | tf_op jit(solution)/shard_map/ppermute | solution.py:283

commit v5 on v4

--- a/solution.py
+++ b/solution.py
@@ -231,26 +231,44 @@
     )(place, *slots, *pair, *before)
 
 
+def field_products(order, own, pieces, kernels, before):
+    products = []
+    for part in range(2):
+        blocks, at = [], 0
+        for high, low in zip(kernels[::2], kernels[1::2], strict=True):
+            width = high.shape[2]
+            total = before[part, :, at : at + width] if before is not None else None
+            for k, piece in zip(order, pieces, strict=True):
+                rows = pl.ds(pl.multiple_of((own ^ k) * PANEL_DEV, PANEL_DEV), PANEL_DEV)
+                for ref in (high, low):
+                    term = jnp.dot(piece[...], ref[part, rows, :], preferred_element_type=F32)
+                    total = term if total is None else total + term
+            blocks.append(total)
+            at += width
+        products.append(blocks)
+    return products
+
+
+def field_start_kernel(order, place_ref, *refs):
+    pieces, kernels, out_ref = refs[: len(order)], refs[len(order) : -1], refs[-1]
+    for part, blocks in enumerate(field_products(order, place_ref[2], pieces, kernels, None)):
+        at = 0
+        for block in blocks:
+            out_ref[part, :, at : at + block.shape[1]] = block
+            at += block.shape[1]
+
+
 def field_kernel(freqs, order, place_ref, *refs):
-    pieces, kernels, out_ref = refs[: len(order)], refs[len(order) : -1], refs[-1]
-    own = place_ref[2]
+    pieces, (*kernels, before_ref, out_ref) = refs[: len(order)], refs[len(order) :]
     columns = pieces[0].shape[0]
     half = columns // 2
     field = out_ref.shape[0]
     wide = 2 * field
-    products = [[None] * (len(kernels) // 2) for _ in range(2)]
-    for k, piece in zip(order, pieces, strict=True):
-        rows = pl.ds(pl.multiple_of((own ^ k) * PANEL_DEV, PANEL_DEV), PANEL_DEV)
-        for part in range(2):
-            for at, ref in enumerate(kernels):
-                term = jnp.dot(piece[...], ref[part, rows, :], preferred_element_type=F32)
-                before = products[part][at // 2]
-                products[part][at // 2] = term if before is None else before + term
     row = lax.broadcasted_iota(jnp.int32, (columns, wide), 0)
     freq_of = (row % half) // (half // freqs)
     sums = []
-    for part in range(2):
-        blocks = [p[:, i : i + wide] for p in products[part] for i in range(0, p.shape[1], wide)]
+    for products in field_products(order, place_ref[2], pieces, kernels, before_ref):
+        blocks = [p[:, i : i + wide] for p in products for i in range(0, p.shape[1], wide)]
         picked = blocks[0]
         for pair in range(1, freqs // 2):
             picked = jnp.where(freq_of // 2 == pair, blocks[pair], picked)
@@ -260,17 +278,18 @@
     out_ref[...] = jnp.concatenate([real, imag], axis=0).T[:field]
 
 
-def field_sums(freqs, field, place, pieces, kernels):
-    columns = pieces[0].shape[0]
+def field_sums(freqs, field, place, pieces, kernels, *before):
+    columns = next(iter(pieces.values())).shape[0]
     vmem = pl.BlockSpec(memory_space=pltpu.VMEM)
+    order = tuple(pieces)
     return pl.pallas_call(
-        functools.partial(field_kernel, freqs, tuple(pieces)),
-        in_specs=[pl.BlockSpec(memory_space=pltpu.SMEM)] + [vmem] * (len(pieces) + len(kernels)),
+        functools.partial(field_kernel, freqs, order) if before else functools.partial(field_start_kernel, order),
+        in_specs=[pl.BlockSpec(memory_space=pltpu.SMEM)] + [vmem] * (len(pieces) + len(kernels) + len(before)),
         out_specs=vmem,
-        out_shape=jax.ShapeDtypeStruct((field, columns), F32),
+        out_shape=jax.ShapeDtypeStruct((field, columns) if before else (2, columns, freqs * field), F32),
         compiler_params=pltpu.CompilerParams(vmem_limit_bytes=24 * MIB),
         name="field_sums",
-    )(place, *pieces.values(), *kernels)
+    )(place, *pieces.values(), *kernels, *before)
 
 
 def tree(terms):
@@ -330,7 +349,7 @@
         sent = [
             pack(lax.dynamic_slice_in_dim(total, (chip ^ k) * group, group, 2), shift) for k in far_first(chips)
         ]
-        sent, panel_known = beside(sent, panel_of)
+        sent, panel_known, omega_known = lax.optimization_barrier((sent, panel_of, omega_force))
         came = [swap(piece, "node", nodes_axis, 2 * k) for k, piece in zip(far_first(chips), sent, strict=True)]
         came, first = beside(came, panel_modes(core.reshape(1), panel_known, modes))
         terms, shifts = [], [shift]
@@ -355,7 +374,7 @@
 
         wmod = lax.dynamic_slice_in_dim(omega_mode, core * width, width).reshape(tiles, 1, 128)
         damp = lax.dynamic_slice_in_dim(damping, core * width, width).reshape(tiles, 1, 128)
-        wcol = jnp.repeat(omega_force, half // omega_force.shape[0])
+        wcol = jnp.repeat(omega_known, half // omega_force.shape[0])
         wcol = lax.dynamic_slice_in_dim(wcol, chip * group, group)[None, :, None]
         real_part = wmod * wmod - wcol * wcol
         imag_part = 2.0 * damp * wmod * wcol
@@ -382,7 +401,10 @@
         pieces = {k: swap(sums, "fld", field_axis, k) for k in (2, 3, 1)} | {0: sums}
         done = sum(x.shape[2] // dist_bin.shape[1] for x in kernels[::2])
         kernels.extend(radiation(done, freqs - done, omega_force, bins))
-        field = field_sums(freqs, dist_bin.shape[1], place, pieces, kernels)
+        arrived = {k: pieces[k] for k in (0, field_axis // 2)}
+        waited = {k: piece for k, piece in pieces.items() if k not in arrived}
+        sizes = (freqs, dist_bin.shape[1], place)
+        field = field_sums(*sizes, waited, kernels, field_sums(*sizes, arrived, kernels))
         field = field + swap(field, "node", nodes_axis, 1)
         return tree([swap(field, "node", nodes_axis, 2 * k) for k in far_first(chips)] + [field])
 

time: 58.4 us -> 57.9 us (level)
  waiting for transfers between devices: 10.2 us -> 8.76 us
  Pallas kernels: 22.8 us -> 23.5 us
    ppermute x21, waiting for transfers between devices: 10.2 us -> 8.76 us  [swap(): return lax.ppermute(x, axis, [(i, i ^ k) for i in range(size)])]
    pallas_call x1 -> x2, Pallas kernels: 1.66 us -> 2.35 us  [field_sums(): pl.pallas_call(functools.partial(field_kernel, freqs, order) if before el...]
  transfers between devices with their start and end apart: 21 -> 21, of which waited for: 11 -> 10; matrix products, arithmetic and copies ran while one was open for 1% -> 1% of each run, Pallas kernels for 26% -> 28%
where the time goes in v5:
time: 57.9 us; the launch traced here: 57.7 us
  Pallas kernels  23.5 us (41%)
  starting transfers between devices  23 us (40%)
  waiting for transfers between devices  8.76 us (15%)
  other arithmetic  1.55 us (3%)
    ppermute x21, starting transfers between devices, swap(): return lax.ppermute(x, axis, [(i, i ^ k) for i in range(size)])  23 us
    ppermute x21, waiting for transfers between devices, swap(): return lax.ppermute(x, axis, [(i, i ^ k) for i in range(size)])  8.76 us
    pallas_call x2, Pallas kernels, panel_modes(): pl.pallas_call(panel_modes_kernel, in_specs=[pl.BlockSpec(memory_space=pl...  7.01 us
    pallas_call x3, Pallas kernels, radiation(): pl.pallas_call(functools.partial(radiation_kernel, first), grid=(count //...  6.07 us
    pallas_call x2, Pallas kernels, forces_half(): pl.pallas_call(first_kernel if first else second_kernel, in_specs=[pl.Blo...  5.74 us
    pallas_call x2, Pallas kernels, field_sums(): pl.pallas_call(functools.partial(field_kernel, freqs, order) if before el...  2.35 us
    pallas_call x2, Pallas kernels, panel_sums(): pl.pallas_call(functools.partial(panel_sums_kernel, len(slots)), in_specs...  2.34 us
  transfers between devices with their start and end apart: 21, of which 10 were waited for; matrix products, arithmetic and copies ran while one was open for 1% of the time, Pallas kernels for 28%

profile of v5, /device:TPU:0, one launch (start us, length us, event | category | flops | bytes accessed | tf_op | source)
XLA Modules:
  0.0 57.7 jit_solution(15778827724202689540)
XLA Ops:
  0.0 4.7 %forces_half.2 = (f32[11,128,128]{2,1,0:T(8,128)S(1)}, f32[8,128]{1,0:T(8,128)S(1)}, bf16[128,1792]{1,0:T(8,128)(2,1)S(1)}) custom-call(s32[1]{0:T(128)} %bitcast.4.half_ref, bf16[7,256,128]{2,1,0:T(8,128)(2,1)} %bitcast.55, bf16[1792,2816]{1,0:T(8,128)(2,1)} %modes_ref.7), custom_call_target="tpu_custom_call" | custom-call | flops 645922816 | bytes 5046272 | tf_op jit(solution)/shard_map/forces_half/pallas_call | solution.py:83
  4.7 0.5 collective-permute-start
  5.3 0.1 collective-permute-start.1
  5.3 0.2 copy-done
  5.5 1.0 %forces_half.3 = (f32[11,128,128]{2,1,0:T(8,128)S(1)}, f32[8,128]{1,0:T(8,128)S(1)}) custom-call(s32[1]{0:T(128)} %bitcast.half_ref, bf16[128,1792]{1,0:T(8,128)(2,1)S(1)} %get-tuple-element.49.left_ref, bf16[1792,2816]{1,0:T(8,128)(2,1)S(1)} %copy-done), custom_call_target="tpu_custom_call" | custom-call | flops 645922816 | bytes 5046272 | tf_op jit(solution)/shard_map/forces_half/pallas_call | solution.py:83
  6.6 0.4 collective-permute-done.1
  7.1 0.1 add.97
  7.3 0.1 pad_maximum_fusion
  7.4 3.9 %collective-permute-start.2 = (f16[360,128]{1,0:T(8,128)(2,1)S(1)}, f16[360,128]{1,0:T(8,128)(2,1)S(1)}, u32[]{:S(2)}, u32[]{:S(2)}) collective-permute-start(f16[360,128]{1,0:T(8,128)(2,1)S(1)} %get-tuple-element.55), channel_id=1, source_target_pairs={{0,24},{4,28},{8,16},{12,20},{16,8},{20,12},{24,0},{28,4},{1,25},{... | collective-permute-start | bytes 276488 | tf_op jit(solution)/shard_map/ppermute | solution.py:302
  11.3 0.5 collective-permute-start.3
  11.8 0.1 collective-permute-start.4
  11.9 3.5 %panel_modes.2 = (bf16[256,1408]{1,0:T(8,128)(2,1)S(1)}, bf16[256,1408]{1,0:T(8,128)(2,1)S(1)}) custom-call(s32[1]{0:T(128)} %bitcast.half_ref, s32[1,1792]{1,0:T(1,128)S(1)} %reshape.278.panel_ref, bf16[1792,2816]{1,0:T(8,128)(2,1)} %modes_ref.7), custom_call_target="tpu_custom_call" | custom-call | flops 1291845632 | bytes 5046272 | tf_op jit(solution)/shard_map/panel_modes/pallas_call | solution.py:117
  15.5 0.8 %collective-permute-done.3 = f16[360,128]{1,0:T(8,128)(2,1)S(1)} collective-permute-done((f16[360,128]{1,0:T(8,128)(2,1)S(1)}, f16[360,128]{1,0:T(8,128)(2,1)S(1)}, u32[]{:S(2)}, u32[]{:S(2)}) %collective-permute-start.3) | collective-permute-done | bytes 92192 | tf_op jit(solution)/shard_map/ppermute | solution.py:302
  16.2 0.2 collective-permute-done.4
  16.6 0.1 multiply_convert_fusion.1
  16.8 1.6 %collective-permute-start.5 = (f16[360,128]{1,0:T(8,128)(2,1)S(1)}, f16[360,128]{1,0:T(8,128)(2,1)S(1)}, u32[]{:S(2)}, u32[]{:S(2)}) collective-permute-start(f16[360,128]{1,0:T(8,128)(2,1)S(1)} %pad_maximum_fusion.3), channel_id=1, source_target_pairs={{0,1},{1,0},{2,3},{3,2},{4,5},{5,4},{6,7},{7,6},{8,9},{9,8},{10,11... | collective-permute-start | bytes 276488 | tf_op jit(solution)/shard_map/ppermute | solution.py:302
  18.4 0.1 multiply_bitcast_fusion.1
  18.6 0.1 reshape.277
  18.6 1.5 %radiation.3 = (bf16[2,1024,128]{2,1,0:T(8,128)(2,1)S(1)}, bf16[2,1024,128]{2,1,0:T(8,128)(2,1)S(1)}) custom-call(f32[8]{0:T(128)S(1)} %copy-done.2, s32[64,1024]{1,0:T(8,128)S(1)} %bitcast.48), custom_call_target="tpu_custom_call" | custom-call | flops 5242880 | bytes 524288 | tf_op jit(solution)/shard_map/radiation/pallas_call | solution.py:181
  20.2 1.2 %collective-permute-done.5 = f16[360,128]{1,0:T(8,128)(2,1)S(1)} collective-permute-done((f16[360,128]{1,0:T(8,128)(2,1)S(1)}, f16[360,128]{1,0:T(8,128)(2,1)S(1)}, u32[]{:S(2)}, u32[]{:S(2)}) %collective-permute-start.5) | collective-permute-done | bytes 92192 | tf_op jit(solution)/shard_map/ppermute | solution.py:302
  21.5 2.7 %collective-permute-start.6 = (f16[360,128]{1,0:T(8,128)(2,1)S(1)}, f16[360,128]{1,0:T(8,128)(2,1)S(1)}, u32[]{:S(2)}, u32[]{:S(2)}) collective-permute-start(f16[360,128]{1,0:T(8,128)(2,1)S(1)} %pad_maximum_fusion.4), channel_id=1, source_target_pairs={{0,2},{1,3},{2,0},{3,1},{4,6},{5,7},{6,4},{7,5},{8,10},{9,11},{10,... | collective-permute-start | bytes 276488 | tf_op jit(solution)/shard_map/ppermute | solution.py:302
  24.2 1.5 %radiation.4 = (bf16[2,1024,128]{2,1,0:T(8,128)(2,1)S(1)}, bf16[2,1024,128]{2,1,0:T(8,128)(2,1)S(1)}) custom-call(f32[8]{0:T(128)S(1)} %copy-done.2, s32[64,1024]{1,0:T(8,128)S(1)} %bitcast.49), custom_call_target="tpu_custom_call" | custom-call | flops 5242880 | bytes 524288 | tf_op jit(solution)/shard_map/radiation/pallas_call | solution.py:181
  25.8 1.3 %collective-permute-done.6 = f16[360,128]{1,0:T(8,128)(2,1)S(1)} collective-permute-done((f16[360,128]{1,0:T(8,128)(2,1)S(1)}, f16[360,128]{1,0:T(8,128)(2,1)S(1)}, u32[]{:S(2)}, u32[]{:S(2)}) %collective-permute-start.6) | collective-permute-done | bytes 92192 | tf_op jit(solution)/shard_map/ppermute | solution.py:302
  27.1 0.1 subtract_convert_fusion
  27.3 1.9 %collective-permute-start.7 = (bf16[11,2,16,128]{3,2,1,0:T(8,128)(2,1)S(1)}, bf16[11,2,16,128]{3,2,1,0:T(8,128)(2,1)S(1)}, u32[]{:S(2)}, u32[]{:S(2)}) collective-permute-start(bf16[11,2,16,128]{3,2,1,0:T(8,128)(2,1)S(1)} %pad_maximum_fusion.5.refs_3_), channel_id=1, source_target_pairs={{0,24},{4,28},{8,16},{12,20},{16,8},{20,12},{24,0},{28,4},{1,25},{... | collective-permute-start | bytes 270344 | tf_op jit(solution)/shard_map/ppermute | solution.py:302
  29.2 1.1 %collective-permute-start.8 = (bf16[11,2,16,128]{3,2,1,0:T(8,128)(2,1)S(1)}, bf16[11,2,16,128]{3,2,1,0:T(8,128)(2,1)S(1)}, u32[]{:S(2)}, u32[]{:S(2)}) collective-permute-start(bf16[11,2,16,128]{3,2,1,0:T(8,128)(2,1)S(1)} %pad_maximum_fusion.5.refs_3_), channel_id=1, source_target_pairs={{0,16},{4,20},{8,24},{12,28},{16,0},{20,4},{24,8},{28,12},{1,17},{... | collective-permute-start | bytes 270344 | tf_op jit(solution)/shard_map/ppermute | solution.py:302
  30.3 1.2 %collective-permute-start.9 = (bf16[11,2,16,128]{3,2,1,0:T(8,128)(2,1)S(1)}, bf16[11,2,16,128]{3,2,1,0:T(8,128)(2,1)S(1)}, u32[]{:S(2)}, u32[]{:S(2)}) collective-permute-start(bf16[11,2,16,128]{3,2,1,0:T(8,128)(2,1)S(1)} %pad_maximum_fusion.5.refs_3_), channel_id=1, source_target_pairs={{0,8},{4,12},{8,0},{12,4},{16,24},{20,28},{24,16},{28,20},{1,9},{5... | collective-permute-start | bytes 270344 | tf_op jit(solution)/shard_map/ppermute | solution.py:302
  31.5 3.5 %panel_modes.3 = (bf16[256,1408]{1,0:T(8,128)(2,1)S(1)}, bf16[256,1408]{1,0:T(8,128)(2,1)S(1)}) custom-call(s32[1]{0:T(128)} %bitcast.4.half_ref, s32[1,1792]{1,0:T(1,128)S(1)} %reshape.282.panel_ref, bf16[1792,2816]{1,0:T(8,128)(2,1)} %modes_ref.7), custom_call_target="tpu_custom_call" | custom-call | flops 1291845632 | bytes 5046272 | tf_op jit(solution)/shard_map/panel_modes/pallas_call | solution.py:117
  35.0 0.6 collective-permute-start.10
  35.6 0.1 collective-permute-start.11
  35.7 0.4 collective-permute-start.12
  36.2 1.2 %panel_sums.2.refs_6_ = f32[128,256]{1,0:T(8,128)S(1)} custom-call(s32[3]{0:T(128)S(1)} %pad_add_fusion.place_ref, bf16[11,2,16,128]{3,2,1,0:T(8,128)(2,1)S(1)} %collective-permute-done.7.refs_0_, bf16[11,2,16,128]{3,2,1,0:T(8,128)(2,1)S(1)} %collective-permute-done.8.refs_1_, bf16[11,2,16,128]{3,2,1,0:T(8,128)(2,1)S(1)} %collective-permute-done.9.refs_2_, ...), custom_call_target="tpu_custom_call" | custom-call | flops 184549376 | bytes 2883584 | tf_op jit(solution)/shard_map/panel_sums/pallas_call | solution.py:220
  37.4 1.2 %panel_sums.3.refs_0_ = bf16[128,256]{1,0:T(8,128)(2,1)S(1)} custom-call(s32[3]{0:T(128)S(1)} %pad_add_fusion.place_ref, bf16[11,2,16,128]{3,2,1,0:T(8,128)(2,1)S(1)} %collective-permute-done.10.refs_0_, bf16[11,2,16,128]{3,2,1,0:T(8,128)(2,1)S(1)} %collective-permute-done.11.refs_1_, bf16[11,2,16,128]{3,2,1,0:T(8,128)(2,1)S(1)} %collective-permute-done.12.refs_2_, ...), custom_call_target="tpu_custom_call" | custom-call | flops 184549376 | bytes 2883584 | tf_op jit(solution)/shard_map/panel_sums/pallas_call | solution.py:220
  38.6 2.1 %collective-permute-start.16 = (bf16[128,256]{1,0:T(8,128)(2,1)S(1)}, bf16[128,256]{1,0:T(8,128)(2,1)S(1)}, u32[]{:S(2)}, u32[]{:S(2)}) collective-permute-start(bf16[128,256]{1,0:T(8,128)(2,1)S(1)} %panel_sums.3.refs_0_), channel_id=1, source_target_pairs={{0,2},{1,3},{2,0},{3,1},{4,6},{5,7},{6,4},{7,5},{8,10},{9,11},{10,... | collective-permute-start | bytes 196616 | tf_op jit(solution)/shard_map/ppermute | solution.py:302
  40.7 1.9 %collective-permute-start.14 = (bf16[128,256]{1,0:T(8,128)(2,1)S(1)}, bf16[128,256]{1,0:T(8,128)(2,1)S(1)}, u32[]{:S(2)}, u32[]{:S(2)}) collective-permute-start(bf16[128,256]{1,0:T(8,128)(2,1)S(1)} %panel_sums.3.refs_0_), channel_id=1, source_target_pairs={{0,3},{1,2},{2,1},{3,0},{4,7},{5,6},{6,5},{7,4},{8,11},{9,10},{10,... | collective-permute-start | bytes 196616 | tf_op jit(solution)/shard_map/ppermute | solution.py:302
  42.6 0.5 collective-permute-start.15
  43.0 3.0 %radiation.5 = (bf16[2,1024,256]{2,1,0:T(8,128)(2,1)S(1)}, bf16[2,1024,256]{2,1,0:T(8,128)(2,1)S(1)}) custom-call(f32[8]{0:T(128)S(1)} %copy-done.2, s32[64,1024]{1,0:T(8,128)S(1)} %bitcast.50), custom_call_target="tpu_custom_call" | custom-call | flops 10485760 | bytes 1048576 | tf_op jit(solution)/shard_map/radiation/pallas_call | solution.py:181
  46.1 1.1 %field_sums.2.refs_8_ = f32[2,128,512]{2,1,0:T(8,128)S(1)} custom-call(s32[3]{0:T(128)S(1)} %pad_add_fusion.place_ref, bf16[128,256]{1,0:T(8,128)(2,1)S(1)} %panel_sums.3.refs_0_, bf16[128,256]{1,0:T(8,128)(2,1)S(1)} %collective-permute-done.16.refs_1_, bf16[2,1024,128]{2,1,0:T(8,128)(2,1)S(1)} %get-tuple-element.86.refs_2_, ...), custom_call_target="tpu_custom_call" | custom-call | tf_op jit(solution)/shard_map/field_sums/pallas_call | solution.py:285
  47.2 0.8 %collective-permute-done.15.refs_1_ = bf16[128,256]{1,0:T(8,128)(2,1)S(1)} collective-permute-done((bf16[128,256]{1,0:T(8,128)(2,1)S(1)}, bf16[128,256]{1,0:T(8,128)(2,1)S(1)}, u32[]{:S(2)}, u32[]{:S(2)}) %collective-permute-start.15) | collective-permute-done | bytes 65568 | tf_op jit(solution)/shard_map/ppermute | solution.py:302
  48.0 1.2 %field_sums.3 = f32[64,128]{1,0:T(8,128)S(1)} custom-call(s32[3]{0:T(128)S(1)} %pad_add_fusion.place_ref, bf16[128,256]{1,0:T(8,128)(2,1)S(1)} %collective-permute-done.14.refs_0_, bf16[128,256]{1,0:T(8,128)(2,1)S(1)} %collective-permute-done.15.refs_1_, bf16[2,1024,128]{2,1,0:T(8,128)(2,1)S(1)} %get-tuple-element.86.refs_2_, ...), custom_call_target="tpu_custom_call" | custom-call | tf_op jit(solution)/shard_map/field_sums/pallas_call | solution.py:285
  49.4 1.2 %collective-permute-done.17 = f32[64,128]{1,0:T(8,128)S(1)} collective-permute-done((f32[64,128]{1,0:T(8,128)S(1)}, f32[64,128]{1,0:T(8,128)S(1)}, u32[]{:S(2)}, u32[]{:S(2)}) %collective-permute-start.17) | collective-permute-done | bytes 32800 | tf_op jit(solution)/shard_map/ppermute | solution.py:302
  50.6 2.2 %collective-permute-start.18 = (f32[64,128]{1,0:T(8,128)S(1)}, f32[64,128]{1,0:T(8,128)S(1)}, u32[]{:S(2)}, u32[]{:S(2)}) collective-permute-start(f32[64,128]{1,0:T(8,128)S(1)} %add.110), channel_id=1, source_target_pairs={{0,24},{4,28},{8,16},{12,20},{16,8},{20,12},{24,0},{28,4},{1,25},{... | collective-permute-start | bytes 98312 | tf_op jit(solution)/shard_map/ppermute | solution.py:302
  52.7 0.5 collective-permute-start.19
  53.2 1.1 %collective-permute-start.20 = (f32[64,128]{1,0:T(8,128)S(1)}, f32[64,128]{1,0:T(8,128)S(1)}, u32[]{:S(2)}, u32[]{:S(2)}) collective-permute-start(f32[64,128]{1,0:T(8,128)S(1)} %add.110), channel_id=1, source_target_pairs={{0,8},{4,12},{8,0},{12,4},{16,24},{20,28},{24,16},{28,20},{1,9},{5... | collective-permute-start | bytes 98312 | tf_op jit(solution)/shard_map/ppermute | solution.py:302
  54.3 1.1 %collective-permute-done.18 = f32[64,128]{1,0:T(8,128)S(1)} collective-permute-done((f32[64,128]{1,0:T(8,128)S(1)}, f32[64,128]{1,0:T(8,128)S(1)}, u32[]{:S(2)}, u32[]{:S(2)}) %collective-permute-start.18) | collective-permute-done | bytes 32800 | tf_op jit(solution)/shard_map/ppermute | solution.py:302
  55.4 1.2 %collective-permute-done.19 = f32[64,128]{1,0:T(8,128)S(1)} collective-permute-done((f32[64,128]{1,0:T(8,128)S(1)}, f32[64,128]{1,0:T(8,128)S(1)}, u32[]{:S(2)}, u32[]{:S(2)}) %collective-permute-start.19) | collective-permute-done | bytes 32800 | tf_op jit(solution)/shard_map/ppermute | solution.py:302
  56.6 0.5 collective-permute-done.20
  57.1 0.6 %add_add_fusion = f32[64,128]{1,0:T(8,128)} fusion(f32[64,128]{1,0:T(8,128)S(1)} %collective-permute-done.20, f32[64,128]{1,0:T(8,128)S(1)} %add.110, f32[64,128]{1,0:T(8,128)S(1)} %collective-permute-done.18, f32[64,128]{1,0:T(8,128)S(1)} %collective-permute-done.19), kind=kLoop, calls=%fused_computation.29 | loop fusion | flops 24576 | bytes 163840 | tf_op jit(solution)/shard_map/add | solution.py:297
  (50 shorter events, 0.8 us)
Async XLA Ops:
  0.0 5.5 %copy-start = (bf16[1792,2816]{1,0:T(8,128)(2,1)S(1)}, bf16[1792,2816]{1,0:T(8,128)(2,1)}, u32[]{:S(2)}) copy-start(bf16[1792,2816]{1,0:T(8,128)(2,1)} %modes_ref.7) | copy-start | bytes 30277636
  0.0 7.4 %copy-start.3 = (s32[1792]{0:T(1024)S(1)}, s32[1792]{0:T(1024)}, u32[]{:S(2)}) copy-start(s32[1792]{0:T(1024)} %param.12) | copy-start | bytes 21508
  4.7 2.4 %collective-permute-start = (f32[11,128,128]{2,1,0:T(8,128)S(1)}, f32[11,128,128]{2,1,0:T(8,128)S(1)}, u32[]{:S(2)}, u32[]{:S(2)}) collective-permute-start(f32[11,128,128]{2,1,0:T(8,128)S(1)} %get-tuple-element.51), channel_id=1, source_target_pairs={{0,4},{4,0},{8,12},{12,8},{16,20},{20,16},{24,28},{28,24},{1,5},{5... | collective-permute-start | bytes 2162696 | tf_op jit(solution)/shard_map/ppermute | solution.py:302
  5.3 1.8 %collective-permute-start.1 = (f32[8,128]{1,0:T(8,128)S(1)}, f32[8,128]{1,0:T(8,128)S(1)}, u32[]{:S(2)}, u32[]{:S(2)}) collective-permute-start(f32[8,128]{1,0:T(8,128)S(1)} %get-tuple-element.53), channel_id=1, source_target_pairs={{0,4},{4,0},{8,12},{12,8},{16,20},{20,16},{24,28},{28,24},{1,5},{5... | collective-permute-start | bytes 12296 | tf_op jit(solution)/shard_map/ppermute | solution.py:302
  6.6 11.8 %copy-start.4 = (f32[2816]{0:T(1024)S(1)}, f32[2816]{0:T(1024)}, u32[]{:S(2)}) copy-start(f32[2816]{0:T(1024)} %param.9) | copy-start | bytes 33796
  6.6 11.8 %copy-start.5 = (f32[2816]{0:T(1024)S(1)}, f32[2816]{0:T(1024)}, u32[]{:S(2)}) copy-start(f32[2816]{0:T(1024)} %param.10) | copy-start | bytes 33796
  6.6 11.9 %copy-start.2 = (f32[8]{0:T(128)S(1)}, f32[8]{0:T(128)}, u32[]{:S(2)}) copy-start(f32[8]{0:T(128)} %omega_ref.5) | copy-start | bytes 100
  6.6 12.0 %copy-start.1 = (s32[1024,64]{0,1:T(8,128)S(1)}, s32[1024,64]{0,1:T(8,128)}, u32[]{:S(2)}) copy-start(s32[1024,64]{0,1:T(8,128)} %param.13) | copy-start | bytes 786436
  7.4 8.0 %collective-permute-start.2 = (f16[360,128]{1,0:T(8,128)(2,1)S(1)}, f16[360,128]{1,0:T(8,128)(2,1)S(1)}, u32[]{:S(2)}, u32[]{:S(2)}) collective-permute-start(f16[360,128]{1,0:T(8,128)(2,1)S(1)} %get-tuple-element.55), channel_id=1, source_target_pairs={{0,24},{4,28},{8,16},{12,20},{16,8},{20,12},{24,0},{28,4},{1,25},{... | collective-permute-start | bytes 276488 | tf_op jit(solution)/shard_map/ppermute | solution.py:302
  11.3 4.9 %collective-permute-start.3 = (f16[360,128]{1,0:T(8,128)(2,1)S(1)}, f16[360,128]{1,0:T(8,128)(2,1)S(1)}, u32[]{:S(2)}, u32[]{:S(2)}) collective-permute-start(f16[360,128]{1,0:T(8,128)(2,1)S(1)} %get-tuple-element.56), channel_id=1, source_target_pairs={{0,16},{4,20},{8,24},{12,28},{16,0},{20,4},{24,8},{28,12},{1,17},{... | collective-permute-start | bytes 276488 | tf_op jit(solution)/shard_map/ppermute | solution.py:302
  11.8 4.7 %collective-permute-start.4 = (f16[360,128]{1,0:T(8,128)(2,1)S(1)}, f16[360,128]{1,0:T(8,128)(2,1)S(1)}, u32[]{:S(2)}, u32[]{:S(2)}) collective-permute-start(f16[360,128]{1,0:T(8,128)(2,1)S(1)} %get-tuple-element.57), channel_id=1, source_target_pairs={{0,8},{4,12},{8,0},{12,4},{16,24},{20,28},{24,16},{28,20},{1,9},{5... | collective-permute-start | bytes 276488 | tf_op jit(solution)/shard_map/ppermute | solution.py:302
  16.8 4.6 %collective-permute-start.5 = (f16[360,128]{1,0:T(8,128)(2,1)S(1)}, f16[360,128]{1,0:T(8,128)(2,1)S(1)}, u32[]{:S(2)}, u32[]{:S(2)}) collective-permute-start(f16[360,128]{1,0:T(8,128)(2,1)S(1)} %pad_maximum_fusion.3), channel_id=1, source_target_pairs={{0,1},{1,0},{2,3},{3,2},{4,5},{5,4},{6,7},{7,6},{8,9},{9,8},{10,11... | collective-permute-start | bytes 276488 | tf_op jit(solution)/shard_map/ppermute | solution.py:302
  21.5 5.5 %collective-permute-start.6 = (f16[360,128]{1,0:T(8,128)(2,1)S(1)}, f16[360,128]{1,0:T(8,128)(2,1)S(1)}, u32[]{:S(2)}, u32[]{:S(2)}) collective-permute-start(f16[360,128]{1,0:T(8,128)(2,1)S(1)} %pad_maximum_fusion.4), channel_id=1, source_target_pairs={{0,2},{1,3},{2,0},{3,1},{4,6},{5,7},{6,4},{7,5},{8,10},{9,11},{10,... | collective-permute-start | bytes 276488 | tf_op jit(solution)/shard_map/ppermute | solution.py:302
  27.3 7.8 %collective-permute-start.7 = (bf16[11,2,16,128]{3,2,1,0:T(8,128)(2,1)S(1)}, bf16[11,2,16,128]{3,2,1,0:T(8,128)(2,1)S(1)}, u32[]{:S(2)}, u32[]{:S(2)}) collective-permute-start(bf16[11,2,16,128]{3,2,1,0:T(8,128)(2,1)S(1)} %pad_maximum_fusion.5.refs_3_), channel_id=1, source_target_pairs={{0,24},{4,28},{8,16},{12,20},{16,8},{20,12},{24,0},{28,4},{1,25},{... | collective-permute-start | bytes 270344 | tf_op jit(solution)/shard_map/ppermute | solution.py:302
  29.2 5.8 %collective-permute-start.8 = (bf16[11,2,16,128]{3,2,1,0:T(8,128)(2,1)S(1)}, bf16[11,2,16,128]{3,2,1,0:T(8,128)(2,1)S(1)}, u32[]{:S(2)}, u32[]{:S(2)}) collective-permute-start(bf16[11,2,16,128]{3,2,1,0:T(8,128)(2,1)S(1)} %pad_maximum_fusion.5.refs_3_), channel_id=1, source_target_pairs={{0,16},{4,20},{8,24},{12,28},{16,0},{20,4},{24,8},{28,12},{1,17},{... | collective-permute-start | bytes 270344 | tf_op jit(solution)/shard_map/ppermute | solution.py:302
  30.3 4.7 %collective-permute-start.9 = (bf16[11,2,16,128]{3,2,1,0:T(8,128)(2,1)S(1)}, bf16[11,2,16,128]{3,2,1,0:T(8,128)(2,1)S(1)}, u32[]{:S(2)}, u32[]{:S(2)}) collective-permute-start(bf16[11,2,16,128]{3,2,1,0:T(8,128)(2,1)S(1)} %pad_maximum_fusion.5.refs_3_), channel_id=1, source_target_pairs={{0,8},{4,12},{8,0},{12,4},{16,24},{20,28},{24,16},{28,20},{1,9},{5... | collective-permute-start | bytes 270344 | tf_op jit(solution)/shard_map/ppermute | solution.py:302
  31.5 5.9 %collective-permute-start.13 = (bf16[11,2,16,128]{3,2,1,0:T(8,128)(2,1)S(1)}, bf16[11,2,16,128]{3,2,1,0:T(8,128)(2,1)S(1)}, u32[]{:S(2)}, u32[]{:S(2)}) collective-permute-start(bf16[11,2,16,128]{3,2,1,0:T(8,128)(2,1)S(1)} %pad_maximum_fusion.5.refs_3_), channel_id=1, source_target_pairs={{0,4},{4,0},{8,12},{12,8},{16,20},{20,16},{24,28},{28,24},{1,5},{5... | collective-permute-start | bytes 270344 | tf_op jit(solution)/shard_map/ppermute | solution.py:302
  35.0 2.3 %collective-permute-start.10 = (bf16[11,2,16,128]{3,2,1,0:T(8,128)(2,1)S(1)}, bf16[11,2,16,128]{3,2,1,0:T(8,128)(2,1)S(1)}, u32[]{:S(2)}, u32[]{:S(2)}) collective-permute-start(bf16[11,2,16,128]{3,2,1,0:T(8,128)(2,1)S(1)} %collective-permute-done.7.refs_0_), channel_id=1, source_target_pairs={{0,4},{4,0},{8,12},{12,8},{16,20},{20,16},{24,28},{28,24},{1,5},{5... | collective-permute-start | bytes 270344 | tf_op jit(solution)/shard_map/ppermute | solution.py:302
  35.6 1.8 %collective-permute-start.11 = (bf16[11,2,16,128]{3,2,1,0:T(8,128)(2,1)S(1)}, bf16[11,2,16,128]{3,2,1,0:T(8,128)(2,1)S(1)}, u32[]{:S(2)}, u32[]{:S(2)}) collective-permute-start(bf16[11,2,16,128]{3,2,1,0:T(8,128)(2,1)S(1)} %collective-permute-done.8.refs_1_), channel_id=1, source_target_pairs={{0,4},{4,0},{8,12},{12,8},{16,20},{20,16},{24,28},{28,24},{1,5},{5... | collective-permute-start | bytes 270344 | tf_op jit(solution)/shard_map/ppermute | solution.py:302
  35.7 1.7 %collective-permute-start.12 = (bf16[11,2,16,128]{3,2,1,0:T(8,128)(2,1)S(1)}, bf16[11,2,16,128]{3,2,1,0:T(8,128)(2,1)S(1)}, u32[]{:S(2)}, u32[]{:S(2)}) collective-permute-start(bf16[11,2,16,128]{3,2,1,0:T(8,128)(2,1)S(1)} %collective-permute-done.9.refs_2_), channel_id=1, source_target_pairs={{0,4},{4,0},{8,12},{12,8},{16,20},{20,16},{24,28},{28,24},{1,5},{5... | collective-permute-start | bytes 270344 | tf_op jit(solution)/shard_map/ppermute | solution.py:302
  38.6 7.5 %collective-permute-start.16 = (bf16[128,256]{1,0:T(8,128)(2,1)S(1)}, bf16[128,256]{1,0:T(8,128)(2,1)S(1)}, u32[]{:S(2)}, u32[]{:S(2)}) collective-permute-start(bf16[128,256]{1,0:T(8,128)(2,1)S(1)} %panel_sums.3.refs_0_), channel_id=1, source_target_pairs={{0,2},{1,3},{2,0},{3,1},{4,6},{5,7},{6,4},{7,5},{8,10},{9,11},{10,... | collective-permute-start | bytes 196616 | tf_op jit(solution)/shard_map/ppermute | solution.py:302
  40.7 6.5 %collective-permute-start.14 = (bf16[128,256]{1,0:T(8,128)(2,1)S(1)}, bf16[128,256]{1,0:T(8,128)(2,1)S(1)}, u32[]{:S(2)}, u32[]{:S(2)}) collective-permute-start(bf16[128,256]{1,0:T(8,128)(2,1)S(1)} %panel_sums.3.refs_0_), channel_id=1, source_target_pairs={{0,3},{1,2},{2,1},{3,0},{4,7},{5,6},{6,5},{7,4},{8,11},{9,10},{10,... | collective-permute-start | bytes 196616 | tf_op jit(solution)/shard_map/ppermute | solution.py:302
  42.6 5.5 %collective-permute-start.15 = (bf16[128,256]{1,0:T(8,128)(2,1)S(1)}, bf16[128,256]{1,0:T(8,128)(2,1)S(1)}, u32[]{:S(2)}, u32[]{:S(2)}) collective-permute-start(bf16[128,256]{1,0:T(8,128)(2,1)S(1)} %panel_sums.3.refs_0_), channel_id=1, source_target_pairs={{0,1},{1,0},{2,3},{3,2},{4,5},{5,4},{6,7},{7,6},{8,9},{9,8},{10,11... | collective-permute-start | bytes 196616 | tf_op jit(solution)/shard_map/ppermute | solution.py:302
  49.3 1.3 %collective-permute-start.17 = (f32[64,128]{1,0:T(8,128)S(1)}, f32[64,128]{1,0:T(8,128)S(1)}, u32[]{:S(2)}, u32[]{:S(2)}) collective-permute-start(f32[64,128]{1,0:T(8,128)S(1)} %field_sums.3), channel_id=1, source_target_pairs={{0,4},{4,0},{8,12},{12,8},{16,20},{20,16},{24,28},{28,24},{1,5},{5... | collective-permute-start | bytes 98312 | tf_op jit(solution)/shard_map/ppermute | solution.py:302
  50.6 4.8 %collective-permute-start.18 = (f32[64,128]{1,0:T(8,128)S(1)}, f32[64,128]{1,0:T(8,128)S(1)}, u32[]{:S(2)}, u32[]{:S(2)}) collective-permute-start(f32[64,128]{1,0:T(8,128)S(1)} %add.110), channel_id=1, source_target_pairs={{0,24},{4,28},{8,16},{12,20},{16,8},{20,12},{24,0},{28,4},{1,25},{... | collective-permute-start | bytes 98312 | tf_op jit(solution)/shard_map/ppermute | solution.py:302
  52.7 3.9 %collective-permute-start.19 = (f32[64,128]{1,0:T(8,128)S(1)}, f32[64,128]{1,0:T(8,128)S(1)}, u32[]{:S(2)}, u32[]{:S(2)}) collective-permute-start(f32[64,128]{1,0:T(8,128)S(1)} %add.110), channel_id=1, source_target_pairs={{0,16},{4,20},{8,24},{12,28},{16,0},{20,4},{24,8},{28,12},{1,17},{... | collective-permute-start | bytes 98312 | tf_op jit(solution)/shard_map/ppermute | solution.py:302
  53.2 3.9 %collective-permute-start.20 = (f32[64,128]{1,0:T(8,128)S(1)}, f32[64,128]{1,0:T(8,128)S(1)}, u32[]{:S(2)}, u32[]{:S(2)}) collective-permute-start(f32[64,128]{1,0:T(8,128)S(1)} %add.110), channel_id=1, source_target_pairs={{0,8},{4,12},{8,0},{12,4},{16,24},{20,28},{24,16},{28,20},{1,9},{5... | collective-permute-start | bytes 98312 | tf_op jit(solution)/shard_map/ppermute | solution.py:302
